TPU v7x, 32 devices: a whole 2x2x4 slice. The times are simulated.
32 devices in a mesh: exp: 16 (over z, y, core), hid: 2 (over x).
Axes of the slice: x: 2, y: 2, z: 4, core: 2. Of those that a mesh axis runs over, the one named last changes fastest.
Arguments:
- tokens: bfloat16 [128, 2048], P(('exp', 'hid')), may hold values from -6 to 6
- grad_out: bfloat16 [128, 2048], P(('exp', 'hid')), may hold values from -3 to 3
- router_logits: float32 [128, 16], P(('exp', 'hid')), may hold values from -12 to 330
- selected: int32 [128, 8], P(('exp', 'hid')), may hold values from 0 to 15, as said below
- router_w: bfloat16 [2048, 16], replicated, may hold values from -0.59765625 to 0.59765625
- w_gate: bfloat16 [32, 2048, 384], P(('exp', 'hid')), may hold values from -0.125 to 0.125
- w_up: bfloat16 [32, 2048, 384], P(('exp', 'hid')), may hold values from -0.125 to 0.125
- w_down: bfloat16 [32, 384, 2048], P(('exp', 'hid')), may hold values from -0.21875 to 0.21875
Outputs:
- x_grad: bfloat16 [128, 2048], P(('exp', 'hid'))
- router_grad: float32 [2048, 16], P(('exp', 'hid'))
Inputs may be any that keep to these rules, and one draw needn't show every extreme that they name: `selected`: each row names 8 different experts; within each aligned block of 8 rows (the tokens of one index of exp) no expert is named by more than 8 rows, and in every block some expert is named by exactly 8 rows.
All inputs are finite; a program needn't handle non-finite values.
Results may differ from a plain program's by a relative error of at most 0.0075.
Values may be sent and summed in bfloat16 or wider, within the bound.
No kernel may reach another device: no remote copies, remote signals or barrier semaphores. Data moves between devices by JAX's collectives and lax.ppermute only.
A program may use at most 64 MiB of HBM per device.

v0:
```python
import functools

import jax
import jax.numpy as jnp
from jax import lax
from jax.experimental import pallas as pl
from jax.experimental.pallas import tpu as pltpu
from jax.sharding import PartitionSpec as P

AXES = ("exp", "hid")
LANES = 128
PIECES = 4
SCORE_PIECES = 2
VMEM_SPEC = pl.BlockSpec(memory_space=pltpu.VMEM)
HBM_SPEC = pl.BlockSpec(memory_space=pltpu.HBM)
F32 = jnp.float32
BF16 = jnp.bfloat16
NT = (((1,), (1,)), ((), ()))
TN = (((0,), (0,)), ((), ()))
PARAMS = pltpu.CompilerParams(vmem_limit_bytes=24 * 2**20)


def stage_masks(exp_size, hid_size):
    hid_bits = hid_size.bit_length() - 1
    all_bits = (exp_size * hid_size).bit_length() - 1
    core = hid_bits
    first = list(range(max(core + 1, all_bits - 2), all_bits))
    middle = [b for b in range(all_bits) if b != core and b not in first]
    groups = [first] + [middle[i : i + 2] for i in range(0, len(middle), 2)]
    bases = [[(sum(1 << b for b in group[i:]),) * 2 for i in range(len(group))] for group in groups]
    bases[0] = bases[0][::-1]
    return bases, core


def cross(a, b):
    return (a[0] ^ b[0], a[1] ^ b[1])


def group_masks(basis):
    masks = [(0, 0)]
    for mask in basis:
        masks = masks + [cross(m, mask) for m in masks]
    return masks


def near_first(basis):
    return [cross(basis[0], basis[1]), basis[1]] if len(basis) == 2 else basis


def swap(block, mask, count, core):
    return lax.ppermute(block, AXES, [(i, i ^ mask[i >> core & 1]) for i in range(count)])


def swaps(block, masks, count, core):
    return [swap(block, m, count, core) for m in masks]


def forward(blocks):
    return blocks[:1] + blocks[:0:-1]


def place_mask(place, basis, upper):
    total = jnp.zeros_like(place)
    for digit, (low, high) in enumerate(basis):
        mask = low if low == high else jnp.where(upper, high, low)
        total = total ^ (((place >> digit) & 1) * mask)
    return total


def own_index():
    return lax.axis_index("exp") * lax.axis_size("hid") + lax.axis_index("hid")


def in_hbm(*arrays):
    return tuple(pltpu.with_memory_space_constraint(a, pltpu.HBM) for a in arrays)


def piece_sum(experts, lanes, axis):
    shape = (lanes, experts) if axis == 0 else (experts, lanes)
    lane = lax.broadcasted_iota(jnp.int32, shape, axis)
    ids = lax.broadcasted_iota(jnp.int32, shape, 1 - axis)
    tally = jnp.zeros(shape, F32)
    for k in range(1, PIECES):
        tally = tally + jnp.where(lane == ids + k * experts, 1.0, 0.0)
    return tally.astype(BF16)


def combine_rows(extras, experts):
    hit = extras[:, :experts].astype(F32) > 0.5
    logits = jnp.dot(extras, piece_sum(experts, extras.shape[1], 0), preferred_element_type=F32)
    top = jnp.max(jnp.where(hit, logits, -jnp.inf), axis=1, keepdims=True)
    raised = jnp.where(hit, jnp.exp(jnp.minimum(logits - top, 0.0)), 0.0)
    return (raised / jnp.sum(raised, axis=1, keepdims=True)).astype(BF16).astype(F32)


def prep_kernel(tokens_in, grad_in, logits_in, chosen_in, out_ref, logits_ref, chosen_ref, sems):
    tok, width = tokens_in.shape
    pairs = [
        (logits_in, logits_ref),
        (chosen_in, chosen_ref),
        (tokens_in, out_ref.at[0, :, 0:width]),
        (grad_in, out_ref.at[1, :, 0:width]),
    ]
    copies = [pltpu.make_async_copy(src, dst, sems.at[i]) for i, (src, dst) in enumerate(pairs)]
    for copy in copies:
        copy.start()
    copies[0].wait()
    copies[1].wait()
    logits = logits_ref[...]
    chosen = chosen_ref[...]
    experts = logits.shape[1]
    ids = lax.broadcasted_iota(jnp.int32, logits.shape, 1)
    hit = ids == chosen[:, 0:1]
    for k in range(1, chosen.shape[1]):
        hit = hit | (ids == chosen[:, k : k + 1])
    parts = [jnp.where(hit, 1.0, 0.0)]
    rest = logits
    for _ in range(PIECES - 1):
        parts.append(rest)
        rest = rest - rest.astype(BF16).astype(F32)
    lanes = out_ref.shape[2] - width
    spare = lanes - PIECES * experts
    extras = jnp.concatenate(parts + ([jnp.zeros((tok, spare), F32)] if spare else []), axis=1)
    out_ref[0, :, width:] = extras.astype(BF16)
    out_ref[1, :, width:] = jnp.zeros((tok, lanes), BF16)
    copies[2].wait()
    copies[3].wait()


def hidden_parts(hidden):
    main = hidden // 256 * 256
    return [(0, main), (main, hidden)] if 0 < main < hidden else [(0, hidden)]


def load_kernel(chunks, block_in, gate_in, up_in, down_in, block_ref, pair_ref, down_ref, sems):
    copies = []

    def add(src, dst):
        copies.append(pltpu.make_async_copy(src, dst, sems.at[len(copies)]))

    hidden, width = down_ref.shape
    for c in range(chunks):
        part = pl.ds(c * (width // chunks), width // chunks)
        for first, last in hidden_parts(hidden):
            for k, ref in enumerate((gate_in, up_in)):
                to = 2 * first + k * (last - first)
                add(ref.at[0, part, first:last], pair_ref.at[part, to : to + last - first])
        part = pl.ds(c * (hidden // chunks), hidden // chunks)
        add(down_in.at[0, part, :], down_ref.at[part, :])
    add(block_in, block_ref)
    for copy in copies:
        copy.start()
    for copy in copies:
        copy.wait()


def join_kernel(*refs):
    blocks, out_ref, rows_ref = forward(refs[:-2]), refs[-2], refs[-1]
    count = len(blocks)
    tok = blocks[0].shape[1]
    for kind in range(2):
        for j, ref in enumerate(blocks):
            first = (kind * count + j) * tok
            rows_ref[first : first + tok, :] = ref[kind].astype(F32)
    out_ref[...] = rows_ref[...].astype(BF16)


def stack_kernel(*refs):
    out_ref = refs[-1]
    rows = refs[0].shape[0]
    for j, ref in enumerate(refs[:-1]):
        out_ref[j * rows : (j + 1) * rows, :] = ref[...]


def token_rows(refs, start, rows, group, kind, columns):
    parts = []
    for ref in refs:
        for j in range(rows // (2 * group)):
            first = start + (2 * j + kind) * group
            if not isinstance(first, int):
                first = pl.multiple_of(first, group)
            parts.append(ref[pl.ds(first, group), columns])
    return parts[0] if len(parts) == 1 else jnp.concatenate(parts, axis=0)


def put_scores(out_ref, scores_ref, width):
    rows = out_ref.shape[0]
    for c in range((out_ref.shape[1] - width) // LANES):
        out_ref[:, width + c * LANES : width + (c + 1) * LANES] = scores_ref[c * rows : (c + 1) * rows, :].astype(BF16)


def get_scores(in_ref, scores_ref, base, size, width):
    rows = in_ref.shape[0]
    for c in range(-(-size // rows)):
        here = min(rows, size - c * rows)
        tall = min(rows, -(-here // 16) * 16)
        block = in_ref[0:tall, width + c * LANES : width + (c + 1) * LANES].astype(F32)
        scores_ref[base + c * rows : base + c * rows + here, :] = block[:here]


def units_kernel(basis, group, tok, experts, core_mask, blocks, *refs):
    own_refs, other_refs = forward(refs[:blocks]), forward(refs[blocks : 2 * blocks])
    pair_ref, down_ref, kept_ref, message_ref, pieces_ref, score_ref, padded_ref = refs[2 * blocks :]
    hidden, width = down_ref.shape
    rows, buf_width = own_refs[0].shape
    tokens = score_ref.shape[1]
    own = own_index()

    def terms(sets, start, step):
        act = token_rows(sets, start, step, group, 0, slice(None))
        count = act.shape[0]
        combine = combine_rows(act[:, width:], experts)
        ids = lax.broadcasted_iota(jnp.int32, combine.shape, 1)
        column = jnp.sum(jnp.where(ids == own // 2, combine, 0.0), axis=1, keepdims=True)
        act = act[:, :width]
        cot = token_rows(sets, start, step, group, 1, slice(0, width))
        score = jnp.zeros((count, 1), F32)
        grads = []
        for first, last in hidden_parts(hidden):
            size = last - first
            pair = jnp.dot(act, pair_ref[:, 2 * first : 2 * last], preferred_element_type=F32)
            gate_pre = pair[:, :size]
            up_pre = pair[:, size:]
            back = lax.dot_general(cot, down_ref[first:last, :], NT, preferred_element_type=F32)
            sig = jax.nn.sigmoid(gate_pre)
            act_gate = gate_pre * sig
            score = score + jnp.sum(act_gate * up_pre * back, axis=1, keepdims=True)
            weighted = column * back
            grad_gate = weighted * up_pre * sig * (1.0 + gate_pre * (1.0 - sig))
            grad_up = weighted * act_gate
            grads += [grad_gate.astype(BF16), grad_up.astype(BF16)]
        grads = jnp.concatenate(grads, axis=1)
        return lax.dot_general(grads, pair_ref[...], NT, preferred_element_type=F32), score

    def in_order(score, place, swap_mask):
        token = lax.broadcasted_iota(jnp.int32, (score.shape[0], tokens), 1)
        side = own ^ swap_mask
        whole = (place_mask(place // tok, basis, side & core_mask != 0) ^ side) * tok + place % tok
        return jnp.sum(jnp.where(whole == token, score, 0.0), axis=0, keepdims=True)

    half = blocks * rows // 2
    if 2 * half <= 128:
        total, score = terms(own_refs + other_refs, 0, rows)
        kept_ref[...] = total[:half]
        message_ref[:, 0:width] = total[half:].astype(BF16)
        row = lax.broadcasted_iota(jnp.int32, (2 * half, tokens), 0)
        score_ref[...] = in_order(score, row % half, jnp.where(row < half, 0, core_mask))
    else:
        step = min(rows, 128)
        score_ref[...] = jnp.zeros(score_ref.shape, F32)
        for out_ref, sets, swap_mask in ((kept_ref, own_refs, 0), (message_ref, other_refs, core_mask)):
            for j, ref in enumerate(sets):

                def one(index):
                    total, score = terms((ref,), index * step, step)
                    first = pl.multiple_of(j * (rows // 2) + index * (step // 2), step // 2)
                    out_ref[pl.ds(first, step // 2), 0:width] = total.astype(out_ref.dtype)
                    place = lax.broadcasted_iota(jnp.int32, (step // 2, tokens), 0) + first
                    score_ref[...] += in_order(score, place, swap_mask)

                pl.loop(0, rows // step)(one)

    lane_blocks = tokens // LANES
    padded_ref[...] = jnp.zeros(padded_ref.shape, F32)
    value = score_ref[...]
    for piece in range(SCORE_PIECES):
        rounded = value.astype(BF16).astype(F32)
        for b in range(lane_blocks):
            at = piece * lane_blocks + b
            padded_ref[at : at + 1, :] = rounded[:, b * LANES : (b + 1) * LANES]
        value = value - rounded
    pieces_ref[...] = padded_ref[0 : pieces_ref.shape[0], :]
    put_scores(message_ref, padded_ref, width)


def add_kernel(arrivals, positions, core_mask, *refs):
    kept_ref, pieces_ref = refs[0], refs[1]
    arrived = refs[2 : 2 + arrivals]
    outs = refs[2 + arrivals :]
    next_kept_ref, next_pieces_ref = outs[0], outs[1]
    sends = outs[2 : 2 + len(positions)]
    total_ref, scores_ref = outs[2 + len(positions) :]
    width = kept_ref.shape[1]
    size = pieces_ref.shape[0]
    total = kept_ref[...]
    for ref in arrived:
        total = total + ref[:, 0:width].astype(F32)
    total_ref[...] = total
    if scores_ref.shape[0] > next_pieces_ref.shape[0]:
        scores_ref[...] = jnp.zeros(scores_ref.shape, F32)
    scores_ref[0:size, :] = pieces_ref[...]
    for j, ref in enumerate(arrived):
        get_scores(ref, scores_ref, (j + 1) * size, size, width)
    rows = next_kept_ref.shape[0]
    next_kept_ref[...] = total_ref[0:rows, :]
    next_pieces_ref[...] = scores_ref[0 : next_pieces_ref.shape[0], :]
    upper = own_index() & core_mask != 0
    for (low, high), ref in zip(positions, sends):
        first = low * rows
        if low != high:
            first = pl.multiple_of(jnp.where(upper, high, low) * rows, rows)
        ref[:, 0:width] = total_ref[pl.ds(first, rows), :].astype(BF16)
        put_scores(ref, scores_ref, width)


def table_kernel(basis, group, tok, core_mask, rows_out, blocks, after_ref, *refs):
    probs_ref, column_ref, mine_ref = refs[2 * blocks :]
    rows, buf_width = refs[0].shape
    half = blocks * rows // 2
    experts, tokens = probs_ref.shape
    lanes = -(-PIECES * experts // LANES) * LANES
    width = buf_width - lanes
    own = own_index()
    column = pl.multiple_of(own * rows_out // LANES * LANES, LANES)
    extras = jnp.zeros((tokens, lanes), F32)
    columns = jnp.zeros((tokens, LANES), F32)
    for index in range(2):
        sets = forward(refs[index * blocks : (index + 1) * blocks])
        row = lax.broadcasted_iota(jnp.int32, (half, tokens), 0)
        token = lax.broadcasted_iota(jnp.int32, (half, tokens), 1)
        side = own ^ (core_mask if index else 0)
        whole = (place_mask(row // tok, basis, side & core_mask != 0) ^ side) * tok + row % tok
        here = jnp.where(whole == token, 1.0, 0.0).astype(BF16)
        part = token_rows(sets, 0, rows, group, 0, slice(width, buf_width))
        extras = extras + lax.dot_general(here, part, TN, preferred_element_type=F32)
        part = token_rows(sets, 0, rows, group, 0, pl.ds(column, LANES))
        columns = columns + lax.dot_general(here, part, TN, preferred_element_type=F32)
    logits = lax.dot_general(piece_sum(experts, lanes, 1), extras.astype(BF16), NT, preferred_element_type=F32)
    raised = jnp.exp(logits - jnp.max(logits, axis=0, keepdims=True))
    probs_ref[...] = raised / jnp.sum(raised, axis=0, keepdims=True)
    column_ref[...] = columns.astype(BF16)
    row = lax.broadcasted_iota(jnp.int32, mine_ref.shape, 0)
    token = lax.broadcasted_iota(jnp.int32, mine_ref.shape, 1)
    mine_ref[...] = jnp.where((row < tok) & (token == own * tok + row), 1.0, 0.0).astype(BF16)


def final_kernel(arrivals, back_basis, core_mask, *refs):
    probs_ref, column_ref, mine_ref, router_ref, kept_ref, pieces_ref = refs[:6]
    arrived = refs[6 : 6 + arrivals]
    x_out, grad_out, x_ref, grad_ref, scores_ref, sems = refs[6 + arrivals :]
    experts, width = router_ref.shape
    size = pieces_ref.shape[0]
    tok = kept_ref.shape[0]
    own = own_index()
    scores_ref[0:size, :] = pieces_ref[...]
    for j, ref in enumerate(arrived):
        get_scores(ref, scores_ref, (j + 1) * size, size, width)
    blocks = probs_ref.shape[1] // LANES
    wide = scores_ref.shape[0] // blocks
    sender = lax.broadcasted_iota(jnp.int32, (experts, wide), 1) // SCORE_PIECES
    ids = lax.broadcasted_iota(jnp.int32, (experts, wide), 0)
    pick = jnp.where(((place_mask(sender, back_basis, own & core_mask != 0) ^ own) >> 1) == ids, 1.0, 0.0).astype(BF16)
    parts = []
    for b in range(blocks):
        block = scores_ref[...] if blocks == 1 else scores_ref[pl.ds(b, wide, stride=blocks), :]
        parts.append(jnp.dot(pick, block.astype(BF16), preferred_element_type=F32))
    scores = parts[0] if blocks == 1 else jnp.concatenate(parts, axis=1)
    probs = probs_ref[...]
    mean = jnp.sum(probs * scores, axis=0, keepdims=True)
    logit_grad = (probs * (scores - mean)).astype(BF16)
    mine = lax.dot_general(mine_ref[...], logit_grad, NT, preferred_element_type=F32)
    part = jnp.dot(mine.astype(BF16), router_ref[...], preferred_element_type=F32)
    total = kept_ref[...]
    for ref in arrived:
        total = total + ref[:, 0:width].astype(F32)
    x_ref[...] = (total + part[:tok]).astype(BF16)
    x_copy = pltpu.make_async_copy(x_ref, x_out, sems.at[0])
    x_copy.start()
    grad = jnp.dot(logit_grad, column_ref[...], preferred_element_type=F32)
    rows_out = grad_ref.shape[1]
    first = own * rows_out % LANES
    grad_ref[...] = pltpu.roll(grad, (LANES - first) % LANES, 1)[:, :rows_out]
    grad_copy = pltpu.make_async_copy(grad_ref, grad_out, sems.at[1])
    grad_copy.start()
    x_copy.wait()
    grad_copy.wait()


def on_device(tokens, grad_out, router_logits, selected, router_w, w_gate, w_up, w_down):
    tok, width = tokens.shape
    experts = router_logits.shape[1]
    hidden = w_gate.shape[2]
    exp_size = lax.axis_size("exp")
    hid_size = lax.axis_size("hid")
    count = exp_size * hid_size
    half = count // 2
    groups, core = stage_masks(exp_size, hid_size)
    core_mask = 1 << core
    basis = [m for group in groups for m in group]
    back_groups = [near_first(group) for group in groups[:0:-1]] + [groups[0]]
    core_pair = (core_mask, core_mask)
    back_basis = [core_pair] + [m for group in back_groups for m in group]
    token_count = count * tok
    lanes = -(-PIECES * experts // LANES) * LANES

    block = pl.pallas_call(
        prep_kernel,
        out_shape=jax.ShapeDtypeStruct((2, tok, width + lanes), BF16),
        in_specs=[HBM_SPEC] * 4,
        out_specs=VMEM_SPEC,
        scratch_shapes=[
            pltpu.VMEM(router_logits.shape, router_logits.dtype),
            pltpu.VMEM(selected.shape, selected.dtype),
            pltpu.SemaphoreType.DMA((4,)),
        ],
        compiler_params=PARAMS,
        name="prep",
    )(*in_hbm(tokens, grad_out, router_logits, selected))

    masks = group_masks(groups[0])
    blocks = [block] + swaps(block, masks[1:], count, core)
    group_rows = tok * len(blocks)
    block = pl.pallas_call(
        join_kernel,
        out_shape=jax.ShapeDtypeStruct((2 * group_rows, width + lanes), BF16),
        in_specs=[VMEM_SPEC] * len(blocks),
        out_specs=VMEM_SPEC,
        scratch_shapes=[pltpu.VMEM((2 * group_rows, width + lanes), F32)],
        compiler_params=PARAMS,
        name="join",
    )(*forward(blocks))
    for group in groups[1:-1]:
        blocks = [block] + swaps(block, group_masks(group)[1:], count, core)
        block = pl.pallas_call(
            stack_kernel,
            out_shape=jax.ShapeDtypeStruct((len(blocks) * block.shape[0], block.shape[1]), BF16),
            in_specs=[VMEM_SPEC] * len(blocks),
            out_specs=VMEM_SPEC,
            compiler_params=PARAMS,
            name="stack",
        )(*blocks)
    chunks = 4
    copied, pair, down = pl.pallas_call(
        functools.partial(load_kernel, chunks),
        out_shape=(
            pltpu.VMEM(block.shape, BF16),
            pltpu.VMEM((width, 2 * hidden), BF16),
            pltpu.VMEM((hidden, width), BF16),
        ),
        in_specs=[VMEM_SPEC] + [HBM_SPEC] * 3,
        out_specs=(VMEM_SPEC,) * 3,
        scratch_shapes=[pltpu.SemaphoreType.DMA(((2 * len(hidden_parts(hidden)) + 1) * chunks + 1,))],
        compiler_params=pltpu.CompilerParams(vmem_limit_bytes=4 * 2**20),
        cost_estimate=pl.CostEstimate(flops=0, bytes_accessed=6 * width * hidden * 2, transcendentals=0),
        name="load",
    )(block, *in_hbm(w_gate, w_up, w_down))
    masks = group_masks(groups[-1]) if len(groups) > 1 else [core_pair]
    blocks = [block] + swaps(block, masks[1:], count, core)
    blocks = forward(blocks)
    blocks = blocks + [swap(b, core_pair, count, core) for b in [copied] + blocks[1:]]
    block_count = len(blocks) // 2

    unit_rows = SCORE_PIECES * token_count // LANES
    extra = -(-unit_rows // (half * tok)) * LANES
    kept, message, pieces = pl.pallas_call(
        functools.partial(units_kernel, basis, group_rows, tok, experts, core_mask, block_count),
        out_shape=(
            jax.ShapeDtypeStruct((half * tok, width), F32),
            jax.ShapeDtypeStruct((half * tok, width + extra), BF16),
            jax.ShapeDtypeStruct((unit_rows, LANES), F32),
        ),
        in_specs=[VMEM_SPEC] * (len(blocks) + 2),
        out_specs=(VMEM_SPEC,) * 3,
        scratch_shapes=[
            pltpu.VMEM((1, token_count), F32),
            pltpu.VMEM((max(half * tok * extra // LANES, unit_rows), LANES), F32),
        ],
        compiler_params=PARAMS,
        cost_estimate=pl.CostEstimate(
            flops=10 * token_count * width * hidden,
            bytes_accessed=3 * width * hidden * 2 + 2 * token_count * width * 2,
            transcendentals=token_count * hidden,
        ),
        name="units",
    )(*blocks, pair, down)

    arrived = [swap(message, core_pair, count, core)]
    tables = None
    rows_out = width // count
    for group, back_group in zip(groups[::-1], back_groups):
        back_masks = group_masks(back_group)
        positions = [
            tuple([m[side] for m in group_masks(group)].index(mask[side]) for side in range(2)) for mask in back_masks[1:]
        ]
        radix = len(back_masks)
        rows = kept.shape[0]
        next_rows = rows // radix
        size = pieces.shape[0] * (1 + len(arrived))
        extra = -(-size // next_rows) * LANES
        sends = [jax.ShapeDtypeStruct((next_rows, width + extra), BF16)] * (radix - 1)
        outs = pl.pallas_call(
            functools.partial(add_kernel, len(arrived), positions, core_mask),
            out_shape=[
                jax.ShapeDtypeStruct((next_rows, width), F32),
                jax.ShapeDtypeStruct((size, LANES), F32),
            ]
            + sends,
            in_specs=[VMEM_SPEC] * (2 + len(arrived)),
            out_specs=[VMEM_SPEC] * (1 + radix),
            scratch_shapes=[
                pltpu.VMEM((rows, width), F32),
                pltpu.VMEM((max(next_rows * extra // LANES, size), LANES), F32),
            ],
            compiler_params=PARAMS,
            name="add",
        )(kept, pieces, *arrived)
        kept, pieces = outs[0], outs[1]
        if tables is None:
            tables = pl.pallas_call(
                functools.partial(table_kernel, basis, group_rows, tok, core_mask, rows_out, block_count),
                out_shape=(
                    jax.ShapeDtypeStruct((experts, token_count), F32),
                    jax.ShapeDtypeStruct((token_count, LANES), BF16),
                    jax.ShapeDtypeStruct((16, token_count), BF16),
                ),
                in_specs=[pl.BlockSpec(memory_space=pl.ANY)] + [VMEM_SPEC] * len(blocks),
                out_specs=(VMEM_SPEC,) * 3,
                compiler_params=PARAMS,
                cost_estimate=pl.CostEstimate(flops=10**9, bytes_accessed=10**6, transcendentals=0),
                name="tables",
            )(pieces, *blocks)
        arrived = [swap(piece, m, count, core) for piece, m in zip(outs[2:], back_masks[1:])]

    x_grad, grad = pl.pallas_call(
        functools.partial(final_kernel, len(arrived), back_basis, core_mask),
        out_shape=(
            jax.ShapeDtypeStruct((tok, width), BF16),
            jax.ShapeDtypeStruct((experts, rows_out), F32),
        ),
        in_specs=[VMEM_SPEC] * (6 + len(arrived)),
        out_specs=(HBM_SPEC, HBM_SPEC),
        scratch_shapes=[
            pltpu.VMEM((tok, width), BF16),
            pltpu.VMEM((experts, rows_out), F32),
            pltpu.VMEM((pieces.shape[0] * (1 + len(arrived)), LANES), F32),
            pltpu.SemaphoreType.DMA((2,)),
        ],
        compiler_params=PARAMS,
        name="final",
    )(*tables, router_w.T, kept, pieces, *arrived)
    return (x_grad, grad.T)


def solution(mesh):
    rows = P(AXES, None)
    units = P(AXES, None, None)
    return jax.shard_map(
        on_device,
        mesh=mesh,
        in_specs=(rows, rows, rows, rows, P(), units, units, units),
        out_specs=(rows, rows),
        check_vma=False,
    )
```

profile of v0, /device:TPU:0, one launch (start us, length us, event | category | flops | bytes accessed | tf_op | source)
XLA Modules:
  0.0 40.2 jit_solution(16468788055255441802)
XLA Ops:
  0.6 0.8 %prep.1.refs_0_ = bf16[2,4,2176]{2,1,0:T(4,128)(2,1)S(1)} custom-call(bf16[4,2048]{1,0:T(4,128)(2,1)} %tokens_in.1, bf16[4,2048]{1,0:T(4,128)(2,1)} %grad_in.1, f32[4,16]{1,0:T(4,128)} %logits_in.1, s32[4,8]{1,0:T(4,128)} %chosen_in.1), custom_call_target="tpu_custom_call" | custom-call | tf_op jit(solution)/shard_map/prep/pallas_call | solution.py:396
  1.5 4.1 %collective-permute-start.2 = (bf16[2,4,2176]{2,1,0:T(4,128)(2,1)S(1)}, bf16[2,4,2176]{2,1,0:T(4,128)(2,1)S(1)}, u32[]{:S(2)}, u32[]{:S(2)}) collective-permute-start(bf16[2,4,2176]{2,1,0:T(4,128)(2,1)S(1)} %prep.1.refs_0_), channel_id=1, source_target_pairs={{0,16},{1,17},{2,18},{3,19},{4,20},{5,21},{6,22},{7,23},{8,24},{9,... | collective-permute-start | bytes 104456 | tf_op jit(solution)/shard_map/ppermute | solution.py:51
  5.6 1.3 %collective-permute-start.1 = (bf16[2,4,2176]{2,1,0:T(4,128)(2,1)S(1)}, bf16[2,4,2176]{2,1,0:T(4,128)(2,1)S(1)}, u32[]{:S(2)}, u32[]{:S(2)}) collective-permute-start(bf16[2,4,2176]{2,1,0:T(4,128)(2,1)S(1)} %prep.1.refs_0_), channel_id=1, source_target_pairs={{0,24},{1,25},{2,26},{3,27},{4,28},{5,29},{6,30},{7,31},{8,16},{9,... | collective-permute-start | bytes 104456 | tf_op jit(solution)/shard_map/ppermute | solution.py:51
  6.9 0.2 collective-permute-start
  7.1 0.7 %collective-permute-done.2.refs_3_ = bf16[2,4,2176]{2,1,0:T(4,128)(2,1)S(1)} collective-permute-done((bf16[2,4,2176]{2,1,0:T(4,128)(2,1)S(1)}, bf16[2,4,2176]{2,1,0:T(4,128)(2,1)S(1)}, u32[]{:S(2)}, u32[]{:S(2)}) %collective-permute-start.2) | collective-permute-done | bytes 34848 | tf_op jit(solution)/shard_map/ppermute | solution.py:51
  7.9 3.4 %collective-permute-done.1.refs_2_ = bf16[2,4,2176]{2,1,0:T(4,128)(2,1)S(1)} collective-permute-done((bf16[2,4,2176]{2,1,0:T(4,128)(2,1)S(1)}, bf16[2,4,2176]{2,1,0:T(4,128)(2,1)S(1)}, u32[]{:S(2)}, u32[]{:S(2)}) %collective-permute-start.1) | collective-permute-done | bytes 34848 | tf_op jit(solution)/shard_map/ppermute | solution.py:51
  11.4 2.5 %collective-permute-start.5 = (bf16[32,2176]{1,0:T(8,128)(2,1)S(1)}, bf16[32,2176]{1,0:T(8,128)(2,1)S(1)}, u32[]{:S(2)}, u32[]{:S(2)}) collective-permute-start(bf16[32,2176]{1,0:T(8,128)(2,1)S(1)} %join.1.block_in.refs_0_), channel_id=1, source_target_pairs={{0,5},{1,4},{2,7},{3,6},{4,1},{5,0},{6,3},{7,2},{8,13},{9,12},{10,... | collective-permute-start | bytes 417800 | tf_op jit(solution)/shard_map/ppermute | solution.py:51
  13.9 0.5 %collective-permute-start.4 = (bf16[32,2176]{1,0:T(8,128)(2,1)S(1)}, bf16[32,2176]{1,0:T(8,128)(2,1)S(1)}, u32[]{:S(2)}, u32[]{:S(2)}) collective-permute-start(bf16[32,2176]{1,0:T(8,128)(2,1)S(1)} %join.1.block_in.refs_0_), channel_id=1, source_target_pairs={{0,4},{1,5},{2,6},{3,7},{4,0},{5,1},{6,2},{7,3},{8,12},{9,13},{10,... | collective-permute-start | bytes 417800 | tf_op jit(solution)/shard_map/ppermute | solution.py:51
  14.4 0.5 %collective-permute-start.3 = (bf16[32,2176]{1,0:T(8,128)(2,1)S(1)}, bf16[32,2176]{1,0:T(8,128)(2,1)S(1)}, u32[]{:S(2)}, u32[]{:S(2)}) collective-permute-start(bf16[32,2176]{1,0:T(8,128)(2,1)S(1)} %join.1.block_in.refs_0_), channel_id=1, source_target_pairs={{0,1},{1,0},{2,3},{3,2},{4,5},{5,4},{6,7},{7,6},{8,9},{9,8},{10,11... | collective-permute-start | bytes 417800 | tf_op jit(solution)/shard_map/ppermute | solution.py:51
  14.9 2.5 %load.1 = (bf16[32,2176]{1,0:T(8,128)(2,1)S(1)}, bf16[2048,768]{1,0:T(8,128)(2,1)S(1)}, bf16[384,2048]{1,0:T(8,128)(2,1)S(1)}) custom-call(bf16[32,2176]{1,0:T(8,128)(2,1)S(1)} %join.1.block_in.refs_0_, bf16[1,2048,384]{2,1,0:T(8,128)(2,1)} %gate_in.1, bf16[1,2048,384]{2,1,0:T(8,128)(2,1)} %up_in.1, bf16[1,384,2048]{2,1,0:T(8,128)(2,1)} %down_in.1), custom_call_target="tpu_custom_call" | custom-call | bytes 9437184 | tf_op jit(solution)/shard_map/load/pallas_call | solution.py:433
  17.5 1.4 %collective-permute-done.5.refs_3_ = bf16[32,2176]{1,0:T(8,128)(2,1)S(1)} collective-permute-done((bf16[32,2176]{1,0:T(8,128)(2,1)S(1)}, bf16[32,2176]{1,0:T(8,128)(2,1)S(1)}, u32[]{:S(2)}, u32[]{:S(2)}) %collective-permute-start.5) | collective-permute-done | bytes 139296 | tf_op jit(solution)/shard_map/ppermute | solution.py:51
  18.9 0.8 %collective-permute-done.4.refs_2_ = bf16[32,2176]{1,0:T(8,128)(2,1)S(1)} collective-permute-done((bf16[32,2176]{1,0:T(8,128)(2,1)S(1)}, bf16[32,2176]{1,0:T(8,128)(2,1)S(1)}, u32[]{:S(2)}, u32[]{:S(2)}) %collective-permute-start.4) | collective-permute-done | bytes 139296 | tf_op jit(solution)/shard_map/ppermute | solution.py:51
  19.7 0.5 %collective-permute-start.7 = (bf16[32,2176]{1,0:T(8,128)(2,1)S(1)}, bf16[32,2176]{1,0:T(8,128)(2,1)S(1)}, u32[]{:S(2)}, u32[]{:S(2)}) collective-permute-start(bf16[32,2176]{1,0:T(8,128)(2,1)S(1)} %collective-permute-done.3.refs_1_), channel_id=1, source_target_pairs={{0,2},{1,3},{2,0},{3,1},{4,6},{5,7},{6,4},{7,5},{8,10},{9,11},{10,... | collective-permute-start | bytes 417800 | tf_op jit(solution)/shard_map/ppermute | solution.py:51
  20.2 0.8 %collective-permute-done.8.refs_6_ = bf16[32,2176]{1,0:T(8,128)(2,1)S(1)} collective-permute-done((bf16[32,2176]{1,0:T(8,128)(2,1)S(1)}, bf16[32,2176]{1,0:T(8,128)(2,1)S(1)}, u32[]{:S(2)}, u32[]{:S(2)}) %collective-permute-start.8) | collective-permute-done | bytes 139296 | tf_op jit(solution)/shard_map/ppermute | solution.py:51
  21.0 0.2 collective-permute-done.7.refs_5_
  21.2 2.1 %units.1 = (f32[64,2048]{1,0:T(8,128)S(1)}, bf16[64,2176]{1,0:T(8,128)(2,1)S(1)}, f32[2,128]{1,0:T(2,128)S(1)}) custom-call(bf16[32,2176]{1,0:T(8,128)(2,1)S(1)} %join.1.block_in.refs_0_, bf16[32,2176]{1,0:T(8,128)(2,1)S(1)} %collective-permute-done.3.refs_1_, bf16[32,2176]{1,0:T(8,128)(2,1)S(1)} %collective-permute-done.4.refs_2_, ...), custom_call_target="tpu_custom_call" | custom-call | flops 1006632960 | bytes 5767168 | tf_op jit(solution)/shard_map/units/pallas_call | solution.py:455
  23.3 0.4 collective-permute-start.10
  23.7 1.2 %collective-permute-done.10.refs_2_ = bf16[64,2176]{1,0:T(8,128)(2,1)S(1)} collective-permute-done((bf16[64,2176]{1,0:T(8,128)(2,1)S(1)}, bf16[64,2176]{1,0:T(8,128)(2,1)S(1)}, u32[]{:S(2)}, u32[]{:S(2)}) %collective-permute-start.10) | collective-permute-done | bytes 278560 | tf_op jit(solution)/shard_map/ppermute | solution.py:51
  24.9 0.1 add.2
  25.0 1.2 %collective-permute-start.11 = (bf16[16,2176]{1,0:T(8,128)(2,1)S(1)}, bf16[16,2176]{1,0:T(8,128)(2,1)S(1)}, u32[]{:S(2)}, u32[]{:S(2)}) collective-permute-start(bf16[16,2176]{1,0:T(8,128)(2,1)S(1)} %get-tuple-element.34), channel_id=1, source_target_pairs={{0,1},{1,0},{2,3},{3,2},{4,5},{5,4},{6,7},{7,6},{8,9},{9,8},{10,11... | collective-permute-start | bytes 208904 | tf_op jit(solution)/shard_map/ppermute | solution.py:51
  26.2 0.8 %collective-permute-start.12 = (bf16[16,2176]{1,0:T(8,128)(2,1)S(1)}, bf16[16,2176]{1,0:T(8,128)(2,1)S(1)}, u32[]{:S(2)}, u32[]{:S(2)}) collective-permute-start(bf16[16,2176]{1,0:T(8,128)(2,1)S(1)} %get-tuple-element.35), channel_id=1, source_target_pairs={{0,4},{1,5},{2,6},{3,7},{4,0},{5,1},{6,2},{7,3},{8,12},{9,13},{10,... | collective-permute-start | bytes 208904 | tf_op jit(solution)/shard_map/ppermute | solution.py:51
  27.0 1.5 %collective-permute-start.13 = (bf16[16,2176]{1,0:T(8,128)(2,1)S(1)}, bf16[16,2176]{1,0:T(8,128)(2,1)S(1)}, u32[]{:S(2)}, u32[]{:S(2)}) collective-permute-start(bf16[16,2176]{1,0:T(8,128)(2,1)S(1)} %get-tuple-element.36), channel_id=1, source_target_pairs={{0,5},{1,4},{2,7},{3,6},{4,1},{5,0},{6,3},{7,2},{8,13},{9,12},{10,... | collective-permute-start | bytes 208904 | tf_op jit(solution)/shard_map/ppermute | solution.py:51
  28.6 0.9 %collective-permute-done.11.refs_2_ = bf16[16,2176]{1,0:T(8,128)(2,1)S(1)} collective-permute-done((bf16[16,2176]{1,0:T(8,128)(2,1)S(1)}, bf16[16,2176]{1,0:T(8,128)(2,1)S(1)}, u32[]{:S(2)}, u32[]{:S(2)}) %collective-permute-start.11) | collective-permute-done | bytes 69664 | tf_op jit(solution)/shard_map/ppermute | solution.py:51
  29.5 1.8 %collective-permute-done.12.refs_3_ = bf16[16,2176]{1,0:T(8,128)(2,1)S(1)} collective-permute-done((bf16[16,2176]{1,0:T(8,128)(2,1)S(1)}, bf16[16,2176]{1,0:T(8,128)(2,1)S(1)}, u32[]{:S(2)}, u32[]{:S(2)}) %collective-permute-start.12) | collective-permute-done | bytes 69664 | tf_op jit(solution)/shard_map/ppermute | solution.py:51
  31.3 1.0 %collective-permute-done.13.refs_4_ = bf16[16,2176]{1,0:T(8,128)(2,1)S(1)} collective-permute-done((bf16[16,2176]{1,0:T(8,128)(2,1)S(1)}, bf16[16,2176]{1,0:T(8,128)(2,1)S(1)}, u32[]{:S(2)}, u32[]{:S(2)}) %collective-permute-start.13) | collective-permute-done | bytes 69664 | tf_op jit(solution)/shard_map/ppermute | solution.py:51
  32.3 1.2 %collective-permute-start.14 = (bf16[4,2560]{1,0:T(4,128)(2,1)S(1)}, bf16[4,2560]{1,0:T(4,128)(2,1)S(1)}, u32[]{:S(2)}, u32[]{:S(2)}) collective-permute-start(bf16[4,2560]{1,0:T(4,128)(2,1)S(1)} %get-tuple-element.39), channel_id=1, source_target_pairs={{0,16},{1,17},{2,18},{3,19},{4,20},{5,21},{6,22},{7,23},{8,24},{9,... | collective-permute-start | bytes 61448 | tf_op jit(solution)/shard_map/ppermute | solution.py:51
  33.6 1.5 %collective-permute-start.15 = (bf16[4,2560]{1,0:T(4,128)(2,1)S(1)}, bf16[4,2560]{1,0:T(4,128)(2,1)S(1)}, u32[]{:S(2)}, u32[]{:S(2)}) collective-permute-start(bf16[4,2560]{1,0:T(4,128)(2,1)S(1)} %get-tuple-element.40), channel_id=1, source_target_pairs={{0,24},{1,25},{2,26},{3,27},{4,28},{5,29},{6,30},{7,31},{8,16},{9,... | collective-permute-start | bytes 61448 | tf_op jit(solution)/shard_map/ppermute | solution.py:51
  35.1 0.8 %collective-permute-start.16 = (bf16[4,2560]{1,0:T(4,128)(2,1)S(1)}, bf16[4,2560]{1,0:T(4,128)(2,1)S(1)}, u32[]{:S(2)}, u32[]{:S(2)}) collective-permute-start(bf16[4,2560]{1,0:T(4,128)(2,1)S(1)} %get-tuple-element.41), channel_id=1, source_target_pairs={{0,8},{1,9},{2,10},{3,11},{4,12},{5,13},{6,14},{7,15},{8,0},{9,1},... | collective-permute-start | bytes 61448 | tf_op jit(solution)/shard_map/ppermute | solution.py:51
  35.9 0.4 tables.1
  36.3 0.8 %collective-permute-done.14.refs_6_ = bf16[4,2560]{1,0:T(4,128)(2,1)S(1)} collective-permute-done((bf16[4,2560]{1,0:T(4,128)(2,1)S(1)}, bf16[4,2560]{1,0:T(4,128)(2,1)S(1)}, u32[]{:S(2)}, u32[]{:S(2)}) %collective-permute-start.14) | collective-permute-done | bytes 20512 | tf_op jit(solution)/shard_map/ppermute | solution.py:51
  37.1 2.1 %collective-permute-done.15.refs_7_ = bf16[4,2560]{1,0:T(4,128)(2,1)S(1)} collective-permute-done((bf16[4,2560]{1,0:T(4,128)(2,1)S(1)}, bf16[4,2560]{1,0:T(4,128)(2,1)S(1)}, u32[]{:S(2)}, u32[]{:S(2)}) %collective-permute-start.15) | collective-permute-done | bytes 20512 | tf_op jit(solution)/shard_map/ppermute | solution.py:51
  39.1 1.1 %final.1 = (bf16[4,2048]{1,0:T(4,128)(2,1)}, f32[16,64]{1,0:T(8,128)}) custom-call(f32[16,128]{1,0:T(8,128)S(1)} %get-tuple-element.30.refs_0_, bf16[128,128]{1,0:T(8,128)(2,1)S(1)} %get-tuple-element.31.refs_1_, bf16[16,128]{1,0:T(8,128)(2,1)S(1)} %get-tuple-element.32.refs_2_, bf16[16,2048]{1,0:T(8,128)(2,1)S(1)} %bitcast.2, ...), custom_call_target="tpu_custom_call" | custom-call | tf_op jit(solution)/shard_map/final/pallas_call | solution.py:524
  (12 shorter events, 0.3 us)
Async XLA Ops:
  1.5 6.4 %collective-permute-start.2 = (bf16[2,4,2176]{2,1,0:T(4,128)(2,1)S(1)}, bf16[2,4,2176]{2,1,0:T(4,128)(2,1)S(1)}, u32[]{:S(2)}, u32[]{:S(2)}) collective-permute-start(bf16[2,4,2176]{2,1,0:T(4,128)(2,1)S(1)} %prep.1.refs_0_), channel_id=1, source_target_pairs={{0,16},{1,17},{2,18},{3,19},{4,20},{5,21},{6,22},{7,23},{8,24},{9,... | collective-permute-start | bytes 104456 | tf_op jit(solution)/shard_map/ppermute | solution.py:51
  5.6 5.7 %collective-permute-start.1 = (bf16[2,4,2176]{2,1,0:T(4,128)(2,1)S(1)}, bf16[2,4,2176]{2,1,0:T(4,128)(2,1)S(1)}, u32[]{:S(2)}, u32[]{:S(2)}) collective-permute-start(bf16[2,4,2176]{2,1,0:T(4,128)(2,1)S(1)} %prep.1.refs_0_), channel_id=1, source_target_pairs={{0,24},{1,25},{2,26},{3,27},{4,28},{5,29},{6,30},{7,31},{8,16},{9,... | collective-permute-start | bytes 104456 | tf_op jit(solution)/shard_map/ppermute | solution.py:51
  6.9 4.4 %collective-permute-start = (bf16[2,4,2176]{2,1,0:T(4,128)(2,1)S(1)}, bf16[2,4,2176]{2,1,0:T(4,128)(2,1)S(1)}, u32[]{:S(2)}, u32[]{:S(2)}) collective-permute-start(bf16[2,4,2176]{2,1,0:T(4,128)(2,1)S(1)} %prep.1.refs_0_), channel_id=1, source_target_pairs={{0,8},{1,9},{2,10},{3,11},{4,12},{5,13},{6,14},{7,15},{8,0},{9,1},... | collective-permute-start | bytes 104456 | tf_op jit(solution)/shard_map/ppermute | solution.py:51
  11.4 7.5 %collective-permute-start.5 = (bf16[32,2176]{1,0:T(8,128)(2,1)S(1)}, bf16[32,2176]{1,0:T(8,128)(2,1)S(1)}, u32[]{:S(2)}, u32[]{:S(2)}) collective-permute-start(bf16[32,2176]{1,0:T(8,128)(2,1)S(1)} %join.1.block_in.refs_0_), channel_id=1, source_target_pairs={{0,5},{1,4},{2,7},{3,6},{4,1},{5,0},{6,3},{7,2},{8,13},{9,12},{10,... | collective-permute-start | bytes 417800 | tf_op jit(solution)/shard_map/ppermute | solution.py:51
  13.9 5.8 %collective-permute-start.4 = (bf16[32,2176]{1,0:T(8,128)(2,1)S(1)}, bf16[32,2176]{1,0:T(8,128)(2,1)S(1)}, u32[]{:S(2)}, u32[]{:S(2)}) collective-permute-start(bf16[32,2176]{1,0:T(8,128)(2,1)S(1)} %join.1.block_in.refs_0_), channel_id=1, source_target_pairs={{0,4},{1,5},{2,6},{3,7},{4,0},{5,1},{6,2},{7,3},{8,12},{9,13},{10,... | collective-permute-start | bytes 417800 | tf_op jit(solution)/shard_map/ppermute | solution.py:51
  14.4 5.3 %collective-permute-start.3 = (bf16[32,2176]{1,0:T(8,128)(2,1)S(1)}, bf16[32,2176]{1,0:T(8,128)(2,1)S(1)}, u32[]{:S(2)}, u32[]{:S(2)}) collective-permute-start(bf16[32,2176]{1,0:T(8,128)(2,1)S(1)} %join.1.block_in.refs_0_), channel_id=1, source_target_pairs={{0,1},{1,0},{2,3},{3,2},{4,5},{5,4},{6,7},{7,6},{8,9},{9,8},{10,11... | collective-permute-start | bytes 417800 | tf_op jit(solution)/shard_map/ppermute | solution.py:51
  17.4 2.8 %collective-permute-start.6 = (bf16[32,2176]{1,0:T(8,128)(2,1)S(1)}, bf16[32,2176]{1,0:T(8,128)(2,1)S(1)}, u32[]{:S(2)}, u32[]{:S(2)}) collective-permute-start(bf16[32,2176]{1,0:T(8,128)(2,1)S(1)} %get-tuple-element.23), channel_id=1, source_target_pairs={{0,2},{1,3},{2,0},{3,1},{4,6},{5,7},{6,4},{7,5},{8,10},{9,11},{10,... | collective-permute-start | bytes 417800 | tf_op jit(solution)/shard_map/ppermute | solution.py:51
  18.9 1.4 %collective-permute-start.9 = (bf16[32,2176]{1,0:T(8,128)(2,1)S(1)}, bf16[32,2176]{1,0:T(8,128)(2,1)S(1)}, u32[]{:S(2)}, u32[]{:S(2)}) collective-permute-start(bf16[32,2176]{1,0:T(8,128)(2,1)S(1)} %collective-permute-done.5.refs_3_), channel_id=1, source_target_pairs={{0,2},{1,3},{2,0},{3,1},{4,6},{5,7},{6,4},{7,5},{8,10},{9,11},{10,... | collective-permute-start | bytes 417800 | tf_op jit(solution)/shard_map/ppermute | solution.py:51
  19.6 1.4 %collective-permute-start.8 = (bf16[32,2176]{1,0:T(8,128)(2,1)S(1)}, bf16[32,2176]{1,0:T(8,128)(2,1)S(1)}, u32[]{:S(2)}, u32[]{:S(2)}) collective-permute-start(bf16[32,2176]{1,0:T(8,128)(2,1)S(1)} %collective-permute-done.4.refs_2_), channel_id=1, source_target_pairs={{0,2},{1,3},{2,0},{3,1},{4,6},{5,7},{6,4},{7,5},{8,10},{9,11},{10,... | collective-permute-start | bytes 417800 | tf_op jit(solution)/shard_map/ppermute | solution.py:51
  19.7 1.6 %collective-permute-start.7 = (bf16[32,2176]{1,0:T(8,128)(2,1)S(1)}, bf16[32,2176]{1,0:T(8,128)(2,1)S(1)}, u32[]{:S(2)}, u32[]{:S(2)}) collective-permute-start(bf16[32,2176]{1,0:T(8,128)(2,1)S(1)} %collective-permute-done.3.refs_1_), channel_id=1, source_target_pairs={{0,2},{1,3},{2,0},{3,1},{4,6},{5,7},{6,4},{7,5},{8,10},{9,11},{10,... | collective-permute-start | bytes 417800 | tf_op jit(solution)/shard_map/ppermute | solution.py:51
  23.3 1.6 %collective-permute-start.10 = (bf16[64,2176]{1,0:T(8,128)(2,1)S(1)}, bf16[64,2176]{1,0:T(8,128)(2,1)S(1)}, u32[]{:S(2)}, u32[]{:S(2)}) collective-permute-start(bf16[64,2176]{1,0:T(8,128)(2,1)S(1)} %get-tuple-element.28), channel_id=1, source_target_pairs={{0,2},{1,3},{2,0},{3,1},{4,6},{5,7},{6,4},{7,5},{8,10},{9,11},{10,... | collective-permute-start | bytes 835592 | tf_op jit(solution)/shard_map/ppermute | solution.py:51
  25.0 4.5 %collective-permute-start.11 = (bf16[16,2176]{1,0:T(8,128)(2,1)S(1)}, bf16[16,2176]{1,0:T(8,128)(2,1)S(1)}, u32[]{:S(2)}, u32[]{:S(2)}) collective-permute-start(bf16[16,2176]{1,0:T(8,128)(2,1)S(1)} %get-tuple-element.34), channel_id=1, source_target_pairs={{0,1},{1,0},{2,3},{3,2},{4,5},{5,4},{6,7},{7,6},{8,9},{9,8},{10,11... | collective-permute-start | bytes 208904 | tf_op jit(solution)/shard_map/ppermute | solution.py:51
  26.2 5.1 %collective-permute-start.12 = (bf16[16,2176]{1,0:T(8,128)(2,1)S(1)}, bf16[16,2176]{1,0:T(8,128)(2,1)S(1)}, u32[]{:S(2)}, u32[]{:S(2)}) collective-permute-start(bf16[16,2176]{1,0:T(8,128)(2,1)S(1)} %get-tuple-element.35), channel_id=1, source_target_pairs={{0,4},{1,5},{2,6},{3,7},{4,0},{5,1},{6,2},{7,3},{8,12},{9,13},{10,... | collective-permute-start | bytes 208904 | tf_op jit(solution)/shard_map/ppermute | solution.py:51
  27.0 5.2 %collective-permute-start.13 = (bf16[16,2176]{1,0:T(8,128)(2,1)S(1)}, bf16[16,2176]{1,0:T(8,128)(2,1)S(1)}, u32[]{:S(2)}, u32[]{:S(2)}) collective-permute-start(bf16[16,2176]{1,0:T(8,128)(2,1)S(1)} %get-tuple-element.36), channel_id=1, source_target_pairs={{0,5},{1,4},{2,7},{3,6},{4,1},{5,0},{6,3},{7,2},{8,13},{9,12},{10,... | collective-permute-start | bytes 208904 | tf_op jit(solution)/shard_map/ppermute | solution.py:51
  32.3 4.7 %collective-permute-start.14 = (bf16[4,2560]{1,0:T(4,128)(2,1)S(1)}, bf16[4,2560]{1,0:T(4,128)(2,1)S(1)}, u32[]{:S(2)}, u32[]{:S(2)}) collective-permute-start(bf16[4,2560]{1,0:T(4,128)(2,1)S(1)} %get-tuple-element.39), channel_id=1, source_target_pairs={{0,16},{1,17},{2,18},{3,19},{4,20},{5,21},{6,22},{7,23},{8,24},{9,... | collective-permute-start | bytes 61448 | tf_op jit(solution)/shard_map/ppermute | solution.py:51
  33.6 5.6 %collective-permute-start.15 = (bf16[4,2560]{1,0:T(4,128)(2,1)S(1)}, bf16[4,2560]{1,0:T(4,128)(2,1)S(1)}, u32[]{:S(2)}, u32[]{:S(2)}) collective-permute-start(bf16[4,2560]{1,0:T(4,128)(2,1)S(1)} %get-tuple-element.40), channel_id=1, source_target_pairs={{0,24},{1,25},{2,26},{3,27},{4,28},{5,29},{6,30},{7,31},{8,16},{9,... | collective-permute-start | bytes 61448 | tf_op jit(solution)/shard_map/ppermute | solution.py:51
  35.1 4.1 %copy-start = (bf16[2048,16]{0,1:T(8,128)(2,1)S(1)}, bf16[2048,16]{0,1:T(8,128)(2,1)}, u32[]{:S(2)}) copy-start(bf16[2048,16]{0,1:T(8,128)(2,1)} %param.12) | copy-start | bytes 196612
  35.1 4.1 %collective-permute-start.16 = (bf16[4,2560]{1,0:T(4,128)(2,1)S(1)}, bf16[4,2560]{1,0:T(4,128)(2,1)S(1)}, u32[]{:S(2)}, u32[]{:S(2)}) collective-permute-start(bf16[4,2560]{1,0:T(4,128)(2,1)S(1)} %get-tuple-element.41), channel_id=1, source_target_pairs={{0,8},{1,9},{2,10},{3,11},{4,12},{5,13},{6,14},{7,15},{8,0},{9,1},... | collective-permute-start | bytes 61448 | tf_op jit(solution)/shard_map/ppermute | solution.py:51
where the time goes:
time: 40.5 us; the launch traced here: 40.2 us
  starting transfers between devices  17.3 us (43%)
  waiting for transfers between devices  15.2 us (38%)
  Pallas kernels  7.08 us (17%)
  between operations  0.7 us (2%)
    ppermute x17, starting transfers between devices, swap(): lax.ppermute(block, AXES, [(i, i ^ mask[i >> core & 1]) for i in range(co...  17.3 us
    ppermute x17, waiting for transfers between devices, swap(): lax.ppermute(block, AXES, [(i, i ^ mask[i >> core & 1]) for i in range(co...  15.2 us
    pallas_call x1, Pallas kernels, on_device(): pl.pallas_call(functools.partial(load_kernel, chunks), out_shape=(pltpu.V...  2.48 us
    pallas_call x1, Pallas kernels, on_device(): pl.pallas_call(functools.partial(units_kernel, basis, group_rows, tok, ex...  2.11 us
    pallas_call x1, Pallas kernels, on_device(): pl.pallas_call(functools.partial(final_kernel, len(arrived), back_basis,...  1.1 us
    pallas_call x1, Pallas kernels, on_device(): pl.pallas_call(prep_kernel, out_shape=jax.ShapeDtypeStruct((2, tok, width...  0.82 us
  transfers between devices with their start and end apart: 17, of which 13 were waited for; matrix products, arithmetic and copies ran while one was open for 0% of the time, Pallas kernels for 7%

commit v1 on v0

--- a/solution.py
+++ b/solution.py
@@ -49,6 +49,20 @@
 
 def swap(block, mask, count, core):
     return lax.ppermute(block, AXES, [(i, i ^ mask[i >> core & 1]) for i in range(count)])
+
+
+REDUCE_STEPS = ((1, 3, 0, 2), (3, 2, 1, 0), (2, 0, 3, 1))
+
+
+def by_member(member, values):
+    total = values[0]
+    for k in range(1, len(values)):
+        total = jnp.where(member == k, values[k], total)
+    return total
+
+
+def shift(block, step, count, low):
+    return lax.ppermute(block, AXES, [(i, i ^ ((i >> low & 3) ^ step[i >> low & 3]) << low) for i in range(count)])
 
 
 def swaps(block, masks, count, core):
@@ -273,7 +287,7 @@
     put_scores(message_ref, padded_ref, width)
 
 
-def add_kernel(arrivals, positions, core_mask, *refs):
+def add_kernel(arrivals, positions, low, *refs):
     kept_ref, pieces_ref = refs[0], refs[1]
     arrived = refs[2 : 2 + arrivals]
     outs = refs[2 + arrivals :]
@@ -294,12 +308,14 @@
     rows = next_kept_ref.shape[0]
     next_kept_ref[...] = total_ref[0:rows, :]
     next_pieces_ref[...] = scores_ref[0 : next_pieces_ref.shape[0], :]
-    upper = own_index() & core_mask != 0
-    for (low, high), ref in zip(positions, sends):
-        first = low * rows
-        if low != high:
-            first = pl.multiple_of(jnp.where(upper, high, low) * rows, rows)
-        ref[:, 0:width] = total_ref[pl.ds(first, rows), :].astype(BF16)
+    chunks = [total_ref[j * rows : (j + 1) * rows, :] for j in range(total_ref.shape[0] // rows)]
+    member = own_index() >> low & 3
+    for position, ref in zip(positions, sends):
+        if isinstance(position, int):
+            chunk = chunks[position]
+        else:
+            chunk = by_member(member, [chunks[p] for p in position])
+        ref[:, 0:width] = chunk.astype(BF16)
         put_scores(ref, scores_ref, width)
 
 
@@ -334,7 +350,7 @@
     mine_ref[...] = jnp.where((row < tok) & (token == own * tok + row), 1.0, 0.0).astype(BF16)
 
 
-def final_kernel(arrivals, back_basis, core_mask, *refs):
+def final_kernel(arrivals, back_basis, core_mask, low, *refs):
     probs_ref, column_ref, mine_ref, router_ref, kept_ref, pieces_ref = refs[:6]
     arrived = refs[6 : 6 + arrivals]
     x_out, grad_out, x_ref, grad_ref, scores_ref, sems = refs[6 + arrivals :]
@@ -349,7 +365,14 @@
     wide = scores_ref.shape[0] // blocks
     sender = lax.broadcasted_iota(jnp.int32, (experts, wide), 1) // SCORE_PIECES
     ids = lax.broadcasted_iota(jnp.int32, (experts, wide), 0)
-    pick = jnp.where(((place_mask(sender, back_basis, own & core_mask != 0) ^ own) >> 1) == ids, 1.0, 0.0).astype(BF16)
+    mask = place_mask(sender, back_basis, own & core_mask != 0)
+    if low is not None:
+        member = own >> low & 3
+        source = sender >> len(back_basis)
+        for k, step in enumerate(REDUCE_STEPS):
+            come = by_member(member, [d ^ step.index(d) for d in range(4)]) << low
+            mask = mask ^ jnp.where(source == k + 1, come, 0)
+    pick = jnp.where(((mask ^ own) >> 1) == ids, 1.0, 0.0).astype(BF16)
     parts = []
     for b in range(blocks):
         block = scores_ref[...] if blocks == 1 else scores_ref[pl.ds(b, wide, stride=blocks), :]
@@ -389,7 +412,12 @@
     basis = [m for group in groups for m in group]
     back_groups = [near_first(group) for group in groups[:0:-1]] + [groups[0]]
     core_pair = (core_mask, core_mask)
+    low = (count - 1).bit_length() - 2 if len(groups[0]) == 2 else None
+    if low is not None:
+        back_groups = back_groups[:-1]
     back_basis = [core_pair] + [m for group in back_groups for m in group]
+    if low is not None:
+        back_groups = back_groups + [None]
     token_count = count * tok
     lanes = -(-PIECES * experts // LANES) * LANES
 
@@ -478,18 +506,20 @@
     tables = None
     rows_out = width // count
     for group, back_group in zip(groups[::-1], back_groups):
-        back_masks = group_masks(back_group)
-        positions = [
-            tuple([m[side] for m in group_masks(group)].index(mask[side]) for side in range(2)) for mask in back_masks[1:]
-        ]
-        radix = len(back_masks)
+        order = [m[0] for m in group_masks(group)]
+        if back_group is None:
+            positions = [[order.index((d ^ step[d]) << low) for d in range(4)] for step in REDUCE_STEPS]
+        else:
+            back_masks = group_masks(back_group)
+            positions = [order.index(m[0]) for m in back_masks[1:]]
+        radix = len(order)
         rows = kept.shape[0]
         next_rows = rows // radix
         size = pieces.shape[0] * (1 + len(arrived))
         extra = -(-size // next_rows) * LANES
         sends = [jax.ShapeDtypeStruct((next_rows, width + extra), BF16)] * (radix - 1)
         outs = pl.pallas_call(
-            functools.partial(add_kernel, len(arrived), positions, core_mask),
+            functools.partial(add_kernel, len(arrived), positions, low or 0),
             out_shape=[
                 jax.ShapeDtypeStruct((next_rows, width), F32),
                 jax.ShapeDtypeStruct((size, LANES), F32),
@@ -519,10 +549,13 @@
                 cost_estimate=pl.CostEstimate(flops=10**9, bytes_accessed=10**6, transcendentals=0),
                 name="tables",
             )(pieces, *blocks)
-        arrived = [swap(piece, m, count, core) for piece, m in zip(outs[2:], back_masks[1:])]
+        if back_group is None:
+            arrived = [shift(piece, step, count, low) for piece, step in zip(outs[2:], REDUCE_STEPS)]
+        else:
+            arrived = [swap(piece, m, count, core) for piece, m in zip(outs[2:], back_masks[1:])]
 
     x_grad, grad = pl.pallas_call(
-        functools.partial(final_kernel, len(arrived), back_basis, core_mask),
+        functools.partial(final_kernel, len(arrived), back_basis, core_mask, low),
         out_shape=(
             jax.ShapeDtypeStruct((tok, width), BF16),
             jax.ShapeDtypeStruct((experts, rows_out), F32),

time: 40.5 us -> 40.2 us (level)
  waiting for transfers between devices: 15.2 us -> 13.7 us
  starting transfers between devices: 17.3 us -> 18.4 us
    ppermute x0 -> x3, starting transfers between devices: none -> 4.66 us  [shift(): lax.ppermute(block, AXES, [(i, i ^ (i >> low & 3 ^ step[i >> low & 3]) <<...]
    ppermute x17 -> x14, starting transfers between devices: 17.3 us -> 13.8 us  [swap(): lax.ppermute(block, AXES, [(i, i ^ mask[i >> core & 1]) for i in range(co...]
    ppermute x17 -> x14, waiting for transfers between devices: 15.2 us -> 12.3 us  [swap(): lax.ppermute(block, AXES, [(i, i ^ mask[i >> core & 1]) for i in range(co...]
    ppermute x0 -> x3, waiting for transfers between devices: none -> 1.44 us  [shift(): lax.ppermute(block, AXES, [(i, i ^ (i >> low & 3 ^ step[i >> low & 3]) <<...]
where the time goes in v1:
time: 40.2 us; the launch traced here: 39.9 us
  starting transfers between devices  18.4 us (46%)
  waiting for transfers between devices  13.7 us (34%)
  Pallas kernels  7.09 us (18%)
  between operations  0.7 us (2%)
    ppermute x14, starting transfers between devices, swap(): lax.ppermute(block, AXES, [(i, i ^ mask[i >> core & 1]) for i in range(co...  13.8 us
    ppermute x14, waiting for transfers between devices, swap(): lax.ppermute(block, AXES, [(i, i ^ mask[i >> core & 1]) for i in range(co...  12.3 us
    ppermute x3, starting transfers between devices, shift(): lax.ppermute(block, AXES, [(i, i ^ (i >> low & 3 ^ step[i >> low & 3]) <<...  4.66 us
    pallas_call x1, Pallas kernels, on_device(): pl.pallas_call(functools.partial(load_kernel, chunks), out_shape=(pltpu.V...  2.48 us
    pallas_call x1, Pallas kernels, on_device(): pl.pallas_call(functools.partial(units_kernel, basis, group_rows, tok, ex...  2.11 us
    ppermute x3, waiting for transfers between devices, shift(): lax.ppermute(block, AXES, [(i, i ^ (i >> low & 3 ^ step[i >> low & 3]) <<...  1.44 us
    pallas_call x1, Pallas kernels, on_device(): pl.pallas_call(functools.partial(final_kernel, len(arrived), back_basis,...  1.1 us
    pallas_call x1, Pallas kernels, on_device(): pl.pallas_call(prep_kernel, out_shape=jax.ShapeDtypeStruct((2, tok, width...  0.82 us
  transfers between devices with their start and end apart: 17, of which 13 were waited for; matrix products, arithmetic and copies ran while one was open for 0% of the time, Pallas kernels for 7%

profile of v1, /device:TPU:0, one launch (start us, length us, event | category | flops | bytes accessed | tf_op | source)
XLA Modules:
  0.0 39.9 jit_solution(13426527045033679429)
XLA Ops:
  0.6 0.8 %prep.1.refs_0_ = bf16[2,4,2176]{2,1,0:T(4,128)(2,1)S(1)} custom-call(bf16[4,2048]{1,0:T(4,128)(2,1)} %tokens_in.1, bf16[4,2048]{1,0:T(4,128)(2,1)} %grad_in.1, f32[4,16]{1,0:T(4,128)} %logits_in.1, s32[4,8]{1,0:T(4,128)} %chosen_in.1), custom_call_target="tpu_custom_call" | custom-call | tf_op jit(solution)/shard_map/prep/pallas_call | solution.py:424
  1.5 4.1 %collective-permute-start.2 = (bf16[2,4,2176]{2,1,0:T(4,128)(2,1)S(1)}, bf16[2,4,2176]{2,1,0:T(4,128)(2,1)S(1)}, u32[]{:S(2)}, u32[]{:S(2)}) collective-permute-start(bf16[2,4,2176]{2,1,0:T(4,128)(2,1)S(1)} %prep.1.refs_0_), channel_id=1, source_target_pairs={{0,16},{1,17},{2,18},{3,19},{4,20},{5,21},{6,22},{7,23},{8,24},{9,... | collective-permute-start | bytes 104456 | tf_op jit(solution)/shard_map/ppermute | solution.py:51
  5.6 1.3 %collective-permute-start.1 = (bf16[2,4,2176]{2,1,0:T(4,128)(2,1)S(1)}, bf16[2,4,2176]{2,1,0:T(4,128)(2,1)S(1)}, u32[]{:S(2)}, u32[]{:S(2)}) collective-permute-start(bf16[2,4,2176]{2,1,0:T(4,128)(2,1)S(1)} %prep.1.refs_0_), channel_id=1, source_target_pairs={{0,24},{1,25},{2,26},{3,27},{4,28},{5,29},{6,30},{7,31},{8,16},{9,... | collective-permute-start | bytes 104456 | tf_op jit(solution)/shard_map/ppermute | solution.py:51
  6.9 0.2 collective-permute-start
  7.1 0.7 %collective-permute-done.2.refs_3_ = bf16[2,4,2176]{2,1,0:T(4,128)(2,1)S(1)} collective-permute-done((bf16[2,4,2176]{2,1,0:T(4,128)(2,1)S(1)}, bf16[2,4,2176]{2,1,0:T(4,128)(2,1)S(1)}, u32[]{:S(2)}, u32[]{:S(2)}) %collective-permute-start.2) | collective-permute-done | bytes 34848 | tf_op jit(solution)/shard_map/ppermute | solution.py:51
  7.9 3.4 %collective-permute-done.1.refs_2_ = bf16[2,4,2176]{2,1,0:T(4,128)(2,1)S(1)} collective-permute-done((bf16[2,4,2176]{2,1,0:T(4,128)(2,1)S(1)}, bf16[2,4,2176]{2,1,0:T(4,128)(2,1)S(1)}, u32[]{:S(2)}, u32[]{:S(2)}) %collective-permute-start.1) | collective-permute-done | bytes 34848 | tf_op jit(solution)/shard_map/ppermute | solution.py:51
  11.4 2.5 %collective-permute-start.5 = (bf16[32,2176]{1,0:T(8,128)(2,1)S(1)}, bf16[32,2176]{1,0:T(8,128)(2,1)S(1)}, u32[]{:S(2)}, u32[]{:S(2)}) collective-permute-start(bf16[32,2176]{1,0:T(8,128)(2,1)S(1)} %join.1.block_in.refs_0_), channel_id=1, source_target_pairs={{0,5},{1,4},{2,7},{3,6},{4,1},{5,0},{6,3},{7,2},{8,13},{9,12},{10,... | collective-permute-start | bytes 417800 | tf_op jit(solution)/shard_map/ppermute | solution.py:51
  13.9 0.5 %collective-permute-start.4 = (bf16[32,2176]{1,0:T(8,128)(2,1)S(1)}, bf16[32,2176]{1,0:T(8,128)(2,1)S(1)}, u32[]{:S(2)}, u32[]{:S(2)}) collective-permute-start(bf16[32,2176]{1,0:T(8,128)(2,1)S(1)} %join.1.block_in.refs_0_), channel_id=1, source_target_pairs={{0,4},{1,5},{2,6},{3,7},{4,0},{5,1},{6,2},{7,3},{8,12},{9,13},{10,... | collective-permute-start | bytes 417800 | tf_op jit(solution)/shard_map/ppermute | solution.py:51
  14.4 0.5 %collective-permute-start.3 = (bf16[32,2176]{1,0:T(8,128)(2,1)S(1)}, bf16[32,2176]{1,0:T(8,128)(2,1)S(1)}, u32[]{:S(2)}, u32[]{:S(2)}) collective-permute-start(bf16[32,2176]{1,0:T(8,128)(2,1)S(1)} %join.1.block_in.refs_0_), channel_id=1, source_target_pairs={{0,1},{1,0},{2,3},{3,2},{4,5},{5,4},{6,7},{7,6},{8,9},{9,8},{10,11... | collective-permute-start | bytes 417800 | tf_op jit(solution)/shard_map/ppermute | solution.py:51
  14.9 2.5 %load.1 = (bf16[32,2176]{1,0:T(8,128)(2,1)S(1)}, bf16[2048,768]{1,0:T(8,128)(2,1)S(1)}, bf16[384,2048]{1,0:T(8,128)(2,1)S(1)}) custom-call(bf16[32,2176]{1,0:T(8,128)(2,1)S(1)} %join.1.block_in.refs_0_, bf16[1,2048,384]{2,1,0:T(8,128)(2,1)} %gate_in.1, bf16[1,2048,384]{2,1,0:T(8,128)(2,1)} %up_in.1, bf16[1,384,2048]{2,1,0:T(8,128)(2,1)} %down_in.1), custom_call_target="tpu_custom_call" | custom-call | bytes 9437184 | tf_op jit(solution)/shard_map/load/pallas_call | solution.py:461
  17.5 1.4 %collective-permute-done.5.refs_3_ = bf16[32,2176]{1,0:T(8,128)(2,1)S(1)} collective-permute-done((bf16[32,2176]{1,0:T(8,128)(2,1)S(1)}, bf16[32,2176]{1,0:T(8,128)(2,1)S(1)}, u32[]{:S(2)}, u32[]{:S(2)}) %collective-permute-start.5) | collective-permute-done | bytes 139296 | tf_op jit(solution)/shard_map/ppermute | solution.py:51
  18.9 0.8 %collective-permute-done.4.refs_2_ = bf16[32,2176]{1,0:T(8,128)(2,1)S(1)} collective-permute-done((bf16[32,2176]{1,0:T(8,128)(2,1)S(1)}, bf16[32,2176]{1,0:T(8,128)(2,1)S(1)}, u32[]{:S(2)}, u32[]{:S(2)}) %collective-permute-start.4) | collective-permute-done | bytes 139296 | tf_op jit(solution)/shard_map/ppermute | solution.py:51
  19.7 0.5 %collective-permute-start.7 = (bf16[32,2176]{1,0:T(8,128)(2,1)S(1)}, bf16[32,2176]{1,0:T(8,128)(2,1)S(1)}, u32[]{:S(2)}, u32[]{:S(2)}) collective-permute-start(bf16[32,2176]{1,0:T(8,128)(2,1)S(1)} %collective-permute-done.3.refs_1_), channel_id=1, source_target_pairs={{0,2},{1,3},{2,0},{3,1},{4,6},{5,7},{6,4},{7,5},{8,10},{9,11},{10,... | collective-permute-start | bytes 417800 | tf_op jit(solution)/shard_map/ppermute | solution.py:51
  20.2 0.8 %collective-permute-done.8.refs_6_ = bf16[32,2176]{1,0:T(8,128)(2,1)S(1)} collective-permute-done((bf16[32,2176]{1,0:T(8,128)(2,1)S(1)}, bf16[32,2176]{1,0:T(8,128)(2,1)S(1)}, u32[]{:S(2)}, u32[]{:S(2)}) %collective-permute-start.8) | collective-permute-done | bytes 139296 | tf_op jit(solution)/shard_map/ppermute | solution.py:51
  21.0 0.2 collective-permute-done.7.refs_5_
  21.2 2.1 %units.1 = (f32[64,2048]{1,0:T(8,128)S(1)}, bf16[64,2176]{1,0:T(8,128)(2,1)S(1)}, f32[2,128]{1,0:T(2,128)S(1)}) custom-call(bf16[32,2176]{1,0:T(8,128)(2,1)S(1)} %join.1.block_in.refs_0_, bf16[32,2176]{1,0:T(8,128)(2,1)S(1)} %collective-permute-done.3.refs_1_, bf16[32,2176]{1,0:T(8,128)(2,1)S(1)} %collective-permute-done.4.refs_2_, ...), custom_call_target="tpu_custom_call" | custom-call | flops 1006632960 | bytes 5767168 | tf_op jit(solution)/shard_map/units/pallas_call | solution.py:483
  23.3 0.4 collective-permute-start.10
  23.7 1.2 %collective-permute-done.10.refs_2_ = bf16[64,2176]{1,0:T(8,128)(2,1)S(1)} collective-permute-done((bf16[64,2176]{1,0:T(8,128)(2,1)S(1)}, bf16[64,2176]{1,0:T(8,128)(2,1)S(1)}, u32[]{:S(2)}, u32[]{:S(2)}) %collective-permute-start.10) | collective-permute-done | bytes 278560 | tf_op jit(solution)/shard_map/ppermute | solution.py:51
  24.9 0.1 add.2
  25.0 1.2 %collective-permute-start.11 = (bf16[16,2176]{1,0:T(8,128)(2,1)S(1)}, bf16[16,2176]{1,0:T(8,128)(2,1)S(1)}, u32[]{:S(2)}, u32[]{:S(2)}) collective-permute-start(bf16[16,2176]{1,0:T(8,128)(2,1)S(1)} %get-tuple-element.34), channel_id=1, source_target_pairs={{0,1},{1,0},{2,3},{3,2},{4,5},{5,4},{6,7},{7,6},{8,9},{9,8},{10,11... | collective-permute-start | bytes 208904 | tf_op jit(solution)/shard_map/ppermute | solution.py:51
  26.2 0.8 %collective-permute-start.12 = (bf16[16,2176]{1,0:T(8,128)(2,1)S(1)}, bf16[16,2176]{1,0:T(8,128)(2,1)S(1)}, u32[]{:S(2)}, u32[]{:S(2)}) collective-permute-start(bf16[16,2176]{1,0:T(8,128)(2,1)S(1)} %get-tuple-element.35), channel_id=1, source_target_pairs={{0,4},{1,5},{2,6},{3,7},{4,0},{5,1},{6,2},{7,3},{8,12},{9,13},{10,... | collective-permute-start | bytes 208904 | tf_op jit(solution)/shard_map/ppermute | solution.py:51
  27.0 1.5 %collective-permute-start.13 = (bf16[16,2176]{1,0:T(8,128)(2,1)S(1)}, bf16[16,2176]{1,0:T(8,128)(2,1)S(1)}, u32[]{:S(2)}, u32[]{:S(2)}) collective-permute-start(bf16[16,2176]{1,0:T(8,128)(2,1)S(1)} %get-tuple-element.36), channel_id=1, source_target_pairs={{0,5},{1,4},{2,7},{3,6},{4,1},{5,0},{6,3},{7,2},{8,13},{9,12},{10,... | collective-permute-start | bytes 208904 | tf_op jit(solution)/shard_map/ppermute | solution.py:51
  28.6 0.9 %collective-permute-done.11.refs_2_ = bf16[16,2176]{1,0:T(8,128)(2,1)S(1)} collective-permute-done((bf16[16,2176]{1,0:T(8,128)(2,1)S(1)}, bf16[16,2176]{1,0:T(8,128)(2,1)S(1)}, u32[]{:S(2)}, u32[]{:S(2)}) %collective-permute-start.11) | collective-permute-done | bytes 69664 | tf_op jit(solution)/shard_map/ppermute | solution.py:51
  29.5 1.8 %collective-permute-done.12.refs_3_ = bf16[16,2176]{1,0:T(8,128)(2,1)S(1)} collective-permute-done((bf16[16,2176]{1,0:T(8,128)(2,1)S(1)}, bf16[16,2176]{1,0:T(8,128)(2,1)S(1)}, u32[]{:S(2)}, u32[]{:S(2)}) %collective-permute-start.12) | collective-permute-done | bytes 69664 | tf_op jit(solution)/shard_map/ppermute | solution.py:51
  31.3 1.0 %collective-permute-done.13.refs_4_ = bf16[16,2176]{1,0:T(8,128)(2,1)S(1)} collective-permute-done((bf16[16,2176]{1,0:T(8,128)(2,1)S(1)}, bf16[16,2176]{1,0:T(8,128)(2,1)S(1)}, u32[]{:S(2)}, u32[]{:S(2)}) %collective-permute-start.13) | collective-permute-done | bytes 69664 | tf_op jit(solution)/shard_map/ppermute | solution.py:51
  32.3 0.4 collective-permute-start.14
  32.7 2.3 %collective-permute-start.15 = (bf16[4,2560]{1,0:T(4,128)(2,1)S(1)}, bf16[4,2560]{1,0:T(4,128)(2,1)S(1)}, u32[]{:S(2)}, u32[]{:S(2)}) collective-permute-start(bf16[4,2560]{1,0:T(4,128)(2,1)S(1)} %get-tuple-element.40), channel_id=1, source_target_pairs={{0,24},{1,25},{2,26},{3,27},{4,28},{5,29},{6,30},{7,31},{8,16},{9,... | collective-permute-start | bytes 61448 | tf_op jit(solution)/shard_map/ppermute | solution.py:65
  35.0 1.9 %collective-permute-start.16 = (bf16[4,2560]{1,0:T(4,128)(2,1)S(1)}, bf16[4,2560]{1,0:T(4,128)(2,1)S(1)}, u32[]{:S(2)}, u32[]{:S(2)}) collective-permute-start(bf16[4,2560]{1,0:T(4,128)(2,1)S(1)} %get-tuple-element.41), channel_id=1, source_target_pairs={{0,16},{1,17},{2,18},{3,19},{4,20},{5,21},{6,22},{7,23},{8,0},{9,1... | collective-permute-start | bytes 61448 | tf_op jit(solution)/shard_map/ppermute | solution.py:65
  37.0 0.4 tables.1
  37.4 0.9 %collective-permute-done.15.refs_7_ = bf16[4,2560]{1,0:T(4,128)(2,1)S(1)} collective-permute-done((bf16[4,2560]{1,0:T(4,128)(2,1)S(1)}, bf16[4,2560]{1,0:T(4,128)(2,1)S(1)}, u32[]{:S(2)}, u32[]{:S(2)}) %collective-permute-start.15) | collective-permute-done | bytes 20512 | tf_op jit(solution)/shard_map/ppermute | solution.py:65
  38.3 0.5 %collective-permute-done.16.refs_8_ = bf16[4,2560]{1,0:T(4,128)(2,1)S(1)} collective-permute-done((bf16[4,2560]{1,0:T(4,128)(2,1)S(1)}, bf16[4,2560]{1,0:T(4,128)(2,1)S(1)}, u32[]{:S(2)}, u32[]{:S(2)}) %collective-permute-start.16) | collective-permute-done | bytes 20512 | tf_op jit(solution)/shard_map/ppermute | solution.py:65
  38.8 1.1 %final.1 = (bf16[4,2048]{1,0:T(4,128)(2,1)}, f32[16,64]{1,0:T(8,128)}) custom-call(f32[16,128]{1,0:T(8,128)S(1)} %get-tuple-element.30.refs_0_, bf16[128,128]{1,0:T(8,128)(2,1)S(1)} %get-tuple-element.31.refs_1_, bf16[16,128]{1,0:T(8,128)(2,1)S(1)} %get-tuple-element.32.refs_2_, bf16[16,2048]{1,0:T(8,128)(2,1)S(1)} %bitcast.2, ...), custom_call_target="tpu_custom_call" | custom-call | tf_op jit(solution)/shard_map/final/pallas_call | solution.py:557
  (12 shorter events, 0.3 us)
Async XLA Ops:
  1.5 6.4 %collective-permute-start.2 = (bf16[2,4,2176]{2,1,0:T(4,128)(2,1)S(1)}, bf16[2,4,2176]{2,1,0:T(4,128)(2,1)S(1)}, u32[]{:S(2)}, u32[]{:S(2)}) collective-permute-start(bf16[2,4,2176]{2,1,0:T(4,128)(2,1)S(1)} %prep.1.refs_0_), channel_id=1, source_target_pairs={{0,16},{1,17},{2,18},{3,19},{4,20},{5,21},{6,22},{7,23},{8,24},{9,... | collective-permute-start | bytes 104456 | tf_op jit(solution)/shard_map/ppermute | solution.py:51
  5.6 5.7 %collective-permute-start.1 = (bf16[2,4,2176]{2,1,0:T(4,128)(2,1)S(1)}, bf16[2,4,2176]{2,1,0:T(4,128)(2,1)S(1)}, u32[]{:S(2)}, u32[]{:S(2)}) collective-permute-start(bf16[2,4,2176]{2,1,0:T(4,128)(2,1)S(1)} %prep.1.refs_0_), channel_id=1, source_target_pairs={{0,24},{1,25},{2,26},{3,27},{4,28},{5,29},{6,30},{7,31},{8,16},{9,... | collective-permute-start | bytes 104456 | tf_op jit(solution)/shard_map/ppermute | solution.py:51
  6.9 4.4 %collective-permute-start = (bf16[2,4,2176]{2,1,0:T(4,128)(2,1)S(1)}, bf16[2,4,2176]{2,1,0:T(4,128)(2,1)S(1)}, u32[]{:S(2)}, u32[]{:S(2)}) collective-permute-start(bf16[2,4,2176]{2,1,0:T(4,128)(2,1)S(1)} %prep.1.refs_0_), channel_id=1, source_target_pairs={{0,8},{1,9},{2,10},{3,11},{4,12},{5,13},{6,14},{7,15},{8,0},{9,1},... | collective-permute-start | bytes 104456 | tf_op jit(solution)/shard_map/ppermute | solution.py:51
  11.4 7.5 %collective-permute-start.5 = (bf16[32,2176]{1,0:T(8,128)(2,1)S(1)}, bf16[32,2176]{1,0:T(8,128)(2,1)S(1)}, u32[]{:S(2)}, u32[]{:S(2)}) collective-permute-start(bf16[32,2176]{1,0:T(8,128)(2,1)S(1)} %join.1.block_in.refs_0_), channel_id=1, source_target_pairs={{0,5},{1,4},{2,7},{3,6},{4,1},{5,0},{6,3},{7,2},{8,13},{9,12},{10,... | collective-permute-start | bytes 417800 | tf_op jit(solution)/shard_map/ppermute | solution.py:51
  13.9 5.8 %collective-permute-start.4 = (bf16[32,2176]{1,0:T(8,128)(2,1)S(1)}, bf16[32,2176]{1,0:T(8,128)(2,1)S(1)}, u32[]{:S(2)}, u32[]{:S(2)}) collective-permute-start(bf16[32,2176]{1,0:T(8,128)(2,1)S(1)} %join.1.block_in.refs_0_), channel_id=1, source_target_pairs={{0,4},{1,5},{2,6},{3,7},{4,0},{5,1},{6,2},{7,3},{8,12},{9,13},{10,... | collective-permute-start | bytes 417800 | tf_op jit(solution)/shard_map/ppermute | solution.py:51
  14.4 5.3 %collective-permute-start.3 = (bf16[32,2176]{1,0:T(8,128)(2,1)S(1)}, bf16[32,2176]{1,0:T(8,128)(2,1)S(1)}, u32[]{:S(2)}, u32[]{:S(2)}) collective-permute-start(bf16[32,2176]{1,0:T(8,128)(2,1)S(1)} %join.1.block_in.refs_0_), channel_id=1, source_target_pairs={{0,1},{1,0},{2,3},{3,2},{4,5},{5,4},{6,7},{7,6},{8,9},{9,8},{10,11... | collective-permute-start | bytes 417800 | tf_op jit(solution)/shard_map/ppermute | solution.py:51
  17.4 2.8 %collective-permute-start.6 = (bf16[32,2176]{1,0:T(8,128)(2,1)S(1)}, bf16[32,2176]{1,0:T(8,128)(2,1)S(1)}, u32[]{:S(2)}, u32[]{:S(2)}) collective-permute-start(bf16[32,2176]{1,0:T(8,128)(2,1)S(1)} %get-tuple-element.23), channel_id=1, source_target_pairs={{0,2},{1,3},{2,0},{3,1},{4,6},{5,7},{6,4},{7,5},{8,10},{9,11},{10,... | collective-permute-start | bytes 417800 | tf_op jit(solution)/shard_map/ppermute | solution.py:51
  18.9 1.4 %collective-permute-start.9 = (bf16[32,2176]{1,0:T(8,128)(2,1)S(1)}, bf16[32,2176]{1,0:T(8,128)(2,1)S(1)}, u32[]{:S(2)}, u32[]{:S(2)}) collective-permute-start(bf16[32,2176]{1,0:T(8,128)(2,1)S(1)} %collective-permute-done.5.refs_3_), channel_id=1, source_target_pairs={{0,2},{1,3},{2,0},{3,1},{4,6},{5,7},{6,4},{7,5},{8,10},{9,11},{10,... | collective-permute-start | bytes 417800 | tf_op jit(solution)/shard_map/ppermute | solution.py:51
  19.6 1.4 %collective-permute-start.8 = (bf16[32,2176]{1,0:T(8,128)(2,1)S(1)}, bf16[32,2176]{1,0:T(8,128)(2,1)S(1)}, u32[]{:S(2)}, u32[]{:S(2)}) collective-permute-start(bf16[32,2176]{1,0:T(8,128)(2,1)S(1)} %collective-permute-done.4.refs_2_), channel_id=1, source_target_pairs={{0,2},{1,3},{2,0},{3,1},{4,6},{5,7},{6,4},{7,5},{8,10},{9,11},{10,... | collective-permute-start | bytes 417800 | tf_op jit(solution)/shard_map/ppermute | solution.py:51
  19.7 1.6 %collective-permute-start.7 = (bf16[32,2176]{1,0:T(8,128)(2,1)S(1)}, bf16[32,2176]{1,0:T(8,128)(2,1)S(1)}, u32[]{:S(2)}, u32[]{:S(2)}) collective-permute-start(bf16[32,2176]{1,0:T(8,128)(2,1)S(1)} %collective-permute-done.3.refs_1_), channel_id=1, source_target_pairs={{0,2},{1,3},{2,0},{3,1},{4,6},{5,7},{6,4},{7,5},{8,10},{9,11},{10,... | collective-permute-start | bytes 417800 | tf_op jit(solution)/shard_map/ppermute | solution.py:51
  23.3 1.6 %collective-permute-start.10 = (bf16[64,2176]{1,0:T(8,128)(2,1)S(1)}, bf16[64,2176]{1,0:T(8,128)(2,1)S(1)}, u32[]{:S(2)}, u32[]{:S(2)}) collective-permute-start(bf16[64,2176]{1,0:T(8,128)(2,1)S(1)} %get-tuple-element.28), channel_id=1, source_target_pairs={{0,2},{1,3},{2,0},{3,1},{4,6},{5,7},{6,4},{7,5},{8,10},{9,11},{10,... | collective-permute-start | bytes 835592 | tf_op jit(solution)/shard_map/ppermute | solution.py:51
  25.0 4.5 %collective-permute-start.11 = (bf16[16,2176]{1,0:T(8,128)(2,1)S(1)}, bf16[16,2176]{1,0:T(8,128)(2,1)S(1)}, u32[]{:S(2)}, u32[]{:S(2)}) collective-permute-start(bf16[16,2176]{1,0:T(8,128)(2,1)S(1)} %get-tuple-element.34), channel_id=1, source_target_pairs={{0,1},{1,0},{2,3},{3,2},{4,5},{5,4},{6,7},{7,6},{8,9},{9,8},{10,11... | collective-permute-start | bytes 208904 | tf_op jit(solution)/shard_map/ppermute | solution.py:51
  26.2 5.1 %collective-permute-start.12 = (bf16[16,2176]{1,0:T(8,128)(2,1)S(1)}, bf16[16,2176]{1,0:T(8,128)(2,1)S(1)}, u32[]{:S(2)}, u32[]{:S(2)}) collective-permute-start(bf16[16,2176]{1,0:T(8,128)(2,1)S(1)} %get-tuple-element.35), channel_id=1, source_target_pairs={{0,4},{1,5},{2,6},{3,7},{4,0},{5,1},{6,2},{7,3},{8,12},{9,13},{10,... | collective-permute-start | bytes 208904 | tf_op jit(solution)/shard_map/ppermute | solution.py:51
  27.0 5.2 %collective-permute-start.13 = (bf16[16,2176]{1,0:T(8,128)(2,1)S(1)}, bf16[16,2176]{1,0:T(8,128)(2,1)S(1)}, u32[]{:S(2)}, u32[]{:S(2)}) collective-permute-start(bf16[16,2176]{1,0:T(8,128)(2,1)S(1)} %get-tuple-element.36), channel_id=1, source_target_pairs={{0,5},{1,4},{2,7},{3,6},{4,1},{5,0},{6,3},{7,2},{8,13},{9,12},{10,... | collective-permute-start | bytes 208904 | tf_op jit(solution)/shard_map/ppermute | solution.py:51
  32.3 5.1 %collective-permute-start.14 = (bf16[4,2560]{1,0:T(4,128)(2,1)S(1)}, bf16[4,2560]{1,0:T(4,128)(2,1)S(1)}, u32[]{:S(2)}, u32[]{:S(2)}) collective-permute-start(bf16[4,2560]{1,0:T(4,128)(2,1)S(1)} %get-tuple-element.39), channel_id=1, source_target_pairs={{0,8},{1,9},{2,10},{3,11},{4,12},{5,13},{6,14},{7,15},{8,24},{9,25... | collective-permute-start | bytes 61448 | tf_op jit(solution)/shard_map/ppermute | solution.py:65
  32.7 5.6 %collective-permute-start.15 = (bf16[4,2560]{1,0:T(4,128)(2,1)S(1)}, bf16[4,2560]{1,0:T(4,128)(2,1)S(1)}, u32[]{:S(2)}, u32[]{:S(2)}) collective-permute-start(bf16[4,2560]{1,0:T(4,128)(2,1)S(1)} %get-tuple-element.40), channel_id=1, source_target_pairs={{0,24},{1,25},{2,26},{3,27},{4,28},{5,29},{6,30},{7,31},{8,16},{9,... | collective-permute-start | bytes 61448 | tf_op jit(solution)/shard_map/ppermute | solution.py:65
  35.0 3.8 %copy-start = (bf16[2048,16]{0,1:T(8,128)(2,1)S(1)}, bf16[2048,16]{0,1:T(8,128)(2,1)}, u32[]{:S(2)}) copy-start(bf16[2048,16]{0,1:T(8,128)(2,1)} %param.12) | copy-start | bytes 196612
  35.0 3.8 %collective-permute-start.16 = (bf16[4,2560]{1,0:T(4,128)(2,1)S(1)}, bf16[4,2560]{1,0:T(4,128)(2,1)S(1)}, u32[]{:S(2)}, u32[]{:S(2)}) collective-permute-start(bf16[4,2560]{1,0:T(4,128)(2,1)S(1)} %get-tuple-element.41), channel_id=1, source_target_pairs={{0,16},{1,17},{2,18},{3,19},{4,20},{5,21},{6,22},{7,23},{8,0},{9,1... | collective-permute-start | bytes 61448 | tf_op jit(solution)/shard_map/ppermute | solution.py:65

commit v2 on v1

--- a/solution.py
+++ b/solution.py
@@ -51,7 +51,8 @@
     return lax.ppermute(block, AXES, [(i, i ^ mask[i >> core & 1]) for i in range(count)])
 
 
-REDUCE_STEPS = ((1, 3, 0, 2), (3, 2, 1, 0), (2, 0, 3, 1))
+GATHER_STEPS = ((2, 3, 1, 0), (3, 2, 0, 1), (1, 0, 3, 2))
+REDUCE_STEPS = ((1, 2, 3, 0), (2, 3, 0, 1), (3, 0, 1, 2))
 
 
 def by_member(member, values):
@@ -168,14 +169,20 @@
         copy.wait()
 
 
-def join_kernel(*refs):
+def join_kernel(order, low, *refs):
     blocks, out_ref, rows_ref = forward(refs[:-2]), refs[-2], refs[-1]
     count = len(blocks)
     tok = blocks[0].shape[1]
+    member = own_index() >> low & 3
     for kind in range(2):
-        for j, ref in enumerate(blocks):
+        rows = [ref[kind].astype(F32) for ref in blocks]
+        if order is not None:
+            come = [[d ^ step.index(d) for d in range(4)] for step in GATHER_STEPS]
+            places = [[[c[d] for c in come].index(mask) for d in range(4)] for mask in order[1:]]
+            rows = rows[:1] + [by_member(member, [rows[1 + k] for k in place]) for place in places]
+        for j, value in enumerate(rows):
             first = (kind * count + j) * tok
-            rows_ref[first : first + tok, :] = ref[kind].astype(F32)
+            rows_ref[first : first + tok, :] = value
     out_ref[...] = rows_ref[...].astype(BF16)
 
 
@@ -435,11 +442,15 @@
         name="prep",
     )(*in_hbm(tokens, grad_out, router_logits, selected))
 
-    masks = group_masks(groups[0])
-    blocks = [block] + swaps(block, masks[1:], count, core)
+    order = None
+    if low is None:
+        blocks = [block] + swaps(block, group_masks(groups[0])[1:], count, core)
+    else:
+        order = [m[0] >> low for m in group_masks(groups[0])]
+        blocks = [block] + [shift(block, step, count, low) for step in GATHER_STEPS]
     group_rows = tok * len(blocks)
     block = pl.pallas_call(
-        join_kernel,
+        functools.partial(join_kernel, order, low or 0),
         out_shape=jax.ShapeDtypeStruct((2 * group_rows, width + lanes), BF16),
         in_specs=[VMEM_SPEC] * len(blocks),
         out_specs=VMEM_SPEC,

time: 40.2 us -> 40.9 us (1.017)
  waiting for transfers between devices: 13.7 us -> 14.4 us
    ppermute x3 -> x6, starting transfers between devices: 4.66 us -> 10.4 us  [shift(): lax.ppermute(block, AXES, [(i, i ^ (i >> low & 3 ^ step[i >> low & 3]) <<...]
    ppermute x14 -> x11, starting transfers between devices: 13.8 us -> 8.08 us  [swap(): lax.ppermute(block, AXES, [(i, i ^ mask[i >> core & 1]) for i in range(co...]
    ppermute x3 -> x6, waiting for transfers between devices: 1.44 us -> 6.3 us  [shift(): lax.ppermute(block, AXES, [(i, i ^ (i >> low & 3 ^ step[i >> low & 3]) <<...]
    ppermute x14 -> x11, waiting for transfers between devices: 12.3 us -> 8.11 us  [swap(): lax.ppermute(block, AXES, [(i, i ^ mask[i >> core & 1]) for i in range(co...]
  transfers between devices with their start and end apart: 17 -> 17, of which waited for: 13 -> 15; matrix products, arithmetic and copies ran while one was open for 0% -> 0% of each run, Pallas kernels for 7% -> 7%
where the time goes in v2:
time: 40.9 us; the launch traced here: 40.7 us
  starting transfers between devices  18.4 us (45%)
  waiting for transfers between devices  14.4 us (35%)
  Pallas kernels  7.11 us (17%)
  between operations  0.7 us (2%)
    ppermute x6, starting transfers between devices, shift(): lax.ppermute(block, AXES, [(i, i ^ (i >> low & 3 ^ step[i >> low & 3]) <<...  10.4 us
    ppermute x11, waiting for transfers between devices, swap(): lax.ppermute(block, AXES, [(i, i ^ mask[i >> core & 1]) for i in range(co...  8.11 us
    ppermute x11, starting transfers between devices, swap(): lax.ppermute(block, AXES, [(i, i ^ mask[i >> core & 1]) for i in range(co...  8.08 us
    ppermute x6, waiting for transfers between devices, shift(): lax.ppermute(block, AXES, [(i, i ^ (i >> low & 3 ^ step[i >> low & 3]) <<...  6.3 us
    pallas_call x1, Pallas kernels, on_device(): pl.pallas_call(functools.partial(load_kernel, chunks), out_shape=(pltpu.V...  2.48 us
    pallas_call x1, Pallas kernels, on_device(): pl.pallas_call(functools.partial(units_kernel, basis, group_rows, tok, ex...  2.11 us
    pallas_call x1, Pallas kernels, on_device(): pl.pallas_call(functools.partial(final_kernel, len(arrived), back_basis,...  1.11 us
    pallas_call x1, Pallas kernels, on_device(): pl.pallas_call(prep_kernel, out_shape=jax.ShapeDtypeStruct((2, tok, width...  0.82 us
  transfers between devices with their start and end apart: 17, of which 15 were waited for; matrix products, arithmetic and copies ran while one was open for 0% of the time, Pallas kernels for 7%

profile of v2, /device:TPU:0, one launch (start us, length us, event | category | flops | bytes accessed | tf_op | source)
XLA Modules:
  0.0 40.7 jit_solution(14205764877008399038)
XLA Ops:
  0.6 0.8 %prep.1.refs_0_ = bf16[2,4,2176]{2,1,0:T(4,128)(2,1)S(1)} custom-call(bf16[4,2048]{1,0:T(4,128)(2,1)} %tokens_in.1, bf16[4,2048]{1,0:T(4,128)(2,1)} %grad_in.1, f32[4,16]{1,0:T(4,128)} %logits_in.1, s32[4,8]{1,0:T(4,128)} %chosen_in.1), custom_call_target="tpu_custom_call" | custom-call | tf_op jit(solution)/shard_map/prep/pallas_call | solution.py:431
  1.5 4.1 %collective-permute-start.2 = (bf16[2,4,2176]{2,1,0:T(4,128)(2,1)S(1)}, bf16[2,4,2176]{2,1,0:T(4,128)(2,1)S(1)}, u32[]{:S(2)}, u32[]{:S(2)}) collective-permute-start(bf16[2,4,2176]{2,1,0:T(4,128)(2,1)S(1)} %prep.1.refs_0_), channel_id=1, source_target_pairs={{0,16},{1,17},{2,18},{3,19},{4,20},{5,21},{6,22},{7,23},{8,24},{9,... | collective-permute-start | bytes 104456 | tf_op jit(solution)/shard_map/ppermute | solution.py:66
  5.5 1.1 %collective-permute-start.1 = (bf16[2,4,2176]{2,1,0:T(4,128)(2,1)S(1)}, bf16[2,4,2176]{2,1,0:T(4,128)(2,1)S(1)}, u32[]{:S(2)}, u32[]{:S(2)}) collective-permute-start(bf16[2,4,2176]{2,1,0:T(4,128)(2,1)S(1)} %prep.1.refs_0_), channel_id=1, source_target_pairs={{0,24},{1,25},{2,26},{3,27},{4,28},{5,29},{6,30},{7,31},{8,16},{9,... | collective-permute-start | bytes 104456 | tf_op jit(solution)/shard_map/ppermute | solution.py:66
  6.6 0.5 %collective-permute-start = (bf16[2,4,2176]{2,1,0:T(4,128)(2,1)S(1)}, bf16[2,4,2176]{2,1,0:T(4,128)(2,1)S(1)}, u32[]{:S(2)}, u32[]{:S(2)}) collective-permute-start(bf16[2,4,2176]{2,1,0:T(4,128)(2,1)S(1)} %prep.1.refs_0_), channel_id=1, source_target_pairs={{0,8},{1,9},{2,10},{3,11},{4,12},{5,13},{6,14},{7,15},{8,0},{9,1},... | collective-permute-start | bytes 104456 | tf_op jit(solution)/shard_map/ppermute | solution.py:66
  7.1 1.3 %collective-permute-done.2.refs_3_ = bf16[2,4,2176]{2,1,0:T(4,128)(2,1)S(1)} collective-permute-done((bf16[2,4,2176]{2,1,0:T(4,128)(2,1)S(1)}, bf16[2,4,2176]{2,1,0:T(4,128)(2,1)S(1)}, u32[]{:S(2)}, u32[]{:S(2)}) %collective-permute-start.2) | collective-permute-done | bytes 34848 | tf_op jit(solution)/shard_map/ppermute | solution.py:66
  8.5 1.9 %collective-permute-done.1.refs_2_ = bf16[2,4,2176]{2,1,0:T(4,128)(2,1)S(1)} collective-permute-done((bf16[2,4,2176]{2,1,0:T(4,128)(2,1)S(1)}, bf16[2,4,2176]{2,1,0:T(4,128)(2,1)S(1)}, u32[]{:S(2)}, u32[]{:S(2)}) %collective-permute-start.1) | collective-permute-done | bytes 34848 | tf_op jit(solution)/shard_map/ppermute | solution.py:66
  10.4 0.4 collective-permute-done.refs_1_
  10.8 2.5 %collective-permute-start.5 = (bf16[32,2176]{1,0:T(8,128)(2,1)S(1)}, bf16[32,2176]{1,0:T(8,128)(2,1)S(1)}, u32[]{:S(2)}, u32[]{:S(2)}) collective-permute-start(bf16[32,2176]{1,0:T(8,128)(2,1)S(1)} %join.1.block_in.refs_0_), channel_id=1, source_target_pairs={{0,5},{1,4},{2,7},{3,6},{4,1},{5,0},{6,3},{7,2},{8,13},{9,12},{10,... | collective-permute-start | bytes 417800 | tf_op jit(solution)/shard_map/ppermute | solution.py:51
  13.3 0.5 %collective-permute-start.4 = (bf16[32,2176]{1,0:T(8,128)(2,1)S(1)}, bf16[32,2176]{1,0:T(8,128)(2,1)S(1)}, u32[]{:S(2)}, u32[]{:S(2)}) collective-permute-start(bf16[32,2176]{1,0:T(8,128)(2,1)S(1)} %join.1.block_in.refs_0_), channel_id=1, source_target_pairs={{0,4},{1,5},{2,6},{3,7},{4,0},{5,1},{6,2},{7,3},{8,12},{9,13},{10,... | collective-permute-start | bytes 417800 | tf_op jit(solution)/shard_map/ppermute | solution.py:51
  13.8 0.5 %collective-permute-start.3 = (bf16[32,2176]{1,0:T(8,128)(2,1)S(1)}, bf16[32,2176]{1,0:T(8,128)(2,1)S(1)}, u32[]{:S(2)}, u32[]{:S(2)}) collective-permute-start(bf16[32,2176]{1,0:T(8,128)(2,1)S(1)} %join.1.block_in.refs_0_), channel_id=1, source_target_pairs={{0,1},{1,0},{2,3},{3,2},{4,5},{5,4},{6,7},{7,6},{8,9},{9,8},{10,11... | collective-permute-start | bytes 417800 | tf_op jit(solution)/shard_map/ppermute | solution.py:51
  14.4 2.5 %load.1 = (bf16[32,2176]{1,0:T(8,128)(2,1)S(1)}, bf16[2048,768]{1,0:T(8,128)(2,1)S(1)}, bf16[384,2048]{1,0:T(8,128)(2,1)S(1)}) custom-call(bf16[32,2176]{1,0:T(8,128)(2,1)S(1)} %join.1.block_in.refs_0_, bf16[1,2048,384]{2,1,0:T(8,128)(2,1)} %gate_in.1, bf16[1,2048,384]{2,1,0:T(8,128)(2,1)} %up_in.1, bf16[1,384,2048]{2,1,0:T(8,128)(2,1)} %down_in.1), custom_call_target="tpu_custom_call" | custom-call | bytes 9437184 | tf_op jit(solution)/shard_map/load/pallas_call | solution.py:472
  16.9 1.5 %collective-permute-done.5.refs_3_ = bf16[32,2176]{1,0:T(8,128)(2,1)S(1)} collective-permute-done((bf16[32,2176]{1,0:T(8,128)(2,1)S(1)}, bf16[32,2176]{1,0:T(8,128)(2,1)S(1)}, u32[]{:S(2)}, u32[]{:S(2)}) %collective-permute-start.5) | collective-permute-done | bytes 139296 | tf_op jit(solution)/shard_map/ppermute | solution.py:51
  18.4 0.7 %collective-permute-done.4.refs_2_ = bf16[32,2176]{1,0:T(8,128)(2,1)S(1)} collective-permute-done((bf16[32,2176]{1,0:T(8,128)(2,1)S(1)}, bf16[32,2176]{1,0:T(8,128)(2,1)S(1)}, u32[]{:S(2)}, u32[]{:S(2)}) %collective-permute-start.4) | collective-permute-done | bytes 139296 | tf_op jit(solution)/shard_map/ppermute | solution.py:51
  19.1 0.5 %collective-permute-start.7 = (bf16[32,2176]{1,0:T(8,128)(2,1)S(1)}, bf16[32,2176]{1,0:T(8,128)(2,1)S(1)}, u32[]{:S(2)}, u32[]{:S(2)}) collective-permute-start(bf16[32,2176]{1,0:T(8,128)(2,1)S(1)} %collective-permute-done.3.refs_1_), channel_id=1, source_target_pairs={{0,2},{1,3},{2,0},{3,1},{4,6},{5,7},{6,4},{7,5},{8,10},{9,11},{10,... | collective-permute-start | bytes 417800 | tf_op jit(solution)/shard_map/ppermute | solution.py:51
  19.8 0.7 %collective-permute-done.8.refs_6_ = bf16[32,2176]{1,0:T(8,128)(2,1)S(1)} collective-permute-done((bf16[32,2176]{1,0:T(8,128)(2,1)S(1)}, bf16[32,2176]{1,0:T(8,128)(2,1)S(1)}, u32[]{:S(2)}, u32[]{:S(2)}) %collective-permute-start.8) | collective-permute-done | bytes 139296 | tf_op jit(solution)/shard_map/ppermute | solution.py:51
  20.7 2.1 %units.1 = (f32[64,2048]{1,0:T(8,128)S(1)}, bf16[64,2176]{1,0:T(8,128)(2,1)S(1)}, f32[2,128]{1,0:T(2,128)S(1)}) custom-call(bf16[32,2176]{1,0:T(8,128)(2,1)S(1)} %join.1.block_in.refs_0_, bf16[32,2176]{1,0:T(8,128)(2,1)S(1)} %collective-permute-done.3.refs_1_, bf16[32,2176]{1,0:T(8,128)(2,1)S(1)} %collective-permute-done.4.refs_2_, ...), custom_call_target="tpu_custom_call" | custom-call | flops 1006632960 | bytes 5767168 | tf_op jit(solution)/shard_map/units/pallas_call | solution.py:494
  22.8 0.4 collective-permute-start.10
  23.2 1.2 %collective-permute-done.10.refs_2_ = bf16[64,2176]{1,0:T(8,128)(2,1)S(1)} collective-permute-done((bf16[64,2176]{1,0:T(8,128)(2,1)S(1)}, bf16[64,2176]{1,0:T(8,128)(2,1)S(1)}, u32[]{:S(2)}, u32[]{:S(2)}) %collective-permute-start.10) | collective-permute-done | bytes 278560 | tf_op jit(solution)/shard_map/ppermute | solution.py:51
  24.5 1.3 %collective-permute-start.11 = (bf16[16,2176]{1,0:T(8,128)(2,1)S(1)}, bf16[16,2176]{1,0:T(8,128)(2,1)S(1)}, u32[]{:S(2)}, u32[]{:S(2)}) collective-permute-start(bf16[16,2176]{1,0:T(8,128)(2,1)S(1)} %get-tuple-element.34), channel_id=1, source_target_pairs={{0,1},{1,0},{2,3},{3,2},{4,5},{5,4},{6,7},{7,6},{8,9},{9,8},{10,11... | collective-permute-start | bytes 208904 | tf_op jit(solution)/shard_map/ppermute | solution.py:51
  25.8 0.7 %collective-permute-start.12 = (bf16[16,2176]{1,0:T(8,128)(2,1)S(1)}, bf16[16,2176]{1,0:T(8,128)(2,1)S(1)}, u32[]{:S(2)}, u32[]{:S(2)}) collective-permute-start(bf16[16,2176]{1,0:T(8,128)(2,1)S(1)} %get-tuple-element.35), channel_id=1, source_target_pairs={{0,4},{1,5},{2,6},{3,7},{4,0},{5,1},{6,2},{7,3},{8,12},{9,13},{10,... | collective-permute-start | bytes 208904 | tf_op jit(solution)/shard_map/ppermute | solution.py:51
  26.5 1.5 %collective-permute-start.13 = (bf16[16,2176]{1,0:T(8,128)(2,1)S(1)}, bf16[16,2176]{1,0:T(8,128)(2,1)S(1)}, u32[]{:S(2)}, u32[]{:S(2)}) collective-permute-start(bf16[16,2176]{1,0:T(8,128)(2,1)S(1)} %get-tuple-element.36), channel_id=1, source_target_pairs={{0,5},{1,4},{2,7},{3,6},{4,1},{5,0},{6,3},{7,2},{8,13},{9,12},{10,... | collective-permute-start | bytes 208904 | tf_op jit(solution)/shard_map/ppermute | solution.py:51
  28.0 0.9 %collective-permute-done.11.refs_2_ = bf16[16,2176]{1,0:T(8,128)(2,1)S(1)} collective-permute-done((bf16[16,2176]{1,0:T(8,128)(2,1)S(1)}, bf16[16,2176]{1,0:T(8,128)(2,1)S(1)}, u32[]{:S(2)}, u32[]{:S(2)}) %collective-permute-start.11) | collective-permute-done | bytes 69664 | tf_op jit(solution)/shard_map/ppermute | solution.py:51
  29.0 1.9 %collective-permute-done.12.refs_3_ = bf16[16,2176]{1,0:T(8,128)(2,1)S(1)} collective-permute-done((bf16[16,2176]{1,0:T(8,128)(2,1)S(1)}, bf16[16,2176]{1,0:T(8,128)(2,1)S(1)}, u32[]{:S(2)}, u32[]{:S(2)}) %collective-permute-start.12) | collective-permute-done | bytes 69664 | tf_op jit(solution)/shard_map/ppermute | solution.py:51
  30.9 0.9 %collective-permute-done.13.refs_4_ = bf16[16,2176]{1,0:T(8,128)(2,1)S(1)} collective-permute-done((bf16[16,2176]{1,0:T(8,128)(2,1)S(1)}, bf16[16,2176]{1,0:T(8,128)(2,1)S(1)}, u32[]{:S(2)}, u32[]{:S(2)}) %collective-permute-start.13) | collective-permute-done | bytes 69664 | tf_op jit(solution)/shard_map/ppermute | solution.py:51
  31.8 1.3 %collective-permute-start.14 = (bf16[4,2560]{1,0:T(4,128)(2,1)S(1)}, bf16[4,2560]{1,0:T(4,128)(2,1)S(1)}, u32[]{:S(2)}, u32[]{:S(2)}) collective-permute-start(bf16[4,2560]{1,0:T(4,128)(2,1)S(1)} %get-tuple-element.39), channel_id=1, source_target_pairs={{0,8},{1,9},{2,10},{3,11},{4,12},{5,13},{6,14},{7,15},{8,16},{9,17... | collective-permute-start | bytes 61448 | tf_op jit(solution)/shard_map/ppermute | solution.py:66
  33.1 2.7 %collective-permute-start.15 = (bf16[4,2560]{1,0:T(4,128)(2,1)S(1)}, bf16[4,2560]{1,0:T(4,128)(2,1)S(1)}, u32[]{:S(2)}, u32[]{:S(2)}) collective-permute-start(bf16[4,2560]{1,0:T(4,128)(2,1)S(1)} %get-tuple-element.40), channel_id=1, source_target_pairs={{0,16},{1,17},{2,18},{3,19},{4,20},{5,21},{6,22},{7,23},{8,24},{9,... | collective-permute-start | bytes 61448 | tf_op jit(solution)/shard_map/ppermute | solution.py:66
  35.8 0.7 %collective-permute-start.16 = (bf16[4,2560]{1,0:T(4,128)(2,1)S(1)}, bf16[4,2560]{1,0:T(4,128)(2,1)S(1)}, u32[]{:S(2)}, u32[]{:S(2)}) collective-permute-start(bf16[4,2560]{1,0:T(4,128)(2,1)S(1)} %get-tuple-element.41), channel_id=1, source_target_pairs={{0,24},{1,25},{2,26},{3,27},{4,28},{5,29},{6,30},{7,31},{8,0},{9,1... | collective-permute-start | bytes 61448 | tf_op jit(solution)/shard_map/ppermute | solution.py:66
  36.5 0.4 tables.1
  36.9 0.6 %collective-permute-done.14.refs_6_ = bf16[4,2560]{1,0:T(4,128)(2,1)S(1)} collective-permute-done((bf16[4,2560]{1,0:T(4,128)(2,1)S(1)}, bf16[4,2560]{1,0:T(4,128)(2,1)S(1)}, u32[]{:S(2)}, u32[]{:S(2)}) %collective-permute-start.14) | collective-permute-done | bytes 20512 | tf_op jit(solution)/shard_map/ppermute | solution.py:66
  37.4 0.3 collective-permute-done.15.refs_7_
  37.7 1.8 %collective-permute-done.16.refs_8_ = bf16[4,2560]{1,0:T(4,128)(2,1)S(1)} collective-permute-done((bf16[4,2560]{1,0:T(4,128)(2,1)S(1)}, bf16[4,2560]{1,0:T(4,128)(2,1)S(1)}, u32[]{:S(2)}, u32[]{:S(2)}) %collective-permute-start.16) | collective-permute-done | bytes 20512 | tf_op jit(solution)/shard_map/ppermute | solution.py:66
  39.5 1.1 %final.1 = (bf16[4,2048]{1,0:T(4,128)(2,1)}, f32[16,64]{1,0:T(8,128)}) custom-call(f32[16,128]{1,0:T(8,128)S(1)} %get-tuple-element.30.refs_0_, bf16[128,128]{1,0:T(8,128)(2,1)S(1)} %get-tuple-element.31.refs_1_, bf16[16,128]{1,0:T(8,128)(2,1)S(1)} %get-tuple-element.32.refs_2_, bf16[16,2048]{1,0:T(8,128)(2,1)S(1)} %bitcast.2, ...), custom_call_target="tpu_custom_call" | custom-call | tf_op jit(solution)/shard_map/final/pallas_call | solution.py:568
  (12 shorter events, 0.6 us)
Async XLA Ops:
  1.5 7.0 %collective-permute-start.2 = (bf16[2,4,2176]{2,1,0:T(4,128)(2,1)S(1)}, bf16[2,4,2176]{2,1,0:T(4,128)(2,1)S(1)}, u32[]{:S(2)}, u32[]{:S(2)}) collective-permute-start(bf16[2,4,2176]{2,1,0:T(4,128)(2,1)S(1)} %prep.1.refs_0_), channel_id=1, source_target_pairs={{0,16},{1,17},{2,18},{3,19},{4,20},{5,21},{6,22},{7,23},{8,24},{9,... | collective-permute-start | bytes 104456 | tf_op jit(solution)/shard_map/ppermute | solution.py:66
  5.5 4.9 %collective-permute-start.1 = (bf16[2,4,2176]{2,1,0:T(4,128)(2,1)S(1)}, bf16[2,4,2176]{2,1,0:T(4,128)(2,1)S(1)}, u32[]{:S(2)}, u32[]{:S(2)}) collective-permute-start(bf16[2,4,2176]{2,1,0:T(4,128)(2,1)S(1)} %prep.1.refs_0_), channel_id=1, source_target_pairs={{0,24},{1,25},{2,26},{3,27},{4,28},{5,29},{6,30},{7,31},{8,16},{9,... | collective-permute-start | bytes 104456 | tf_op jit(solution)/shard_map/ppermute | solution.py:66
  6.6 4.1 %collective-permute-start = (bf16[2,4,2176]{2,1,0:T(4,128)(2,1)S(1)}, bf16[2,4,2176]{2,1,0:T(4,128)(2,1)S(1)}, u32[]{:S(2)}, u32[]{:S(2)}) collective-permute-start(bf16[2,4,2176]{2,1,0:T(4,128)(2,1)S(1)} %prep.1.refs_0_), channel_id=1, source_target_pairs={{0,8},{1,9},{2,10},{3,11},{4,12},{5,13},{6,14},{7,15},{8,0},{9,1},... | collective-permute-start | bytes 104456 | tf_op jit(solution)/shard_map/ppermute | solution.py:66
  10.8 7.6 %collective-permute-start.5 = (bf16[32,2176]{1,0:T(8,128)(2,1)S(1)}, bf16[32,2176]{1,0:T(8,128)(2,1)S(1)}, u32[]{:S(2)}, u32[]{:S(2)}) collective-permute-start(bf16[32,2176]{1,0:T(8,128)(2,1)S(1)} %join.1.block_in.refs_0_), channel_id=1, source_target_pairs={{0,5},{1,4},{2,7},{3,6},{4,1},{5,0},{6,3},{7,2},{8,13},{9,12},{10,... | collective-permute-start | bytes 417800 | tf_op jit(solution)/shard_map/ppermute | solution.py:51
  13.3 5.8 %collective-permute-start.4 = (bf16[32,2176]{1,0:T(8,128)(2,1)S(1)}, bf16[32,2176]{1,0:T(8,128)(2,1)S(1)}, u32[]{:S(2)}, u32[]{:S(2)}) collective-permute-start(bf16[32,2176]{1,0:T(8,128)(2,1)S(1)} %join.1.block_in.refs_0_), channel_id=1, source_target_pairs={{0,4},{1,5},{2,6},{3,7},{4,0},{5,1},{6,2},{7,3},{8,12},{9,13},{10,... | collective-permute-start | bytes 417800 | tf_op jit(solution)/shard_map/ppermute | solution.py:51
  13.8 5.3 %collective-permute-start.3 = (bf16[32,2176]{1,0:T(8,128)(2,1)S(1)}, bf16[32,2176]{1,0:T(8,128)(2,1)S(1)}, u32[]{:S(2)}, u32[]{:S(2)}) collective-permute-start(bf16[32,2176]{1,0:T(8,128)(2,1)S(1)} %join.1.block_in.refs_0_), channel_id=1, source_target_pairs={{0,1},{1,0},{2,3},{3,2},{4,5},{5,4},{6,7},{7,6},{8,9},{9,8},{10,11... | collective-permute-start | bytes 417800 | tf_op jit(solution)/shard_map/ppermute | solution.py:51
  16.9 2.8 %collective-permute-start.6 = (bf16[32,2176]{1,0:T(8,128)(2,1)S(1)}, bf16[32,2176]{1,0:T(8,128)(2,1)S(1)}, u32[]{:S(2)}, u32[]{:S(2)}) collective-permute-start(bf16[32,2176]{1,0:T(8,128)(2,1)S(1)} %get-tuple-element.23), channel_id=1, source_target_pairs={{0,2},{1,3},{2,0},{3,1},{4,6},{5,7},{6,4},{7,5},{8,10},{9,11},{10,... | collective-permute-start | bytes 417800 | tf_op jit(solution)/shard_map/ppermute | solution.py:51
  18.4 1.4 %collective-permute-start.9 = (bf16[32,2176]{1,0:T(8,128)(2,1)S(1)}, bf16[32,2176]{1,0:T(8,128)(2,1)S(1)}, u32[]{:S(2)}, u32[]{:S(2)}) collective-permute-start(bf16[32,2176]{1,0:T(8,128)(2,1)S(1)} %collective-permute-done.5.refs_3_), channel_id=1, source_target_pairs={{0,2},{1,3},{2,0},{3,1},{4,6},{5,7},{6,4},{7,5},{8,10},{9,11},{10,... | collective-permute-start | bytes 417800 | tf_op jit(solution)/shard_map/ppermute | solution.py:51
  19.1 1.4 %collective-permute-start.8 = (bf16[32,2176]{1,0:T(8,128)(2,1)S(1)}, bf16[32,2176]{1,0:T(8,128)(2,1)S(1)}, u32[]{:S(2)}, u32[]{:S(2)}) collective-permute-start(bf16[32,2176]{1,0:T(8,128)(2,1)S(1)} %collective-permute-done.4.refs_2_), channel_id=1, source_target_pairs={{0,2},{1,3},{2,0},{3,1},{4,6},{5,7},{6,4},{7,5},{8,10},{9,11},{10,... | collective-permute-start | bytes 417800 | tf_op jit(solution)/shard_map/ppermute | solution.py:51
  19.1 1.6 %collective-permute-start.7 = (bf16[32,2176]{1,0:T(8,128)(2,1)S(1)}, bf16[32,2176]{1,0:T(8,128)(2,1)S(1)}, u32[]{:S(2)}, u32[]{:S(2)}) collective-permute-start(bf16[32,2176]{1,0:T(8,128)(2,1)S(1)} %collective-permute-done.3.refs_1_), channel_id=1, source_target_pairs={{0,2},{1,3},{2,0},{3,1},{4,6},{5,7},{6,4},{7,5},{8,10},{9,11},{10,... | collective-permute-start | bytes 417800 | tf_op jit(solution)/shard_map/ppermute | solution.py:51
  22.8 1.6 %collective-permute-start.10 = (bf16[64,2176]{1,0:T(8,128)(2,1)S(1)}, bf16[64,2176]{1,0:T(8,128)(2,1)S(1)}, u32[]{:S(2)}, u32[]{:S(2)}) collective-permute-start(bf16[64,2176]{1,0:T(8,128)(2,1)S(1)} %get-tuple-element.28), channel_id=1, source_target_pairs={{0,2},{1,3},{2,0},{3,1},{4,6},{5,7},{6,4},{7,5},{8,10},{9,11},{10,... | collective-permute-start | bytes 835592 | tf_op jit(solution)/shard_map/ppermute | solution.py:51
  24.5 4.5 %collective-permute-start.11 = (bf16[16,2176]{1,0:T(8,128)(2,1)S(1)}, bf16[16,2176]{1,0:T(8,128)(2,1)S(1)}, u32[]{:S(2)}, u32[]{:S(2)}) collective-permute-start(bf16[16,2176]{1,0:T(8,128)(2,1)S(1)} %get-tuple-element.34), channel_id=1, source_target_pairs={{0,1},{1,0},{2,3},{3,2},{4,5},{5,4},{6,7},{7,6},{8,9},{9,8},{10,11... | collective-permute-start | bytes 208904 | tf_op jit(solution)/shard_map/ppermute | solution.py:51
  25.8 5.1 %collective-permute-start.12 = (bf16[16,2176]{1,0:T(8,128)(2,1)S(1)}, bf16[16,2176]{1,0:T(8,128)(2,1)S(1)}, u32[]{:S(2)}, u32[]{:S(2)}) collective-permute-start(bf16[16,2176]{1,0:T(8,128)(2,1)S(1)} %get-tuple-element.35), channel_id=1, source_target_pairs={{0,4},{1,5},{2,6},{3,7},{4,0},{5,1},{6,2},{7,3},{8,12},{9,13},{10,... | collective-permute-start | bytes 208904 | tf_op jit(solution)/shard_map/ppermute | solution.py:51
  26.5 5.2 %collective-permute-start.13 = (bf16[16,2176]{1,0:T(8,128)(2,1)S(1)}, bf16[16,2176]{1,0:T(8,128)(2,1)S(1)}, u32[]{:S(2)}, u32[]{:S(2)}) collective-permute-start(bf16[16,2176]{1,0:T(8,128)(2,1)S(1)} %get-tuple-element.36), channel_id=1, source_target_pairs={{0,5},{1,4},{2,7},{3,6},{4,1},{5,0},{6,3},{7,2},{8,13},{9,12},{10,... | collective-permute-start | bytes 208904 | tf_op jit(solution)/shard_map/ppermute | solution.py:51
  31.8 5.6 %collective-permute-start.14 = (bf16[4,2560]{1,0:T(4,128)(2,1)S(1)}, bf16[4,2560]{1,0:T(4,128)(2,1)S(1)}, u32[]{:S(2)}, u32[]{:S(2)}) collective-permute-start(bf16[4,2560]{1,0:T(4,128)(2,1)S(1)} %get-tuple-element.39), channel_id=1, source_target_pairs={{0,8},{1,9},{2,10},{3,11},{4,12},{5,13},{6,14},{7,15},{8,16},{9,17... | collective-permute-start | bytes 61448 | tf_op jit(solution)/shard_map/ppermute | solution.py:66
  33.1 4.7 %collective-permute-start.15 = (bf16[4,2560]{1,0:T(4,128)(2,1)S(1)}, bf16[4,2560]{1,0:T(4,128)(2,1)S(1)}, u32[]{:S(2)}, u32[]{:S(2)}) collective-permute-start(bf16[4,2560]{1,0:T(4,128)(2,1)S(1)} %get-tuple-element.40), channel_id=1, source_target_pairs={{0,16},{1,17},{2,18},{3,19},{4,20},{5,21},{6,22},{7,23},{8,24},{9,... | collective-permute-start | bytes 61448 | tf_op jit(solution)/shard_map/ppermute | solution.py:66
  35.8 3.8 %copy-start = (bf16[2048,16]{0,1:T(8,128)(2,1)S(1)}, bf16[2048,16]{0,1:T(8,128)(2,1)}, u32[]{:S(2)}) copy-start(bf16[2048,16]{0,1:T(8,128)(2,1)} %param.12) | copy-start | bytes 196612
  35.8 3.8 %collective-permute-start.16 = (bf16[4,2560]{1,0:T(4,128)(2,1)S(1)}, bf16[4,2560]{1,0:T(4,128)(2,1)S(1)}, u32[]{:S(2)}, u32[]{:S(2)}) collective-permute-start(bf16[4,2560]{1,0:T(4,128)(2,1)S(1)} %get-tuple-element.41), channel_id=1, source_target_pairs={{0,24},{1,25},{2,26},{3,27},{4,28},{5,29},{6,30},{7,31},{8,0},{9,1... | collective-permute-start | bytes 61448 | tf_op jit(solution)/shard_map/ppermute | solution.py:66

commit v3 on v2

--- a/solution.py
+++ b/solution.py
@@ -52,7 +52,7 @@
 
 
 GATHER_STEPS = ((2, 3, 1, 0), (3, 2, 0, 1), (1, 0, 3, 2))
-REDUCE_STEPS = ((1, 2, 3, 0), (2, 3, 0, 1), (3, 0, 1, 2))
+REDUCE_STEPS = ((1, 3, 0, 2), (3, 2, 1, 0), (2, 0, 3, 1))
 
 
 def by_member(member, values):

time: 40.9 us -> 40.4 us (0.988)
  waiting for transfers between devices: 14.4 us -> 13.2 us
  starting transfers between devices: 18.4 us -> 19.2 us
    ppermute x6, waiting for transfers between devices: 6.3 us -> 5.07 us  [shift(): lax.ppermute(block, AXES, [(i, i ^ (i >> low & 3 ^ step[i >> low & 3]) <<...]
    ppermute x6, starting transfers between devices: 10.4 us -> 11.1 us  [shift(): lax.ppermute(block, AXES, [(i, i ^ (i >> low & 3 ^ step[i >> low & 3]) <<...]
  transfers between devices with their start and end apart: 17 -> 17, of which waited for: 15 -> 14; matrix products, arithmetic and copies ran while one was open for 0% -> 0% of each run, Pallas kernels for 7% -> 7%
where the time goes in v3:
time: 40.4 us; the launch traced here: 40.2 us
  starting transfers between devices  19.2 us (48%)
  waiting for transfers between devices  13.2 us (33%)
  Pallas kernels  7.1 us (18%)
  between operations  0.7 us (2%)
    ppermute x6, starting transfers between devices, shift(): lax.ppermute(block, AXES, [(i, i ^ (i >> low & 3 ^ step[i >> low & 3]) <<...  11.1 us
    ppermute x11, waiting for transfers between devices, swap(): lax.ppermute(block, AXES, [(i, i ^ mask[i >> core & 1]) for i in range(co...  8.11 us
    ppermute x11, starting transfers between devices, swap(): lax.ppermute(block, AXES, [(i, i ^ mask[i >> core & 1]) for i in range(co...  8.08 us
    ppermute x6, waiting for transfers between devices, shift(): lax.ppermute(block, AXES, [(i, i ^ (i >> low & 3 ^ step[i >> low & 3]) <<...  5.07 us
    pallas_call x1, Pallas kernels, on_device(): pl.pallas_call(functools.partial(load_kernel, chunks), out_shape=(pltpu.V...  2.48 us
    pallas_call x1, Pallas kernels, on_device(): pl.pallas_call(functools.partial(units_kernel, basis, group_rows, tok, ex...  2.11 us
    pallas_call x1, Pallas kernels, on_device(): pl.pallas_call(functools.partial(final_kernel, len(arrived), back_basis,...  1.1 us
    pallas_call x1, Pallas kernels, on_device(): pl.pallas_call(prep_kernel, out_shape=jax.ShapeDtypeStruct((2, tok, width...  0.82 us
  transfers between devices with their start and end apart: 17, of which 14 were waited for; matrix products, arithmetic and copies ran while one was open for 0% of the time, Pallas kernels for 7%

profile of v3, /device:TPU:0, one launch (start us, length us, event | category | flops | bytes accessed | tf_op | source)
XLA Modules:
  0.0 40.2 jit_solution(5109315375308148499)
XLA Ops:
  0.6 0.8 %prep.1.refs_0_ = bf16[2,4,2176]{2,1,0:T(4,128)(2,1)S(1)} custom-call(bf16[4,2048]{1,0:T(4,128)(2,1)} %tokens_in.1, bf16[4,2048]{1,0:T(4,128)(2,1)} %grad_in.1, f32[4,16]{1,0:T(4,128)} %logits_in.1, s32[4,8]{1,0:T(4,128)} %chosen_in.1), custom_call_target="tpu_custom_call" | custom-call | tf_op jit(solution)/shard_map/prep/pallas_call | solution.py:431
  1.5 4.1 %collective-permute-start.2 = (bf16[2,4,2176]{2,1,0:T(4,128)(2,1)S(1)}, bf16[2,4,2176]{2,1,0:T(4,128)(2,1)S(1)}, u32[]{:S(2)}, u32[]{:S(2)}) collective-permute-start(bf16[2,4,2176]{2,1,0:T(4,128)(2,1)S(1)} %prep.1.refs_0_), channel_id=1, source_target_pairs={{0,16},{1,17},{2,18},{3,19},{4,20},{5,21},{6,22},{7,23},{8,24},{9,... | collective-permute-start | bytes 104456 | tf_op jit(solution)/shard_map/ppermute | solution.py:66
  5.5 1.1 %collective-permute-start.1 = (bf16[2,4,2176]{2,1,0:T(4,128)(2,1)S(1)}, bf16[2,4,2176]{2,1,0:T(4,128)(2,1)S(1)}, u32[]{:S(2)}, u32[]{:S(2)}) collective-permute-start(bf16[2,4,2176]{2,1,0:T(4,128)(2,1)S(1)} %prep.1.refs_0_), channel_id=1, source_target_pairs={{0,24},{1,25},{2,26},{3,27},{4,28},{5,29},{6,30},{7,31},{8,16},{9,... | collective-permute-start | bytes 104456 | tf_op jit(solution)/shard_map/ppermute | solution.py:66
  6.6 0.5 %collective-permute-start = (bf16[2,4,2176]{2,1,0:T(4,128)(2,1)S(1)}, bf16[2,4,2176]{2,1,0:T(4,128)(2,1)S(1)}, u32[]{:S(2)}, u32[]{:S(2)}) collective-permute-start(bf16[2,4,2176]{2,1,0:T(4,128)(2,1)S(1)} %prep.1.refs_0_), channel_id=1, source_target_pairs={{0,8},{1,9},{2,10},{3,11},{4,12},{5,13},{6,14},{7,15},{8,0},{9,1},... | collective-permute-start | bytes 104456 | tf_op jit(solution)/shard_map/ppermute | solution.py:66
  7.1 1.3 %collective-permute-done.2.refs_3_ = bf16[2,4,2176]{2,1,0:T(4,128)(2,1)S(1)} collective-permute-done((bf16[2,4,2176]{2,1,0:T(4,128)(2,1)S(1)}, bf16[2,4,2176]{2,1,0:T(4,128)(2,1)S(1)}, u32[]{:S(2)}, u32[]{:S(2)}) %collective-permute-start.2) | collective-permute-done | bytes 34848 | tf_op jit(solution)/shard_map/ppermute | solution.py:66
  8.5 1.9 %collective-permute-done.1.refs_2_ = bf16[2,4,2176]{2,1,0:T(4,128)(2,1)S(1)} collective-permute-done((bf16[2,4,2176]{2,1,0:T(4,128)(2,1)S(1)}, bf16[2,4,2176]{2,1,0:T(4,128)(2,1)S(1)}, u32[]{:S(2)}, u32[]{:S(2)}) %collective-permute-start.1) | collective-permute-done | bytes 34848 | tf_op jit(solution)/shard_map/ppermute | solution.py:66
  10.4 0.4 collective-permute-done.refs_1_
  10.8 2.5 %collective-permute-start.5 = (bf16[32,2176]{1,0:T(8,128)(2,1)S(1)}, bf16[32,2176]{1,0:T(8,128)(2,1)S(1)}, u32[]{:S(2)}, u32[]{:S(2)}) collective-permute-start(bf16[32,2176]{1,0:T(8,128)(2,1)S(1)} %join.1.block_in.refs_0_), channel_id=1, source_target_pairs={{0,5},{1,4},{2,7},{3,6},{4,1},{5,0},{6,3},{7,2},{8,13},{9,12},{10,... | collective-permute-start | bytes 417800 | tf_op jit(solution)/shard_map/ppermute | solution.py:51
  13.3 0.5 %collective-permute-start.4 = (bf16[32,2176]{1,0:T(8,128)(2,1)S(1)}, bf16[32,2176]{1,0:T(8,128)(2,1)S(1)}, u32[]{:S(2)}, u32[]{:S(2)}) collective-permute-start(bf16[32,2176]{1,0:T(8,128)(2,1)S(1)} %join.1.block_in.refs_0_), channel_id=1, source_target_pairs={{0,4},{1,5},{2,6},{3,7},{4,0},{5,1},{6,2},{7,3},{8,12},{9,13},{10,... | collective-permute-start | bytes 417800 | tf_op jit(solution)/shard_map/ppermute | solution.py:51
  13.8 0.5 %collective-permute-start.3 = (bf16[32,2176]{1,0:T(8,128)(2,1)S(1)}, bf16[32,2176]{1,0:T(8,128)(2,1)S(1)}, u32[]{:S(2)}, u32[]{:S(2)}) collective-permute-start(bf16[32,2176]{1,0:T(8,128)(2,1)S(1)} %join.1.block_in.refs_0_), channel_id=1, source_target_pairs={{0,1},{1,0},{2,3},{3,2},{4,5},{5,4},{6,7},{7,6},{8,9},{9,8},{10,11... | collective-permute-start | bytes 417800 | tf_op jit(solution)/shard_map/ppermute | solution.py:51
  14.4 2.5 %load.1 = (bf16[32,2176]{1,0:T(8,128)(2,1)S(1)}, bf16[2048,768]{1,0:T(8,128)(2,1)S(1)}, bf16[384,2048]{1,0:T(8,128)(2,1)S(1)}) custom-call(bf16[32,2176]{1,0:T(8,128)(2,1)S(1)} %join.1.block_in.refs_0_, bf16[1,2048,384]{2,1,0:T(8,128)(2,1)} %gate_in.1, bf16[1,2048,384]{2,1,0:T(8,128)(2,1)} %up_in.1, bf16[1,384,2048]{2,1,0:T(8,128)(2,1)} %down_in.1), custom_call_target="tpu_custom_call" | custom-call | bytes 9437184 | tf_op jit(solution)/shard_map/load/pallas_call | solution.py:472
  16.9 1.5 %collective-permute-done.5.refs_3_ = bf16[32,2176]{1,0:T(8,128)(2,1)S(1)} collective-permute-done((bf16[32,2176]{1,0:T(8,128)(2,1)S(1)}, bf16[32,2176]{1,0:T(8,128)(2,1)S(1)}, u32[]{:S(2)}, u32[]{:S(2)}) %collective-permute-start.5) | collective-permute-done | bytes 139296 | tf_op jit(solution)/shard_map/ppermute | solution.py:51
  18.4 0.7 %collective-permute-done.4.refs_2_ = bf16[32,2176]{1,0:T(8,128)(2,1)S(1)} collective-permute-done((bf16[32,2176]{1,0:T(8,128)(2,1)S(1)}, bf16[32,2176]{1,0:T(8,128)(2,1)S(1)}, u32[]{:S(2)}, u32[]{:S(2)}) %collective-permute-start.4) | collective-permute-done | bytes 139296 | tf_op jit(solution)/shard_map/ppermute | solution.py:51
  19.1 0.5 %collective-permute-start.7 = (bf16[32,2176]{1,0:T(8,128)(2,1)S(1)}, bf16[32,2176]{1,0:T(8,128)(2,1)S(1)}, u32[]{:S(2)}, u32[]{:S(2)}) collective-permute-start(bf16[32,2176]{1,0:T(8,128)(2,1)S(1)} %collective-permute-done.3.refs_1_), channel_id=1, source_target_pairs={{0,2},{1,3},{2,0},{3,1},{4,6},{5,7},{6,4},{7,5},{8,10},{9,11},{10,... | collective-permute-start | bytes 417800 | tf_op jit(solution)/shard_map/ppermute | solution.py:51
  19.8 0.7 %collective-permute-done.8.refs_6_ = bf16[32,2176]{1,0:T(8,128)(2,1)S(1)} collective-permute-done((bf16[32,2176]{1,0:T(8,128)(2,1)S(1)}, bf16[32,2176]{1,0:T(8,128)(2,1)S(1)}, u32[]{:S(2)}, u32[]{:S(2)}) %collective-permute-start.8) | collective-permute-done | bytes 139296 | tf_op jit(solution)/shard_map/ppermute | solution.py:51
  20.5 0.2 collective-permute-done.7.refs_5_
  20.7 2.1 %units.1 = (f32[64,2048]{1,0:T(8,128)S(1)}, bf16[64,2176]{1,0:T(8,128)(2,1)S(1)}, f32[2,128]{1,0:T(2,128)S(1)}) custom-call(bf16[32,2176]{1,0:T(8,128)(2,1)S(1)} %join.1.block_in.refs_0_, bf16[32,2176]{1,0:T(8,128)(2,1)S(1)} %collective-permute-done.3.refs_1_, bf16[32,2176]{1,0:T(8,128)(2,1)S(1)} %collective-permute-done.4.refs_2_, ...), custom_call_target="tpu_custom_call" | custom-call | flops 1006632960 | bytes 5767168 | tf_op jit(solution)/shard_map/units/pallas_call | solution.py:494
  22.8 0.4 collective-permute-start.10
  23.2 1.2 %collective-permute-done.10.refs_2_ = bf16[64,2176]{1,0:T(8,128)(2,1)S(1)} collective-permute-done((bf16[64,2176]{1,0:T(8,128)(2,1)S(1)}, bf16[64,2176]{1,0:T(8,128)(2,1)S(1)}, u32[]{:S(2)}, u32[]{:S(2)}) %collective-permute-start.10) | collective-permute-done | bytes 278560 | tf_op jit(solution)/shard_map/ppermute | solution.py:51
  24.5 1.3 %collective-permute-start.11 = (bf16[16,2176]{1,0:T(8,128)(2,1)S(1)}, bf16[16,2176]{1,0:T(8,128)(2,1)S(1)}, u32[]{:S(2)}, u32[]{:S(2)}) collective-permute-start(bf16[16,2176]{1,0:T(8,128)(2,1)S(1)} %get-tuple-element.34), channel_id=1, source_target_pairs={{0,1},{1,0},{2,3},{3,2},{4,5},{5,4},{6,7},{7,6},{8,9},{9,8},{10,11... | collective-permute-start | bytes 208904 | tf_op jit(solution)/shard_map/ppermute | solution.py:51
  25.8 0.7 %collective-permute-start.12 = (bf16[16,2176]{1,0:T(8,128)(2,1)S(1)}, bf16[16,2176]{1,0:T(8,128)(2,1)S(1)}, u32[]{:S(2)}, u32[]{:S(2)}) collective-permute-start(bf16[16,2176]{1,0:T(8,128)(2,1)S(1)} %get-tuple-element.35), channel_id=1, source_target_pairs={{0,4},{1,5},{2,6},{3,7},{4,0},{5,1},{6,2},{7,3},{8,12},{9,13},{10,... | collective-permute-start | bytes 208904 | tf_op jit(solution)/shard_map/ppermute | solution.py:51
  26.5 1.5 %collective-permute-start.13 = (bf16[16,2176]{1,0:T(8,128)(2,1)S(1)}, bf16[16,2176]{1,0:T(8,128)(2,1)S(1)}, u32[]{:S(2)}, u32[]{:S(2)}) collective-permute-start(bf16[16,2176]{1,0:T(8,128)(2,1)S(1)} %get-tuple-element.36), channel_id=1, source_target_pairs={{0,5},{1,4},{2,7},{3,6},{4,1},{5,0},{6,3},{7,2},{8,13},{9,12},{10,... | collective-permute-start | bytes 208904 | tf_op jit(solution)/shard_map/ppermute | solution.py:51
  28.0 0.9 %collective-permute-done.11.refs_2_ = bf16[16,2176]{1,0:T(8,128)(2,1)S(1)} collective-permute-done((bf16[16,2176]{1,0:T(8,128)(2,1)S(1)}, bf16[16,2176]{1,0:T(8,128)(2,1)S(1)}, u32[]{:S(2)}, u32[]{:S(2)}) %collective-permute-start.11) | collective-permute-done | bytes 69664 | tf_op jit(solution)/shard_map/ppermute | solution.py:51
  29.0 1.9 %collective-permute-done.12.refs_3_ = bf16[16,2176]{1,0:T(8,128)(2,1)S(1)} collective-permute-done((bf16[16,2176]{1,0:T(8,128)(2,1)S(1)}, bf16[16,2176]{1,0:T(8,128)(2,1)S(1)}, u32[]{:S(2)}, u32[]{:S(2)}) %collective-permute-start.12) | collective-permute-done | bytes 69664 | tf_op jit(solution)/shard_map/ppermute | solution.py:51
  30.9 0.9 %collective-permute-done.13.refs_4_ = bf16[16,2176]{1,0:T(8,128)(2,1)S(1)} collective-permute-done((bf16[16,2176]{1,0:T(8,128)(2,1)S(1)}, bf16[16,2176]{1,0:T(8,128)(2,1)S(1)}, u32[]{:S(2)}, u32[]{:S(2)}) %collective-permute-start.13) | collective-permute-done | bytes 69664 | tf_op jit(solution)/shard_map/ppermute | solution.py:51
  31.8 1.3 %collective-permute-start.14 = (bf16[4,2560]{1,0:T(4,128)(2,1)S(1)}, bf16[4,2560]{1,0:T(4,128)(2,1)S(1)}, u32[]{:S(2)}, u32[]{:S(2)}) collective-permute-start(bf16[4,2560]{1,0:T(4,128)(2,1)S(1)} %get-tuple-element.39), channel_id=1, source_target_pairs={{0,8},{1,9},{2,10},{3,11},{4,12},{5,13},{6,14},{7,15},{8,24},{9,25... | collective-permute-start | bytes 61448 | tf_op jit(solution)/shard_map/ppermute | solution.py:66
  33.0 2.2 %collective-permute-start.15 = (bf16[4,2560]{1,0:T(4,128)(2,1)S(1)}, bf16[4,2560]{1,0:T(4,128)(2,1)S(1)}, u32[]{:S(2)}, u32[]{:S(2)}) collective-permute-start(bf16[4,2560]{1,0:T(4,128)(2,1)S(1)} %get-tuple-element.40), channel_id=1, source_target_pairs={{0,24},{1,25},{2,26},{3,27},{4,28},{5,29},{6,30},{7,31},{8,16},{9,... | collective-permute-start | bytes 61448 | tf_op jit(solution)/shard_map/ppermute | solution.py:66
  35.3 1.9 %collective-permute-start.16 = (bf16[4,2560]{1,0:T(4,128)(2,1)S(1)}, bf16[4,2560]{1,0:T(4,128)(2,1)S(1)}, u32[]{:S(2)}, u32[]{:S(2)}) collective-permute-start(bf16[4,2560]{1,0:T(4,128)(2,1)S(1)} %get-tuple-element.41), channel_id=1, source_target_pairs={{0,16},{1,17},{2,18},{3,19},{4,20},{5,21},{6,22},{7,23},{8,0},{9,1... | collective-permute-start | bytes 61448 | tf_op jit(solution)/shard_map/ppermute | solution.py:66
  37.2 0.4 tables.1
  37.6 1.0 %collective-permute-done.15.refs_7_ = bf16[4,2560]{1,0:T(4,128)(2,1)S(1)} collective-permute-done((bf16[4,2560]{1,0:T(4,128)(2,1)S(1)}, bf16[4,2560]{1,0:T(4,128)(2,1)S(1)}, u32[]{:S(2)}, u32[]{:S(2)}) %collective-permute-start.15) | collective-permute-done | bytes 20512 | tf_op jit(solution)/shard_map/ppermute | solution.py:66
  38.6 0.4 %collective-permute-done.16.refs_8_ = bf16[4,2560]{1,0:T(4,128)(2,1)S(1)} collective-permute-done((bf16[4,2560]{1,0:T(4,128)(2,1)S(1)}, bf16[4,2560]{1,0:T(4,128)(2,1)S(1)}, u32[]{:S(2)}, u32[]{:S(2)}) %collective-permute-start.16) | collective-permute-done | bytes 20512 | tf_op jit(solution)/shard_map/ppermute | solution.py:66
  39.0 1.1 %final.1 = (bf16[4,2048]{1,0:T(4,128)(2,1)}, f32[16,64]{1,0:T(8,128)}) custom-call(f32[16,128]{1,0:T(8,128)S(1)} %get-tuple-element.30.refs_0_, bf16[128,128]{1,0:T(8,128)(2,1)S(1)} %get-tuple-element.31.refs_1_, bf16[16,128]{1,0:T(8,128)(2,1)S(1)} %get-tuple-element.32.refs_2_, bf16[16,2048]{1,0:T(8,128)(2,1)S(1)} %bitcast.2, ...), custom_call_target="tpu_custom_call" | custom-call | tf_op jit(solution)/shard_map/final/pallas_call | solution.py:568
  (12 shorter events, 0.4 us)
Async XLA Ops:
  1.5 7.0 %collective-permute-start.2 = (bf16[2,4,2176]{2,1,0:T(4,128)(2,1)S(1)}, bf16[2,4,2176]{2,1,0:T(4,128)(2,1)S(1)}, u32[]{:S(2)}, u32[]{:S(2)}) collective-permute-start(bf16[2,4,2176]{2,1,0:T(4,128)(2,1)S(1)} %prep.1.refs_0_), channel_id=1, source_target_pairs={{0,16},{1,17},{2,18},{3,19},{4,20},{5,21},{6,22},{7,23},{8,24},{9,... | collective-permute-start | bytes 104456 | tf_op jit(solution)/shard_map/ppermute | solution.py:66
  5.5 4.9 %collective-permute-start.1 = (bf16[2,4,2176]{2,1,0:T(4,128)(2,1)S(1)}, bf16[2,4,2176]{2,1,0:T(4,128)(2,1)S(1)}, u32[]{:S(2)}, u32[]{:S(2)}) collective-permute-start(bf16[2,4,2176]{2,1,0:T(4,128)(2,1)S(1)} %prep.1.refs_0_), channel_id=1, source_target_pairs={{0,24},{1,25},{2,26},{3,27},{4,28},{5,29},{6,30},{7,31},{8,16},{9,... | collective-permute-start | bytes 104456 | tf_op jit(solution)/shard_map/ppermute | solution.py:66
  6.6 4.1 %collective-permute-start = (bf16[2,4,2176]{2,1,0:T(4,128)(2,1)S(1)}, bf16[2,4,2176]{2,1,0:T(4,128)(2,1)S(1)}, u32[]{:S(2)}, u32[]{:S(2)}) collective-permute-start(bf16[2,4,2176]{2,1,0:T(4,128)(2,1)S(1)} %prep.1.refs_0_), channel_id=1, source_target_pairs={{0,8},{1,9},{2,10},{3,11},{4,12},{5,13},{6,14},{7,15},{8,0},{9,1},... | collective-permute-start | bytes 104456 | tf_op jit(solution)/shard_map/ppermute | solution.py:66
  10.8 7.6 %collective-permute-start.5 = (bf16[32,2176]{1,0:T(8,128)(2,1)S(1)}, bf16[32,2176]{1,0:T(8,128)(2,1)S(1)}, u32[]{:S(2)}, u32[]{:S(2)}) collective-permute-start(bf16[32,2176]{1,0:T(8,128)(2,1)S(1)} %join.1.block_in.refs_0_), channel_id=1, source_target_pairs={{0,5},{1,4},{2,7},{3,6},{4,1},{5,0},{6,3},{7,2},{8,13},{9,12},{10,... | collective-permute-start | bytes 417800 | tf_op jit(solution)/shard_map/ppermute | solution.py:51
  13.3 5.8 %collective-permute-start.4 = (bf16[32,2176]{1,0:T(8,128)(2,1)S(1)}, bf16[32,2176]{1,0:T(8,128)(2,1)S(1)}, u32[]{:S(2)}, u32[]{:S(2)}) collective-permute-start(bf16[32,2176]{1,0:T(8,128)(2,1)S(1)} %join.1.block_in.refs_0_), channel_id=1, source_target_pairs={{0,4},{1,5},{2,6},{3,7},{4,0},{5,1},{6,2},{7,3},{8,12},{9,13},{10,... | collective-permute-start | bytes 417800 | tf_op jit(solution)/shard_map/ppermute | solution.py:51
  13.8 5.3 %collective-permute-start.3 = (bf16[32,2176]{1,0:T(8,128)(2,1)S(1)}, bf16[32,2176]{1,0:T(8,128)(2,1)S(1)}, u32[]{:S(2)}, u32[]{:S(2)}) collective-permute-start(bf16[32,2176]{1,0:T(8,128)(2,1)S(1)} %join.1.block_in.refs_0_), channel_id=1, source_target_pairs={{0,1},{1,0},{2,3},{3,2},{4,5},{5,4},{6,7},{7,6},{8,9},{9,8},{10,11... | collective-permute-start | bytes 417800 | tf_op jit(solution)/shard_map/ppermute | solution.py:51
  16.9 2.8 %collective-permute-start.6 = (bf16[32,2176]{1,0:T(8,128)(2,1)S(1)}, bf16[32,2176]{1,0:T(8,128)(2,1)S(1)}, u32[]{:S(2)}, u32[]{:S(2)}) collective-permute-start(bf16[32,2176]{1,0:T(8,128)(2,1)S(1)} %get-tuple-element.23), channel_id=1, source_target_pairs={{0,2},{1,3},{2,0},{3,1},{4,6},{5,7},{6,4},{7,5},{8,10},{9,11},{10,... | collective-permute-start | bytes 417800 | tf_op jit(solution)/shard_map/ppermute | solution.py:51
  18.4 1.4 %collective-permute-start.9 = (bf16[32,2176]{1,0:T(8,128)(2,1)S(1)}, bf16[32,2176]{1,0:T(8,128)(2,1)S(1)}, u32[]{:S(2)}, u32[]{:S(2)}) collective-permute-start(bf16[32,2176]{1,0:T(8,128)(2,1)S(1)} %collective-permute-done.5.refs_3_), channel_id=1, source_target_pairs={{0,2},{1,3},{2,0},{3,1},{4,6},{5,7},{6,4},{7,5},{8,10},{9,11},{10,... | collective-permute-start | bytes 417800 | tf_op jit(solution)/shard_map/ppermute | solution.py:51
  19.1 1.4 %collective-permute-start.8 = (bf16[32,2176]{1,0:T(8,128)(2,1)S(1)}, bf16[32,2176]{1,0:T(8,128)(2,1)S(1)}, u32[]{:S(2)}, u32[]{:S(2)}) collective-permute-start(bf16[32,2176]{1,0:T(8,128)(2,1)S(1)} %collective-permute-done.4.refs_2_), channel_id=1, source_target_pairs={{0,2},{1,3},{2,0},{3,1},{4,6},{5,7},{6,4},{7,5},{8,10},{9,11},{10,... | collective-permute-start | bytes 417800 | tf_op jit(solution)/shard_map/ppermute | solution.py:51
  19.1 1.6 %collective-permute-start.7 = (bf16[32,2176]{1,0:T(8,128)(2,1)S(1)}, bf16[32,2176]{1,0:T(8,128)(2,1)S(1)}, u32[]{:S(2)}, u32[]{:S(2)}) collective-permute-start(bf16[32,2176]{1,0:T(8,128)(2,1)S(1)} %collective-permute-done.3.refs_1_), channel_id=1, source_target_pairs={{0,2},{1,3},{2,0},{3,1},{4,6},{5,7},{6,4},{7,5},{8,10},{9,11},{10,... | collective-permute-start | bytes 417800 | tf_op jit(solution)/shard_map/ppermute | solution.py:51
  22.8 1.6 %collective-permute-start.10 = (bf16[64,2176]{1,0:T(8,128)(2,1)S(1)}, bf16[64,2176]{1,0:T(8,128)(2,1)S(1)}, u32[]{:S(2)}, u32[]{:S(2)}) collective-permute-start(bf16[64,2176]{1,0:T(8,128)(2,1)S(1)} %get-tuple-element.28), channel_id=1, source_target_pairs={{0,2},{1,3},{2,0},{3,1},{4,6},{5,7},{6,4},{7,5},{8,10},{9,11},{10,... | collective-permute-start | bytes 835592 | tf_op jit(solution)/shard_map/ppermute | solution.py:51
  24.5 4.5 %collective-permute-start.11 = (bf16[16,2176]{1,0:T(8,128)(2,1)S(1)}, bf16[16,2176]{1,0:T(8,128)(2,1)S(1)}, u32[]{:S(2)}, u32[]{:S(2)}) collective-permute-start(bf16[16,2176]{1,0:T(8,128)(2,1)S(1)} %get-tuple-element.34), channel_id=1, source_target_pairs={{0,1},{1,0},{2,3},{3,2},{4,5},{5,4},{6,7},{7,6},{8,9},{9,8},{10,11... | collective-permute-start | bytes 208904 | tf_op jit(solution)/shard_map/ppermute | solution.py:51
  25.8 5.1 %collective-permute-start.12 = (bf16[16,2176]{1,0:T(8,128)(2,1)S(1)}, bf16[16,2176]{1,0:T(8,128)(2,1)S(1)}, u32[]{:S(2)}, u32[]{:S(2)}) collective-permute-start(bf16[16,2176]{1,0:T(8,128)(2,1)S(1)} %get-tuple-element.35), channel_id=1, source_target_pairs={{0,4},{1,5},{2,6},{3,7},{4,0},{5,1},{6,2},{7,3},{8,12},{9,13},{10,... | collective-permute-start | bytes 208904 | tf_op jit(solution)/shard_map/ppermute | solution.py:51
  26.5 5.2 %collective-permute-start.13 = (bf16[16,2176]{1,0:T(8,128)(2,1)S(1)}, bf16[16,2176]{1,0:T(8,128)(2,1)S(1)}, u32[]{:S(2)}, u32[]{:S(2)}) collective-permute-start(bf16[16,2176]{1,0:T(8,128)(2,1)S(1)} %get-tuple-element.36), channel_id=1, source_target_pairs={{0,5},{1,4},{2,7},{3,6},{4,1},{5,0},{6,3},{7,2},{8,13},{9,12},{10,... | collective-permute-start | bytes 208904 | tf_op jit(solution)/shard_map/ppermute | solution.py:51
  31.8 5.8 %collective-permute-start.14 = (bf16[4,2560]{1,0:T(4,128)(2,1)S(1)}, bf16[4,2560]{1,0:T(4,128)(2,1)S(1)}, u32[]{:S(2)}, u32[]{:S(2)}) collective-permute-start(bf16[4,2560]{1,0:T(4,128)(2,1)S(1)} %get-tuple-element.39), channel_id=1, source_target_pairs={{0,8},{1,9},{2,10},{3,11},{4,12},{5,13},{6,14},{7,15},{8,24},{9,25... | collective-permute-start | bytes 61448 | tf_op jit(solution)/shard_map/ppermute | solution.py:66
  33.0 5.6 %collective-permute-start.15 = (bf16[4,2560]{1,0:T(4,128)(2,1)S(1)}, bf16[4,2560]{1,0:T(4,128)(2,1)S(1)}, u32[]{:S(2)}, u32[]{:S(2)}) collective-permute-start(bf16[4,2560]{1,0:T(4,128)(2,1)S(1)} %get-tuple-element.40), channel_id=1, source_target_pairs={{0,24},{1,25},{2,26},{3,27},{4,28},{5,29},{6,30},{7,31},{8,16},{9,... | collective-permute-start | bytes 61448 | tf_op jit(solution)/shard_map/ppermute | solution.py:66
  35.3 3.8 %copy-start = (bf16[2048,16]{0,1:T(8,128)(2,1)S(1)}, bf16[2048,16]{0,1:T(8,128)(2,1)}, u32[]{:S(2)}) copy-start(bf16[2048,16]{0,1:T(8,128)(2,1)} %param.12) | copy-start | bytes 196612
  35.3 3.8 %collective-permute-start.16 = (bf16[4,2560]{1,0:T(4,128)(2,1)S(1)}, bf16[4,2560]{1,0:T(4,128)(2,1)S(1)}, u32[]{:S(2)}, u32[]{:S(2)}) collective-permute-start(bf16[4,2560]{1,0:T(4,128)(2,1)S(1)} %get-tuple-element.41), channel_id=1, source_target_pairs={{0,16},{1,17},{2,18},{3,19},{4,20},{5,21},{6,22},{7,23},{8,0},{9,1... | collective-permute-start | bytes 61448 | tf_op jit(solution)/shard_map/ppermute | solution.py:66

commit v4 on v1

--- a/solution.py
+++ b/solution.py
@@ -243,8 +243,10 @@
             grad_gate = weighted * up_pre * sig * (1.0 + gate_pre * (1.0 - sig))
             grad_up = weighted * act_gate
             grads += [grad_gate.astype(BF16), grad_up.astype(BF16)]
-        grads = jnp.concatenate(grads, axis=1)
-        return lax.dot_general(grads, pair_ref[...], NT, preferred_element_type=F32), score
+        return jnp.concatenate(grads, axis=1), score
+
+    def back_product(grads):
+        return lax.dot_general(grads, pair_ref[...], NT, preferred_element_type=F32)
 
     def in_order(score, place, swap_mask):
         token = lax.broadcasted_iota(jnp.int32, (score.shape[0], tokens), 1)
@@ -252,13 +254,28 @@
         whole = (place_mask(place // tok, basis, side & core_mask != 0) ^ side) * tok + place % tok
         return jnp.sum(jnp.where(whole == token, score, 0.0), axis=0, keepdims=True)
 
+    def send_scores():
+        lane_blocks = tokens // LANES
+        padded_ref[...] = jnp.zeros(padded_ref.shape, F32)
+        value = score_ref[...]
+        for piece in range(SCORE_PIECES):
+            rounded = value.astype(BF16).astype(F32)
+            for b in range(lane_blocks):
+                at = piece * lane_blocks + b
+                padded_ref[at : at + 1, :] = rounded[:, b * LANES : (b + 1) * LANES]
+            value = value - rounded
+        pieces_ref[...] = padded_ref[0 : pieces_ref.shape[0], :]
+        put_scores(message_ref, padded_ref, width)
+
     half = blocks * rows // 2
     if 2 * half <= 128:
-        total, score = terms(own_refs + other_refs, 0, rows)
+        grads, score = terms(own_refs + other_refs, 0, rows)
+        row = lax.broadcasted_iota(jnp.int32, (2 * half, tokens), 0)
+        score_ref[...] = in_order(score, row % half, jnp.where(row < half, 0, core_mask))
+        send_scores()
+        total = back_product(grads)
         kept_ref[...] = total[:half]
         message_ref[:, 0:width] = total[half:].astype(BF16)
-        row = lax.broadcasted_iota(jnp.int32, (2 * half, tokens), 0)
-        score_ref[...] = in_order(score, row % half, jnp.where(row < half, 0, core_mask))
     else:
         step = min(rows, 128)
         score_ref[...] = jnp.zeros(score_ref.shape, F32)
@@ -266,7 +283,8 @@
             for j, ref in enumerate(sets):
 
                 def one(index):
-                    total, score = terms((ref,), index * step, step)
+                    grads, score = terms((ref,), index * step, step)
+                    total = back_product(grads)
                     first = pl.multiple_of(j * (rows // 2) + index * (step // 2), step // 2)
                     out_ref[pl.ds(first, step // 2), 0:width] = total.astype(out_ref.dtype)
                     place = lax.broadcasted_iota(jnp.int32, (step // 2, tokens), 0) + first
@@ -274,17 +292,7 @@
 
                 pl.loop(0, rows // step)(one)
 
-    lane_blocks = tokens // LANES
-    padded_ref[...] = jnp.zeros(padded_ref.shape, F32)
-    value = score_ref[...]
-    for piece in range(SCORE_PIECES):
-        rounded = value.astype(BF16).astype(F32)
-        for b in range(lane_blocks):
-            at = piece * lane_blocks + b
-            padded_ref[at : at + 1, :] = rounded[:, b * LANES : (b + 1) * LANES]
-        value = value - rounded
-    pieces_ref[...] = padded_ref[0 : pieces_ref.shape[0], :]
-    put_scores(message_ref, padded_ref, width)
+        send_scores()
 
 
 def add_kernel(arrivals, positions, low, *refs):
@@ -319,8 +327,8 @@
         put_scores(ref, scores_ref, width)
 
 
-def table_kernel(basis, group, tok, core_mask, rows_out, blocks, after_ref, *refs):
-    probs_ref, column_ref, mine_ref = refs[2 * blocks :]
+def table_kernel(basis, back_basis, low, group, tok, core_mask, rows_out, blocks, after_ref, *refs):
+    probs_ref, column_ref, mine_ref, pick_ref = refs[2 * blocks :]
     rows, buf_width = refs[0].shape
     half = blocks * rows // 2
     experts, tokens = probs_ref.shape
@@ -348,12 +356,23 @@
     row = lax.broadcasted_iota(jnp.int32, mine_ref.shape, 0)
     token = lax.broadcasted_iota(jnp.int32, mine_ref.shape, 1)
     mine_ref[...] = jnp.where((row < tok) & (token == own * tok + row), 1.0, 0.0).astype(BF16)
-
-
-def final_kernel(arrivals, back_basis, core_mask, low, *refs):
-    probs_ref, column_ref, mine_ref, router_ref, kept_ref, pieces_ref = refs[:6]
-    arrived = refs[6 : 6 + arrivals]
-    x_out, grad_out, x_ref, grad_ref, scores_ref, sems = refs[6 + arrivals :]
+    wide = pick_ref.shape[1]
+    sender = lax.broadcasted_iota(jnp.int32, (experts, wide), 1) // SCORE_PIECES
+    ids = lax.broadcasted_iota(jnp.int32, (experts, wide), 0)
+    mask = place_mask(sender, back_basis, own & core_mask != 0)
+    if low is not None:
+        member = own >> low & 3
+        source = sender >> len(back_basis)
+        for k, step in enumerate(REDUCE_STEPS):
+            come = by_member(member, [d ^ step.index(d) for d in range(4)]) << low
+            mask = mask ^ jnp.where(source == k + 1, come, 0)
+    pick_ref[...] = jnp.where(((mask ^ own) >> 1) == ids, 1.0, 0.0).astype(BF16)
+
+
+def final_kernel(arrivals, *refs):
+    probs_ref, column_ref, mine_ref, pick_ref, router_ref, kept_ref, pieces_ref = refs[:7]
+    arrived = refs[7 : 7 + arrivals]
+    x_out, grad_out, x_ref, grad_ref, scores_ref, sems = refs[7 + arrivals :]
     experts, width = router_ref.shape
     size = pieces_ref.shape[0]
     tok = kept_ref.shape[0]
@@ -363,20 +382,10 @@
         get_scores(ref, scores_ref, (j + 1) * size, size, width)
     blocks = probs_ref.shape[1] // LANES
     wide = scores_ref.shape[0] // blocks
-    sender = lax.broadcasted_iota(jnp.int32, (experts, wide), 1) // SCORE_PIECES
-    ids = lax.broadcasted_iota(jnp.int32, (experts, wide), 0)
-    mask = place_mask(sender, back_basis, own & core_mask != 0)
-    if low is not None:
-        member = own >> low & 3
-        source = sender >> len(back_basis)
-        for k, step in enumerate(REDUCE_STEPS):
-            come = by_member(member, [d ^ step.index(d) for d in range(4)]) << low
-            mask = mask ^ jnp.where(source == k + 1, come, 0)
-    pick = jnp.where(((mask ^ own) >> 1) == ids, 1.0, 0.0).astype(BF16)
     parts = []
     for b in range(blocks):
         block = scores_ref[...] if blocks == 1 else scores_ref[pl.ds(b, wide, stride=blocks), :]
-        parts.append(jnp.dot(pick, block.astype(BF16), preferred_element_type=F32))
+        parts.append(jnp.dot(pick_ref[...], block.astype(BF16), preferred_element_type=F32))
     scores = parts[0] if blocks == 1 else jnp.concatenate(parts, axis=1)
     probs = probs_ref[...]
     mean = jnp.sum(probs * scores, axis=0, keepdims=True)
@@ -537,14 +546,15 @@
         kept, pieces = outs[0], outs[1]
         if tables is None:
             tables = pl.pallas_call(
-                functools.partial(table_kernel, basis, group_rows, tok, core_mask, rows_out, block_count),
+                functools.partial(table_kernel, basis, back_basis, low, group_rows, tok, core_mask, rows_out, block_count),
                 out_shape=(
                     jax.ShapeDtypeStruct((experts, token_count), F32),
                     jax.ShapeDtypeStruct((token_count, LANES), BF16),
                     jax.ShapeDtypeStruct((16, token_count), BF16),
+                    jax.ShapeDtypeStruct((experts, SCORE_PIECES * count), BF16),
                 ),
                 in_specs=[pl.BlockSpec(memory_space=pl.ANY)] + [VMEM_SPEC] * len(blocks),
-                out_specs=(VMEM_SPEC,) * 3,
+                out_specs=(VMEM_SPEC,) * 4,
                 compiler_params=PARAMS,
                 cost_estimate=pl.CostEstimate(flops=10**9, bytes_accessed=10**6, transcendentals=0),
                 name="tables",
@@ -555,12 +565,12 @@
             arrived = [swap(piece, m, count, core) for piece, m in zip(outs[2:], back_masks[1:])]
 
     x_grad, grad = pl.pallas_call(
-        functools.partial(final_kernel, len(arrived), back_basis, core_mask, low),
+        functools.partial(final_kernel, len(arrived)),
         out_shape=(
             jax.ShapeDtypeStruct((tok, width), BF16),
             jax.ShapeDtypeStruct((experts, rows_out), F32),
         ),
-        in_specs=[VMEM_SPEC] * (6 + len(arrived)),
+        in_specs=[VMEM_SPEC] * (7 + len(arrived)),
         out_specs=(HBM_SPEC, HBM_SPEC),
         scratch_shapes=[
             pltpu.VMEM((tok, width), BF16),

time: 40.2 us -> 40.2 us (level)
  no operation moved by 1% of the time
where the time goes in v4:
time: 40.2 us; the launch traced here: 39.9 us
  starting transfers between devices  18.4 us (46%)
  waiting for transfers between devices  13.7 us (34%)
  Pallas kernels  7.1 us (18%)
  between operations  0.7 us (2%)
    ppermute x14, starting transfers between devices, swap(): lax.ppermute(block, AXES, [(i, i ^ mask[i >> core & 1]) for i in range(co...  13.8 us
    ppermute x14, waiting for transfers between devices, swap(): lax.ppermute(block, AXES, [(i, i ^ mask[i >> core & 1]) for i in range(co...  12.3 us
    ppermute x3, starting transfers between devices, shift(): lax.ppermute(block, AXES, [(i, i ^ (i >> low & 3 ^ step[i >> low & 3]) <<...  4.66 us
    pallas_call x1, Pallas kernels, on_device(): pl.pallas_call(functools.partial(load_kernel, chunks), out_shape=(pltpu.V...  2.48 us
    pallas_call x1, Pallas kernels, on_device(): pl.pallas_call(functools.partial(units_kernel, basis, group_rows, tok, ex...  2.12 us
    ppermute x3, waiting for transfers between devices, shift(): lax.ppermute(block, AXES, [(i, i ^ (i >> low & 3 ^ step[i >> low & 3]) <<...  1.44 us
    pallas_call x1, Pallas kernels, on_device(): pl.pallas_call(functools.partial(final_kernel, len(arrived)), out_shape=(...  1.09 us
    pallas_call x1, Pallas kernels, on_device(): pl.pallas_call(prep_kernel, out_shape=jax.ShapeDtypeStruct((2, tok, width...  0.82 us
  transfers between devices with their start and end apart: 17, of which 13 were waited for; matrix products, arithmetic and copies ran while one was open for 0% of the time, Pallas kernels for 7%

profile of v4, /device:TPU:0, one launch (start us, length us, event | category | flops | bytes accessed | tf_op | source)
XLA Modules:
  0.0 39.9 jit_solution(304587895957902210)
XLA Ops:
  0.6 0.8 %prep.1.refs_0_ = bf16[2,4,2176]{2,1,0:T(4,128)(2,1)S(1)} custom-call(bf16[4,2048]{1,0:T(4,128)(2,1)} %tokens_in.1, bf16[4,2048]{1,0:T(4,128)(2,1)} %grad_in.1, f32[4,16]{1,0:T(4,128)} %logits_in.1, s32[4,8]{1,0:T(4,128)} %chosen_in.1), custom_call_target="tpu_custom_call" | custom-call | tf_op jit(solution)/shard_map/prep/pallas_call | solution.py:433
  1.5 4.1 %collective-permute-start.2 = (bf16[2,4,2176]{2,1,0:T(4,128)(2,1)S(1)}, bf16[2,4,2176]{2,1,0:T(4,128)(2,1)S(1)}, u32[]{:S(2)}, u32[]{:S(2)}) collective-permute-start(bf16[2,4,2176]{2,1,0:T(4,128)(2,1)S(1)} %prep.1.refs_0_), channel_id=1, source_target_pairs={{0,16},{1,17},{2,18},{3,19},{4,20},{5,21},{6,22},{7,23},{8,24},{9,... | collective-permute-start | bytes 104456 | tf_op jit(solution)/shard_map/ppermute | solution.py:51
  5.6 1.3 %collective-permute-start.1 = (bf16[2,4,2176]{2,1,0:T(4,128)(2,1)S(1)}, bf16[2,4,2176]{2,1,0:T(4,128)(2,1)S(1)}, u32[]{:S(2)}, u32[]{:S(2)}) collective-permute-start(bf16[2,4,2176]{2,1,0:T(4,128)(2,1)S(1)} %prep.1.refs_0_), channel_id=1, source_target_pairs={{0,24},{1,25},{2,26},{3,27},{4,28},{5,29},{6,30},{7,31},{8,16},{9,... | collective-permute-start | bytes 104456 | tf_op jit(solution)/shard_map/ppermute | solution.py:51
  6.9 0.2 collective-permute-start
  7.1 0.7 %collective-permute-done.2.refs_3_ = bf16[2,4,2176]{2,1,0:T(4,128)(2,1)S(1)} collective-permute-done((bf16[2,4,2176]{2,1,0:T(4,128)(2,1)S(1)}, bf16[2,4,2176]{2,1,0:T(4,128)(2,1)S(1)}, u32[]{:S(2)}, u32[]{:S(2)}) %collective-permute-start.2) | collective-permute-done | bytes 34848 | tf_op jit(solution)/shard_map/ppermute | solution.py:51
  7.9 3.4 %collective-permute-done.1.refs_2_ = bf16[2,4,2176]{2,1,0:T(4,128)(2,1)S(1)} collective-permute-done((bf16[2,4,2176]{2,1,0:T(4,128)(2,1)S(1)}, bf16[2,4,2176]{2,1,0:T(4,128)(2,1)S(1)}, u32[]{:S(2)}, u32[]{:S(2)}) %collective-permute-start.1) | collective-permute-done | bytes 34848 | tf_op jit(solution)/shard_map/ppermute | solution.py:51
  11.4 2.5 %collective-permute-start.5 = (bf16[32,2176]{1,0:T(8,128)(2,1)S(1)}, bf16[32,2176]{1,0:T(8,128)(2,1)S(1)}, u32[]{:S(2)}, u32[]{:S(2)}) collective-permute-start(bf16[32,2176]{1,0:T(8,128)(2,1)S(1)} %join.1.block_in.refs_0_), channel_id=1, source_target_pairs={{0,5},{1,4},{2,7},{3,6},{4,1},{5,0},{6,3},{7,2},{8,13},{9,12},{10,... | collective-permute-start | bytes 417800 | tf_op jit(solution)/shard_map/ppermute | solution.py:51
  13.9 0.5 %collective-permute-start.4 = (bf16[32,2176]{1,0:T(8,128)(2,1)S(1)}, bf16[32,2176]{1,0:T(8,128)(2,1)S(1)}, u32[]{:S(2)}, u32[]{:S(2)}) collective-permute-start(bf16[32,2176]{1,0:T(8,128)(2,1)S(1)} %join.1.block_in.refs_0_), channel_id=1, source_target_pairs={{0,4},{1,5},{2,6},{3,7},{4,0},{5,1},{6,2},{7,3},{8,12},{9,13},{10,... | collective-permute-start | bytes 417800 | tf_op jit(solution)/shard_map/ppermute | solution.py:51
  14.4 0.5 %collective-permute-start.3 = (bf16[32,2176]{1,0:T(8,128)(2,1)S(1)}, bf16[32,2176]{1,0:T(8,128)(2,1)S(1)}, u32[]{:S(2)}, u32[]{:S(2)}) collective-permute-start(bf16[32,2176]{1,0:T(8,128)(2,1)S(1)} %join.1.block_in.refs_0_), channel_id=1, source_target_pairs={{0,1},{1,0},{2,3},{3,2},{4,5},{5,4},{6,7},{7,6},{8,9},{9,8},{10,11... | collective-permute-start | bytes 417800 | tf_op jit(solution)/shard_map/ppermute | solution.py:51
  14.9 2.5 %load.1 = (bf16[32,2176]{1,0:T(8,128)(2,1)S(1)}, bf16[2048,768]{1,0:T(8,128)(2,1)S(1)}, bf16[384,2048]{1,0:T(8,128)(2,1)S(1)}) custom-call(bf16[32,2176]{1,0:T(8,128)(2,1)S(1)} %join.1.block_in.refs_0_, bf16[1,2048,384]{2,1,0:T(8,128)(2,1)} %gate_in.1, bf16[1,2048,384]{2,1,0:T(8,128)(2,1)} %up_in.1, bf16[1,384,2048]{2,1,0:T(8,128)(2,1)} %down_in.1), custom_call_target="tpu_custom_call" | custom-call | bytes 9437184 | tf_op jit(solution)/shard_map/load/pallas_call | solution.py:470
  17.5 1.4 %collective-permute-done.5.refs_3_ = bf16[32,2176]{1,0:T(8,128)(2,1)S(1)} collective-permute-done((bf16[32,2176]{1,0:T(8,128)(2,1)S(1)}, bf16[32,2176]{1,0:T(8,128)(2,1)S(1)}, u32[]{:S(2)}, u32[]{:S(2)}) %collective-permute-start.5) | collective-permute-done | bytes 139296 | tf_op jit(solution)/shard_map/ppermute | solution.py:51
  18.9 0.8 %collective-permute-done.4.refs_2_ = bf16[32,2176]{1,0:T(8,128)(2,1)S(1)} collective-permute-done((bf16[32,2176]{1,0:T(8,128)(2,1)S(1)}, bf16[32,2176]{1,0:T(8,128)(2,1)S(1)}, u32[]{:S(2)}, u32[]{:S(2)}) %collective-permute-start.4) | collective-permute-done | bytes 139296 | tf_op jit(solution)/shard_map/ppermute | solution.py:51
  19.7 0.5 %collective-permute-start.7 = (bf16[32,2176]{1,0:T(8,128)(2,1)S(1)}, bf16[32,2176]{1,0:T(8,128)(2,1)S(1)}, u32[]{:S(2)}, u32[]{:S(2)}) collective-permute-start(bf16[32,2176]{1,0:T(8,128)(2,1)S(1)} %collective-permute-done.3.refs_1_), channel_id=1, source_target_pairs={{0,2},{1,3},{2,0},{3,1},{4,6},{5,7},{6,4},{7,5},{8,10},{9,11},{10,... | collective-permute-start | bytes 417800 | tf_op jit(solution)/shard_map/ppermute | solution.py:51
  20.2 0.8 %collective-permute-done.8.refs_6_ = bf16[32,2176]{1,0:T(8,128)(2,1)S(1)} collective-permute-done((bf16[32,2176]{1,0:T(8,128)(2,1)S(1)}, bf16[32,2176]{1,0:T(8,128)(2,1)S(1)}, u32[]{:S(2)}, u32[]{:S(2)}) %collective-permute-start.8) | collective-permute-done | bytes 139296 | tf_op jit(solution)/shard_map/ppermute | solution.py:51
  21.0 0.2 collective-permute-done.7.refs_5_
  21.2 2.1 %units.1 = (f32[64,2048]{1,0:T(8,128)S(1)}, bf16[64,2176]{1,0:T(8,128)(2,1)S(1)}, f32[2,128]{1,0:T(2,128)S(1)}) custom-call(bf16[32,2176]{1,0:T(8,128)(2,1)S(1)} %join.1.block_in.refs_0_, bf16[32,2176]{1,0:T(8,128)(2,1)S(1)} %collective-permute-done.3.refs_1_, bf16[32,2176]{1,0:T(8,128)(2,1)S(1)} %collective-permute-done.4.refs_2_, ...), custom_call_target="tpu_custom_call" | custom-call | flops 1006632960 | bytes 5767168 | tf_op jit(solution)/shard_map/units/pallas_call | solution.py:492
  23.3 0.4 collective-permute-start.10
  23.7 1.2 %collective-permute-done.10.refs_2_ = bf16[64,2176]{1,0:T(8,128)(2,1)S(1)} collective-permute-done((bf16[64,2176]{1,0:T(8,128)(2,1)S(1)}, bf16[64,2176]{1,0:T(8,128)(2,1)S(1)}, u32[]{:S(2)}, u32[]{:S(2)}) %collective-permute-start.10) | collective-permute-done | bytes 278560 | tf_op jit(solution)/shard_map/ppermute | solution.py:51
  25.0 0.1 add.2
  25.0 1.2 %collective-permute-start.11 = (bf16[16,2176]{1,0:T(8,128)(2,1)S(1)}, bf16[16,2176]{1,0:T(8,128)(2,1)S(1)}, u32[]{:S(2)}, u32[]{:S(2)}) collective-permute-start(bf16[16,2176]{1,0:T(8,128)(2,1)S(1)} %get-tuple-element.36), channel_id=1, source_target_pairs={{0,1},{1,0},{2,3},{3,2},{4,5},{5,4},{6,7},{7,6},{8,9},{9,8},{10,11... | collective-permute-start | bytes 208904 | tf_op jit(solution)/shard_map/ppermute | solution.py:51
  26.2 0.8 %collective-permute-start.12 = (bf16[16,2176]{1,0:T(8,128)(2,1)S(1)}, bf16[16,2176]{1,0:T(8,128)(2,1)S(1)}, u32[]{:S(2)}, u32[]{:S(2)}) collective-permute-start(bf16[16,2176]{1,0:T(8,128)(2,1)S(1)} %get-tuple-element.37), channel_id=1, source_target_pairs={{0,4},{1,5},{2,6},{3,7},{4,0},{5,1},{6,2},{7,3},{8,12},{9,13},{10,... | collective-permute-start | bytes 208904 | tf_op jit(solution)/shard_map/ppermute | solution.py:51
  27.1 1.5 %collective-permute-start.13 = (bf16[16,2176]{1,0:T(8,128)(2,1)S(1)}, bf16[16,2176]{1,0:T(8,128)(2,1)S(1)}, u32[]{:S(2)}, u32[]{:S(2)}) collective-permute-start(bf16[16,2176]{1,0:T(8,128)(2,1)S(1)} %get-tuple-element.38), channel_id=1, source_target_pairs={{0,5},{1,4},{2,7},{3,6},{4,1},{5,0},{6,3},{7,2},{8,13},{9,12},{10,... | collective-permute-start | bytes 208904 | tf_op jit(solution)/shard_map/ppermute | solution.py:51
  28.6 0.9 %collective-permute-done.11.refs_2_ = bf16[16,2176]{1,0:T(8,128)(2,1)S(1)} collective-permute-done((bf16[16,2176]{1,0:T(8,128)(2,1)S(1)}, bf16[16,2176]{1,0:T(8,128)(2,1)S(1)}, u32[]{:S(2)}, u32[]{:S(2)}) %collective-permute-start.11) | collective-permute-done | bytes 69664 | tf_op jit(solution)/shard_map/ppermute | solution.py:51
  29.5 1.8 %collective-permute-done.12.refs_3_ = bf16[16,2176]{1,0:T(8,128)(2,1)S(1)} collective-permute-done((bf16[16,2176]{1,0:T(8,128)(2,1)S(1)}, bf16[16,2176]{1,0:T(8,128)(2,1)S(1)}, u32[]{:S(2)}, u32[]{:S(2)}) %collective-permute-start.12) | collective-permute-done | bytes 69664 | tf_op jit(solution)/shard_map/ppermute | solution.py:51
  31.3 1.0 %collective-permute-done.13.refs_4_ = bf16[16,2176]{1,0:T(8,128)(2,1)S(1)} collective-permute-done((bf16[16,2176]{1,0:T(8,128)(2,1)S(1)}, bf16[16,2176]{1,0:T(8,128)(2,1)S(1)}, u32[]{:S(2)}, u32[]{:S(2)}) %collective-permute-start.13) | collective-permute-done | bytes 69664 | tf_op jit(solution)/shard_map/ppermute | solution.py:51
  32.3 0.4 collective-permute-start.14
  32.7 2.3 %collective-permute-start.15 = (bf16[4,2560]{1,0:T(4,128)(2,1)S(1)}, bf16[4,2560]{1,0:T(4,128)(2,1)S(1)}, u32[]{:S(2)}, u32[]{:S(2)}) collective-permute-start(bf16[4,2560]{1,0:T(4,128)(2,1)S(1)} %get-tuple-element.42), channel_id=1, source_target_pairs={{0,24},{1,25},{2,26},{3,27},{4,28},{5,29},{6,30},{7,31},{8,16},{9,... | collective-permute-start | bytes 61448 | tf_op jit(solution)/shard_map/ppermute | solution.py:65
  35.1 1.9 %collective-permute-start.16 = (bf16[4,2560]{1,0:T(4,128)(2,1)S(1)}, bf16[4,2560]{1,0:T(4,128)(2,1)S(1)}, u32[]{:S(2)}, u32[]{:S(2)}) collective-permute-start(bf16[4,2560]{1,0:T(4,128)(2,1)S(1)} %get-tuple-element.43), channel_id=1, source_target_pairs={{0,16},{1,17},{2,18},{3,19},{4,20},{5,21},{6,22},{7,23},{8,0},{9,1... | collective-permute-start | bytes 61448 | tf_op jit(solution)/shard_map/ppermute | solution.py:65
  37.0 0.4 tables.1
  37.4 0.9 %collective-permute-done.15.refs_8_ = bf16[4,2560]{1,0:T(4,128)(2,1)S(1)} collective-permute-done((bf16[4,2560]{1,0:T(4,128)(2,1)S(1)}, bf16[4,2560]{1,0:T(4,128)(2,1)S(1)}, u32[]{:S(2)}, u32[]{:S(2)}) %collective-permute-start.15) | collective-permute-done | bytes 20512 | tf_op jit(solution)/shard_map/ppermute | solution.py:65
  38.3 0.5 %collective-permute-done.16.refs_9_ = bf16[4,2560]{1,0:T(4,128)(2,1)S(1)} collective-permute-done((bf16[4,2560]{1,0:T(4,128)(2,1)S(1)}, bf16[4,2560]{1,0:T(4,128)(2,1)S(1)}, u32[]{:S(2)}, u32[]{:S(2)}) %collective-permute-start.16) | collective-permute-done | bytes 20512 | tf_op jit(solution)/shard_map/ppermute | solution.py:65
  38.8 1.1 %final.1 = (bf16[4,2048]{1,0:T(4,128)(2,1)}, f32[16,64]{1,0:T(8,128)}) custom-call(f32[16,128]{1,0:T(8,128)S(1)} %get-tuple-element.31.refs_0_, bf16[128,128]{1,0:T(8,128)(2,1)S(1)} %get-tuple-element.32.refs_1_, bf16[16,128]{1,0:T(8,128)(2,1)S(1)} %get-tuple-element.33.refs_2_, bf16[16,64]{1,0:T(8,128)(2,1)S(1)} %get-tuple-element.34.refs_3_, ...), custom_call_target="tpu_custom_call" | custom-call | tf_op jit(solution)/shard_map/final/pallas_call | solution.py:567
  (12 shorter events, 0.3 us)
Async XLA Ops:
  1.5 6.4 %collective-permute-start.2 = (bf16[2,4,2176]{2,1,0:T(4,128)(2,1)S(1)}, bf16[2,4,2176]{2,1,0:T(4,128)(2,1)S(1)}, u32[]{:S(2)}, u32[]{:S(2)}) collective-permute-start(bf16[2,4,2176]{2,1,0:T(4,128)(2,1)S(1)} %prep.1.refs_0_), channel_id=1, source_target_pairs={{0,16},{1,17},{2,18},{3,19},{4,20},{5,21},{6,22},{7,23},{8,24},{9,... | collective-permute-start | bytes 104456 | tf_op jit(solution)/shard_map/ppermute | solution.py:51
  5.6 5.7 %collective-permute-start.1 = (bf16[2,4,2176]{2,1,0:T(4,128)(2,1)S(1)}, bf16[2,4,2176]{2,1,0:T(4,128)(2,1)S(1)}, u32[]{:S(2)}, u32[]{:S(2)}) collective-permute-start(bf16[2,4,2176]{2,1,0:T(4,128)(2,1)S(1)} %prep.1.refs_0_), channel_id=1, source_target_pairs={{0,24},{1,25},{2,26},{3,27},{4,28},{5,29},{6,30},{7,31},{8,16},{9,... | collective-permute-start | bytes 104456 | tf_op jit(solution)/shard_map/ppermute | solution.py:51
  6.9 4.4 %collective-permute-start = (bf16[2,4,2176]{2,1,0:T(4,128)(2,1)S(1)}, bf16[2,4,2176]{2,1,0:T(4,128)(2,1)S(1)}, u32[]{:S(2)}, u32[]{:S(2)}) collective-permute-start(bf16[2,4,2176]{2,1,0:T(4,128)(2,1)S(1)} %prep.1.refs_0_), channel_id=1, source_target_pairs={{0,8},{1,9},{2,10},{3,11},{4,12},{5,13},{6,14},{7,15},{8,0},{9,1},... | collective-permute-start | bytes 104456 | tf_op jit(solution)/shard_map/ppermute | solution.py:51
  11.4 7.5 %collective-permute-start.5 = (bf16[32,2176]{1,0:T(8,128)(2,1)S(1)}, bf16[32,2176]{1,0:T(8,128)(2,1)S(1)}, u32[]{:S(2)}, u32[]{:S(2)}) collective-permute-start(bf16[32,2176]{1,0:T(8,128)(2,1)S(1)} %join.1.block_in.refs_0_), channel_id=1, source_target_pairs={{0,5},{1,4},{2,7},{3,6},{4,1},{5,0},{6,3},{7,2},{8,13},{9,12},{10,... | collective-permute-start | bytes 417800 | tf_op jit(solution)/shard_map/ppermute | solution.py:51
  13.9 5.8 %collective-permute-start.4 = (bf16[32,2176]{1,0:T(8,128)(2,1)S(1)}, bf16[32,2176]{1,0:T(8,128)(2,1)S(1)}, u32[]{:S(2)}, u32[]{:S(2)}) collective-permute-start(bf16[32,2176]{1,0:T(8,128)(2,1)S(1)} %join.1.block_in.refs_0_), channel_id=1, source_target_pairs={{0,4},{1,5},{2,6},{3,7},{4,0},{5,1},{6,2},{7,3},{8,12},{9,13},{10,... | collective-permute-start | bytes 417800 | tf_op jit(solution)/shard_map/ppermute | solution.py:51
  14.4 5.3 %collective-permute-start.3 = (bf16[32,2176]{1,0:T(8,128)(2,1)S(1)}, bf16[32,2176]{1,0:T(8,128)(2,1)S(1)}, u32[]{:S(2)}, u32[]{:S(2)}) collective-permute-start(bf16[32,2176]{1,0:T(8,128)(2,1)S(1)} %join.1.block_in.refs_0_), channel_id=1, source_target_pairs={{0,1},{1,0},{2,3},{3,2},{4,5},{5,4},{6,7},{7,6},{8,9},{9,8},{10,11... | collective-permute-start | bytes 417800 | tf_op jit(solution)/shard_map/ppermute | solution.py:51
  17.4 2.8 %collective-permute-start.6 = (bf16[32,2176]{1,0:T(8,128)(2,1)S(1)}, bf16[32,2176]{1,0:T(8,128)(2,1)S(1)}, u32[]{:S(2)}, u32[]{:S(2)}) collective-permute-start(bf16[32,2176]{1,0:T(8,128)(2,1)S(1)} %get-tuple-element.24), channel_id=1, source_target_pairs={{0,2},{1,3},{2,0},{3,1},{4,6},{5,7},{6,4},{7,5},{8,10},{9,11},{10,... | collective-permute-start | bytes 417800 | tf_op jit(solution)/shard_map/ppermute | solution.py:51
  18.9 1.4 %collective-permute-start.9 = (bf16[32,2176]{1,0:T(8,128)(2,1)S(1)}, bf16[32,2176]{1,0:T(8,128)(2,1)S(1)}, u32[]{:S(2)}, u32[]{:S(2)}) collective-permute-start(bf16[32,2176]{1,0:T(8,128)(2,1)S(1)} %collective-permute-done.5.refs_3_), channel_id=1, source_target_pairs={{0,2},{1,3},{2,0},{3,1},{4,6},{5,7},{6,4},{7,5},{8,10},{9,11},{10,... | collective-permute-start | bytes 417800 | tf_op jit(solution)/shard_map/ppermute | solution.py:51
  19.6 1.4 %collective-permute-start.8 = (bf16[32,2176]{1,0:T(8,128)(2,1)S(1)}, bf16[32,2176]{1,0:T(8,128)(2,1)S(1)}, u32[]{:S(2)}, u32[]{:S(2)}) collective-permute-start(bf16[32,2176]{1,0:T(8,128)(2,1)S(1)} %collective-permute-done.4.refs_2_), channel_id=1, source_target_pairs={{0,2},{1,3},{2,0},{3,1},{4,6},{5,7},{6,4},{7,5},{8,10},{9,11},{10,... | collective-permute-start | bytes 417800 | tf_op jit(solution)/shard_map/ppermute | solution.py:51
  19.7 1.6 %collective-permute-start.7 = (bf16[32,2176]{1,0:T(8,128)(2,1)S(1)}, bf16[32,2176]{1,0:T(8,128)(2,1)S(1)}, u32[]{:S(2)}, u32[]{:S(2)}) collective-permute-start(bf16[32,2176]{1,0:T(8,128)(2,1)S(1)} %collective-permute-done.3.refs_1_), channel_id=1, source_target_pairs={{0,2},{1,3},{2,0},{3,1},{4,6},{5,7},{6,4},{7,5},{8,10},{9,11},{10,... | collective-permute-start | bytes 417800 | tf_op jit(solution)/shard_map/ppermute | solution.py:51
  23.3 1.6 %collective-permute-start.10 = (bf16[64,2176]{1,0:T(8,128)(2,1)S(1)}, bf16[64,2176]{1,0:T(8,128)(2,1)S(1)}, u32[]{:S(2)}, u32[]{:S(2)}) collective-permute-start(bf16[64,2176]{1,0:T(8,128)(2,1)S(1)} %get-tuple-element.29), channel_id=1, source_target_pairs={{0,2},{1,3},{2,0},{3,1},{4,6},{5,7},{6,4},{7,5},{8,10},{9,11},{10,... | collective-permute-start | bytes 835592 | tf_op jit(solution)/shard_map/ppermute | solution.py:51
  25.0 4.5 %collective-permute-start.11 = (bf16[16,2176]{1,0:T(8,128)(2,1)S(1)}, bf16[16,2176]{1,0:T(8,128)(2,1)S(1)}, u32[]{:S(2)}, u32[]{:S(2)}) collective-permute-start(bf16[16,2176]{1,0:T(8,128)(2,1)S(1)} %get-tuple-element.36), channel_id=1, source_target_pairs={{0,1},{1,0},{2,3},{3,2},{4,5},{5,4},{6,7},{7,6},{8,9},{9,8},{10,11... | collective-permute-start | bytes 208904 | tf_op jit(solution)/shard_map/ppermute | solution.py:51
  26.2 5.1 %collective-permute-start.12 = (bf16[16,2176]{1,0:T(8,128)(2,1)S(1)}, bf16[16,2176]{1,0:T(8,128)(2,1)S(1)}, u32[]{:S(2)}, u32[]{:S(2)}) collective-permute-start(bf16[16,2176]{1,0:T(8,128)(2,1)S(1)} %get-tuple-element.37), channel_id=1, source_target_pairs={{0,4},{1,5},{2,6},{3,7},{4,0},{5,1},{6,2},{7,3},{8,12},{9,13},{10,... | collective-permute-start | bytes 208904 | tf_op jit(solution)/shard_map/ppermute | solution.py:51
  27.1 5.2 %collective-permute-start.13 = (bf16[16,2176]{1,0:T(8,128)(2,1)S(1)}, bf16[16,2176]{1,0:T(8,128)(2,1)S(1)}, u32[]{:S(2)}, u32[]{:S(2)}) collective-permute-start(bf16[16,2176]{1,0:T(8,128)(2,1)S(1)} %get-tuple-element.38), channel_id=1, source_target_pairs={{0,5},{1,4},{2,7},{3,6},{4,1},{5,0},{6,3},{7,2},{8,13},{9,12},{10,... | collective-permute-start | bytes 208904 | tf_op jit(solution)/shard_map/ppermute | solution.py:51
  32.3 5.1 %collective-permute-start.14 = (bf16[4,2560]{1,0:T(4,128)(2,1)S(1)}, bf16[4,2560]{1,0:T(4,128)(2,1)S(1)}, u32[]{:S(2)}, u32[]{:S(2)}) collective-permute-start(bf16[4,2560]{1,0:T(4,128)(2,1)S(1)} %get-tuple-element.41), channel_id=1, source_target_pairs={{0,8},{1,9},{2,10},{3,11},{4,12},{5,13},{6,14},{7,15},{8,24},{9,25... | collective-permute-start | bytes 61448 | tf_op jit(solution)/shard_map/ppermute | solution.py:65
  32.7 5.6 %collective-permute-start.15 = (bf16[4,2560]{1,0:T(4,128)(2,1)S(1)}, bf16[4,2560]{1,0:T(4,128)(2,1)S(1)}, u32[]{:S(2)}, u32[]{:S(2)}) collective-permute-start(bf16[4,2560]{1,0:T(4,128)(2,1)S(1)} %get-tuple-element.42), channel_id=1, source_target_pairs={{0,24},{1,25},{2,26},{3,27},{4,28},{5,29},{6,30},{7,31},{8,16},{9,... | collective-permute-start | bytes 61448 | tf_op jit(solution)/shard_map/ppermute | solution.py:65
  35.1 3.8 %copy-start = (bf16[2048,16]{0,1:T(8,128)(2,1)S(1)}, bf16[2048,16]{0,1:T(8,128)(2,1)}, u32[]{:S(2)}) copy-start(bf16[2048,16]{0,1:T(8,128)(2,1)} %param.12) | copy-start | bytes 196612
  35.1 3.8 %collective-permute-start.16 = (bf16[4,2560]{1,0:T(4,128)(2,1)S(1)}, bf16[4,2560]{1,0:T(4,128)(2,1)S(1)}, u32[]{:S(2)}, u32[]{:S(2)}) collective-permute-start(bf16[4,2560]{1,0:T(4,128)(2,1)S(1)} %get-tuple-element.43), channel_id=1, source_target_pairs={{0,16},{1,17},{2,18},{3,19},{4,20},{5,21},{6,22},{7,23},{8,0},{9,1... | collective-permute-start | bytes 61448 | tf_op jit(solution)/shard_map/ppermute | solution.py:65

commit v5 on v4

--- a/solution.py
+++ b/solution.py
@@ -27,8 +27,8 @@
     first = list(range(max(core + 1, all_bits - 2), all_bits))
     middle = [b for b in range(all_bits) if b != core and b not in first]
     groups = [first] + [middle[i : i + 2] for i in range(0, len(middle), 2)]
-    bases = [[(sum(1 << b for b in group[i:]),) * 2 for i in range(len(group))] for group in groups]
-    bases[0] = bases[0][::-1]
+    bases = [[(sum(1 << b for b in group[: len(group) - i]),) * 2 for i in range(len(group))] for group in groups]
+    bases[0] = [(sum(1 << b for b in first[i:]),) * 2 for i in range(len(first))][::-1]
     return bases, core
 
 

time: 40.2 us -> 40.7 us (1.012)
  waiting for transfers between devices: 13.7 us -> 14.2 us
    ppermute x14, waiting for transfers between devices: 12.3 us -> 12.7 us  [swap(): lax.ppermute(block, AXES, [(i, i ^ mask[i >> core & 1]) for i in range(co...]
where the time goes in v5:
time: 40.7 us; the launch traced here: 40.4 us
  starting transfers between devices  18.4 us (45%)
  waiting for transfers between devices  14.2 us (35%)
  Pallas kernels  7.11 us (17%)
  between operations  0.7 us (2%)
    ppermute x14, starting transfers between devices, swap(): lax.ppermute(block, AXES, [(i, i ^ mask[i >> core & 1]) for i in range(co...  13.8 us
    ppermute x14, waiting for transfers between devices, swap(): lax.ppermute(block, AXES, [(i, i ^ mask[i >> core & 1]) for i in range(co...  12.7 us
    ppermute x3, starting transfers between devices, shift(): lax.ppermute(block, AXES, [(i, i ^ (i >> low & 3 ^ step[i >> low & 3]) <<...  4.65 us
    pallas_call x1, Pallas kernels, on_device(): pl.pallas_call(functools.partial(load_kernel, chunks), out_shape=(pltpu.V...  2.48 us
    pallas_call x1, Pallas kernels, on_device(): pl.pallas_call(functools.partial(units_kernel, basis, group_rows, tok, ex...  2.13 us
    ppermute x3, waiting for transfers between devices, shift(): lax.ppermute(block, AXES, [(i, i ^ (i >> low & 3 ^ step[i >> low & 3]) <<...  1.44 us
    pallas_call x1, Pallas kernels, on_device(): pl.pallas_call(functools.partial(final_kernel, len(arrived)), out_shape=(...  1.09 us
    pallas_call x1, Pallas kernels, on_device(): pl.pallas_call(prep_kernel, out_shape=jax.ShapeDtypeStruct((2, tok, width...  0.82 us
  transfers between devices with their start and end apart: 17, of which 13 were waited for; matrix products, arithmetic and copies ran while one was open for 0% of the time, Pallas kernels for 7%

profile of v5, /device:TPU:0, one launch (start us, length us, event | category | flops | bytes accessed | tf_op | source)
XLA Modules:
  0.0 40.4 jit_solution(11059396078123803686)
XLA Ops:
  0.6 0.8 %prep.1.refs_0_ = bf16[2,4,2176]{2,1,0:T(4,128)(2,1)S(1)} custom-call(bf16[4,2048]{1,0:T(4,128)(2,1)} %tokens_in.1, bf16[4,2048]{1,0:T(4,128)(2,1)} %grad_in.1, f32[4,16]{1,0:T(4,128)} %logits_in.1, s32[4,8]{1,0:T(4,128)} %chosen_in.1), custom_call_target="tpu_custom_call" | custom-call | tf_op jit(solution)/shard_map/prep/pallas_call | solution.py:433
  1.5 4.1 %collective-permute-start.2 = (bf16[2,4,2176]{2,1,0:T(4,128)(2,1)S(1)}, bf16[2,4,2176]{2,1,0:T(4,128)(2,1)S(1)}, u32[]{:S(2)}, u32[]{:S(2)}) collective-permute-start(bf16[2,4,2176]{2,1,0:T(4,128)(2,1)S(1)} %prep.1.refs_0_), channel_id=1, source_target_pairs={{0,16},{1,17},{2,18},{3,19},{4,20},{5,21},{6,22},{7,23},{8,24},{9,... | collective-permute-start | bytes 104456 | tf_op jit(solution)/shard_map/ppermute | solution.py:51
  5.6 1.3 %collective-permute-start.1 = (bf16[2,4,2176]{2,1,0:T(4,128)(2,1)S(1)}, bf16[2,4,2176]{2,1,0:T(4,128)(2,1)S(1)}, u32[]{:S(2)}, u32[]{:S(2)}) collective-permute-start(bf16[2,4,2176]{2,1,0:T(4,128)(2,1)S(1)} %prep.1.refs_0_), channel_id=1, source_target_pairs={{0,24},{1,25},{2,26},{3,27},{4,28},{5,29},{6,30},{7,31},{8,16},{9,... | collective-permute-start | bytes 104456 | tf_op jit(solution)/shard_map/ppermute | solution.py:51
  6.9 0.2 collective-permute-start
  7.1 0.7 %collective-permute-done.2.refs_3_ = bf16[2,4,2176]{2,1,0:T(4,128)(2,1)S(1)} collective-permute-done((bf16[2,4,2176]{2,1,0:T(4,128)(2,1)S(1)}, bf16[2,4,2176]{2,1,0:T(4,128)(2,1)S(1)}, u32[]{:S(2)}, u32[]{:S(2)}) %collective-permute-start.2) | collective-permute-done | bytes 34848 | tf_op jit(solution)/shard_map/ppermute | solution.py:51
  7.9 3.4 %collective-permute-done.1.refs_2_ = bf16[2,4,2176]{2,1,0:T(4,128)(2,1)S(1)} collective-permute-done((bf16[2,4,2176]{2,1,0:T(4,128)(2,1)S(1)}, bf16[2,4,2176]{2,1,0:T(4,128)(2,1)S(1)}, u32[]{:S(2)}, u32[]{:S(2)}) %collective-permute-start.1) | collective-permute-done | bytes 34848 | tf_op jit(solution)/shard_map/ppermute | solution.py:51
  11.4 2.5 %collective-permute-start.5 = (bf16[32,2176]{1,0:T(8,128)(2,1)S(1)}, bf16[32,2176]{1,0:T(8,128)(2,1)S(1)}, u32[]{:S(2)}, u32[]{:S(2)}) collective-permute-start(bf16[32,2176]{1,0:T(8,128)(2,1)S(1)} %join.1.block_in.refs_0_), channel_id=1, source_target_pairs={{0,5},{1,4},{2,7},{3,6},{4,1},{5,0},{6,3},{7,2},{8,13},{9,12},{10,... | collective-permute-start | bytes 417800 | tf_op jit(solution)/shard_map/ppermute | solution.py:51
  13.9 0.5 %collective-permute-start.4 = (bf16[32,2176]{1,0:T(8,128)(2,1)S(1)}, bf16[32,2176]{1,0:T(8,128)(2,1)S(1)}, u32[]{:S(2)}, u32[]{:S(2)}) collective-permute-start(bf16[32,2176]{1,0:T(8,128)(2,1)S(1)} %join.1.block_in.refs_0_), channel_id=1, source_target_pairs={{0,1},{1,0},{2,3},{3,2},{4,5},{5,4},{6,7},{7,6},{8,9},{9,8},{10,11... | collective-permute-start | bytes 417800 | tf_op jit(solution)/shard_map/ppermute | solution.py:51
  14.4 0.5 %collective-permute-start.3 = (bf16[32,2176]{1,0:T(8,128)(2,1)S(1)}, bf16[32,2176]{1,0:T(8,128)(2,1)S(1)}, u32[]{:S(2)}, u32[]{:S(2)}) collective-permute-start(bf16[32,2176]{1,0:T(8,128)(2,1)S(1)} %join.1.block_in.refs_0_), channel_id=1, source_target_pairs={{0,4},{1,5},{2,6},{3,7},{4,0},{5,1},{6,2},{7,3},{8,12},{9,13},{10,... | collective-permute-start | bytes 417800 | tf_op jit(solution)/shard_map/ppermute | solution.py:51
  14.9 2.5 %load.1 = (bf16[32,2176]{1,0:T(8,128)(2,1)S(1)}, bf16[2048,768]{1,0:T(8,128)(2,1)S(1)}, bf16[384,2048]{1,0:T(8,128)(2,1)S(1)}) custom-call(bf16[32,2176]{1,0:T(8,128)(2,1)S(1)} %join.1.block_in.refs_0_, bf16[1,2048,384]{2,1,0:T(8,128)(2,1)} %gate_in.1, bf16[1,2048,384]{2,1,0:T(8,128)(2,1)} %up_in.1, bf16[1,384,2048]{2,1,0:T(8,128)(2,1)} %down_in.1), custom_call_target="tpu_custom_call" | custom-call | bytes 9437184 | tf_op jit(solution)/shard_map/load/pallas_call | solution.py:470
  17.5 0.3 collective-permute-done.5.refs_3_
  17.8 0.2 collective-permute-start.9
  18.0 1.4 %collective-permute-done.4.refs_2_ = bf16[32,2176]{1,0:T(8,128)(2,1)S(1)} collective-permute-done((bf16[32,2176]{1,0:T(8,128)(2,1)S(1)}, bf16[32,2176]{1,0:T(8,128)(2,1)S(1)}, u32[]{:S(2)}, u32[]{:S(2)}) %collective-permute-start.4) | collective-permute-done | bytes 139296 | tf_op jit(solution)/shard_map/ppermute | solution.py:51
  19.5 0.4 collective-permute-start.7
  19.9 0.8 %collective-permute-done.8.refs_6_ = bf16[32,2176]{1,0:T(8,128)(2,1)S(1)} collective-permute-done((bf16[32,2176]{1,0:T(8,128)(2,1)S(1)}, bf16[32,2176]{1,0:T(8,128)(2,1)S(1)}, u32[]{:S(2)}, u32[]{:S(2)}) %collective-permute-start.8) | collective-permute-done | bytes 139296 | tf_op jit(solution)/shard_map/ppermute | solution.py:51
  20.7 0.2 collective-permute-done.7.refs_5_
  20.9 2.1 %units.1 = (f32[64,2048]{1,0:T(8,128)S(1)}, bf16[64,2176]{1,0:T(8,128)(2,1)S(1)}, f32[2,128]{1,0:T(2,128)S(1)}) custom-call(bf16[32,2176]{1,0:T(8,128)(2,1)S(1)} %join.1.block_in.refs_0_, bf16[32,2176]{1,0:T(8,128)(2,1)S(1)} %collective-permute-done.3.refs_1_, bf16[32,2176]{1,0:T(8,128)(2,1)S(1)} %collective-permute-done.4.refs_2_, ...), custom_call_target="tpu_custom_call" | custom-call | flops 1006632960 | bytes 5767168 | tf_op jit(solution)/shard_map/units/pallas_call | solution.py:492
  23.0 0.4 collective-permute-start.10
  23.4 1.2 %collective-permute-done.10.refs_2_ = bf16[64,2176]{1,0:T(8,128)(2,1)S(1)} collective-permute-done((bf16[64,2176]{1,0:T(8,128)(2,1)S(1)}, bf16[64,2176]{1,0:T(8,128)(2,1)S(1)}, u32[]{:S(2)}, u32[]{:S(2)}) %collective-permute-start.10) | collective-permute-done | bytes 278560 | tf_op jit(solution)/shard_map/ppermute | solution.py:51
  24.7 1.3 %collective-permute-start.11 = (bf16[16,2176]{1,0:T(8,128)(2,1)S(1)}, bf16[16,2176]{1,0:T(8,128)(2,1)S(1)}, u32[]{:S(2)}, u32[]{:S(2)}) collective-permute-start(bf16[16,2176]{1,0:T(8,128)(2,1)S(1)} %get-tuple-element.36), channel_id=1, source_target_pairs={{0,4},{1,5},{2,6},{3,7},{4,0},{5,1},{6,2},{7,3},{8,12},{9,13},{10,... | collective-permute-start | bytes 208904 | tf_op jit(solution)/shard_map/ppermute | solution.py:51
  26.0 1.5 %collective-permute-start.12 = (bf16[16,2176]{1,0:T(8,128)(2,1)S(1)}, bf16[16,2176]{1,0:T(8,128)(2,1)S(1)}, u32[]{:S(2)}, u32[]{:S(2)}) collective-permute-start(bf16[16,2176]{1,0:T(8,128)(2,1)S(1)} %get-tuple-element.37), channel_id=1, source_target_pairs={{0,1},{1,0},{2,3},{3,2},{4,5},{5,4},{6,7},{7,6},{8,9},{9,8},{10,11... | collective-permute-start | bytes 208904 | tf_op jit(solution)/shard_map/ppermute | solution.py:51
  27.6 0.7 %collective-permute-start.13 = (bf16[16,2176]{1,0:T(8,128)(2,1)S(1)}, bf16[16,2176]{1,0:T(8,128)(2,1)S(1)}, u32[]{:S(2)}, u32[]{:S(2)}) collective-permute-start(bf16[16,2176]{1,0:T(8,128)(2,1)S(1)} %get-tuple-element.38), channel_id=1, source_target_pairs={{0,5},{1,4},{2,7},{3,6},{4,1},{5,0},{6,3},{7,2},{8,13},{9,12},{10,... | collective-permute-start | bytes 208904 | tf_op jit(solution)/shard_map/ppermute | solution.py:51
  28.3 0.9 %collective-permute-done.11.refs_2_ = bf16[16,2176]{1,0:T(8,128)(2,1)S(1)} collective-permute-done((bf16[16,2176]{1,0:T(8,128)(2,1)S(1)}, bf16[16,2176]{1,0:T(8,128)(2,1)S(1)}, u32[]{:S(2)}, u32[]{:S(2)}) %collective-permute-start.11) | collective-permute-done | bytes 69664 | tf_op jit(solution)/shard_map/ppermute | solution.py:51
  29.2 1.5 %collective-permute-done.12.refs_3_ = bf16[16,2176]{1,0:T(8,128)(2,1)S(1)} collective-permute-done((bf16[16,2176]{1,0:T(8,128)(2,1)S(1)}, bf16[16,2176]{1,0:T(8,128)(2,1)S(1)}, u32[]{:S(2)}, u32[]{:S(2)}) %collective-permute-start.12) | collective-permute-done | bytes 69664 | tf_op jit(solution)/shard_map/ppermute | solution.py:51
  30.7 2.1 %collective-permute-done.13.refs_4_ = bf16[16,2176]{1,0:T(8,128)(2,1)S(1)} collective-permute-done((bf16[16,2176]{1,0:T(8,128)(2,1)S(1)}, bf16[16,2176]{1,0:T(8,128)(2,1)S(1)}, u32[]{:S(2)}, u32[]{:S(2)}) %collective-permute-start.13) | collective-permute-done | bytes 69664 | tf_op jit(solution)/shard_map/ppermute | solution.py:51
  32.9 0.4 collective-permute-start.14
  33.2 2.3 %collective-permute-start.15 = (bf16[4,2560]{1,0:T(4,128)(2,1)S(1)}, bf16[4,2560]{1,0:T(4,128)(2,1)S(1)}, u32[]{:S(2)}, u32[]{:S(2)}) collective-permute-start(bf16[4,2560]{1,0:T(4,128)(2,1)S(1)} %get-tuple-element.42), channel_id=1, source_target_pairs={{0,24},{1,25},{2,26},{3,27},{4,28},{5,29},{6,30},{7,31},{8,16},{9,... | collective-permute-start | bytes 61448 | tf_op jit(solution)/shard_map/ppermute | solution.py:65
  35.6 1.9 %collective-permute-start.16 = (bf16[4,2560]{1,0:T(4,128)(2,1)S(1)}, bf16[4,2560]{1,0:T(4,128)(2,1)S(1)}, u32[]{:S(2)}, u32[]{:S(2)}) collective-permute-start(bf16[4,2560]{1,0:T(4,128)(2,1)S(1)} %get-tuple-element.43), channel_id=1, source_target_pairs={{0,16},{1,17},{2,18},{3,19},{4,20},{5,21},{6,22},{7,23},{8,0},{9,1... | collective-permute-start | bytes 61448 | tf_op jit(solution)/shard_map/ppermute | solution.py:65
  37.5 0.4 tables.1
  37.9 0.9 %collective-permute-done.15.refs_8_ = bf16[4,2560]{1,0:T(4,128)(2,1)S(1)} collective-permute-done((bf16[4,2560]{1,0:T(4,128)(2,1)S(1)}, bf16[4,2560]{1,0:T(4,128)(2,1)S(1)}, u32[]{:S(2)}, u32[]{:S(2)}) %collective-permute-start.15) | collective-permute-done | bytes 20512 | tf_op jit(solution)/shard_map/ppermute | solution.py:65
  38.8 0.5 %collective-permute-done.16.refs_9_ = bf16[4,2560]{1,0:T(4,128)(2,1)S(1)} collective-permute-done((bf16[4,2560]{1,0:T(4,128)(2,1)S(1)}, bf16[4,2560]{1,0:T(4,128)(2,1)S(1)}, u32[]{:S(2)}, u32[]{:S(2)}) %collective-permute-start.16) | collective-permute-done | bytes 20512 | tf_op jit(solution)/shard_map/ppermute | solution.py:65
  39.3 1.1 %final.1 = (bf16[4,2048]{1,0:T(4,128)(2,1)}, f32[16,64]{1,0:T(8,128)}) custom-call(f32[16,128]{1,0:T(8,128)S(1)} %get-tuple-element.31.refs_0_, bf16[128,128]{1,0:T(8,128)(2,1)S(1)} %get-tuple-element.32.refs_1_, bf16[16,128]{1,0:T(8,128)(2,1)S(1)} %get-tuple-element.33.refs_2_, bf16[16,64]{1,0:T(8,128)(2,1)S(1)} %get-tuple-element.34.refs_3_, ...), custom_call_target="tpu_custom_call" | custom-call | tf_op jit(solution)/shard_map/final/pallas_call | solution.py:567
  (12 shorter events, 0.4 us)
Async XLA Ops:
  1.5 6.4 %collective-permute-start.2 = (bf16[2,4,2176]{2,1,0:T(4,128)(2,1)S(1)}, bf16[2,4,2176]{2,1,0:T(4,128)(2,1)S(1)}, u32[]{:S(2)}, u32[]{:S(2)}) collective-permute-start(bf16[2,4,2176]{2,1,0:T(4,128)(2,1)S(1)} %prep.1.refs_0_), channel_id=1, source_target_pairs={{0,16},{1,17},{2,18},{3,19},{4,20},{5,21},{6,22},{7,23},{8,24},{9,... | collective-permute-start | bytes 104456 | tf_op jit(solution)/shard_map/ppermute | solution.py:51
  5.6 5.7 %collective-permute-start.1 = (bf16[2,4,2176]{2,1,0:T(4,128)(2,1)S(1)}, bf16[2,4,2176]{2,1,0:T(4,128)(2,1)S(1)}, u32[]{:S(2)}, u32[]{:S(2)}) collective-permute-start(bf16[2,4,2176]{2,1,0:T(4,128)(2,1)S(1)} %prep.1.refs_0_), channel_id=1, source_target_pairs={{0,24},{1,25},{2,26},{3,27},{4,28},{5,29},{6,30},{7,31},{8,16},{9,... | collective-permute-start | bytes 104456 | tf_op jit(solution)/shard_map/ppermute | solution.py:51
  6.9 4.4 %collective-permute-start = (bf16[2,4,2176]{2,1,0:T(4,128)(2,1)S(1)}, bf16[2,4,2176]{2,1,0:T(4,128)(2,1)S(1)}, u32[]{:S(2)}, u32[]{:S(2)}) collective-permute-start(bf16[2,4,2176]{2,1,0:T(4,128)(2,1)S(1)} %prep.1.refs_0_), channel_id=1, source_target_pairs={{0,8},{1,9},{2,10},{3,11},{4,12},{5,13},{6,14},{7,15},{8,0},{9,1},... | collective-permute-start | bytes 104456 | tf_op jit(solution)/shard_map/ppermute | solution.py:51
  11.4 6.5 %collective-permute-start.5 = (bf16[32,2176]{1,0:T(8,128)(2,1)S(1)}, bf16[32,2176]{1,0:T(8,128)(2,1)S(1)}, u32[]{:S(2)}, u32[]{:S(2)}) collective-permute-start(bf16[32,2176]{1,0:T(8,128)(2,1)S(1)} %join.1.block_in.refs_0_), channel_id=1, source_target_pairs={{0,5},{1,4},{2,7},{3,6},{4,1},{5,0},{6,3},{7,2},{8,13},{9,12},{10,... | collective-permute-start | bytes 417800 | tf_op jit(solution)/shard_map/ppermute | solution.py:51
  13.9 5.5 %collective-permute-start.4 = (bf16[32,2176]{1,0:T(8,128)(2,1)S(1)}, bf16[32,2176]{1,0:T(8,128)(2,1)S(1)}, u32[]{:S(2)}, u32[]{:S(2)}) collective-permute-start(bf16[32,2176]{1,0:T(8,128)(2,1)S(1)} %join.1.block_in.refs_0_), channel_id=1, source_target_pairs={{0,1},{1,0},{2,3},{3,2},{4,5},{5,4},{6,7},{7,6},{8,9},{9,8},{10,11... | collective-permute-start | bytes 417800 | tf_op jit(solution)/shard_map/ppermute | solution.py:51
  14.4 5.1 %collective-permute-start.3 = (bf16[32,2176]{1,0:T(8,128)(2,1)S(1)}, bf16[32,2176]{1,0:T(8,128)(2,1)S(1)}, u32[]{:S(2)}, u32[]{:S(2)}) collective-permute-start(bf16[32,2176]{1,0:T(8,128)(2,1)S(1)} %join.1.block_in.refs_0_), channel_id=1, source_target_pairs={{0,4},{1,5},{2,6},{3,7},{4,0},{5,1},{6,2},{7,3},{8,12},{9,13},{10,... | collective-permute-start | bytes 417800 | tf_op jit(solution)/shard_map/ppermute | solution.py:51
  17.4 2.5 %collective-permute-start.6 = (bf16[32,2176]{1,0:T(8,128)(2,1)S(1)}, bf16[32,2176]{1,0:T(8,128)(2,1)S(1)}, u32[]{:S(2)}, u32[]{:S(2)}) collective-permute-start(bf16[32,2176]{1,0:T(8,128)(2,1)S(1)} %get-tuple-element.24), channel_id=1, source_target_pairs={{0,2},{1,3},{2,0},{3,1},{4,6},{5,7},{6,4},{7,5},{8,10},{9,11},{10,... | collective-permute-start | bytes 417800 | tf_op jit(solution)/shard_map/ppermute | solution.py:51
  17.8 2.0 %collective-permute-start.9 = (bf16[32,2176]{1,0:T(8,128)(2,1)S(1)}, bf16[32,2176]{1,0:T(8,128)(2,1)S(1)}, u32[]{:S(2)}, u32[]{:S(2)}) collective-permute-start(bf16[32,2176]{1,0:T(8,128)(2,1)S(1)} %collective-permute-done.5.refs_3_), channel_id=1, source_target_pairs={{0,2},{1,3},{2,0},{3,1},{4,6},{5,7},{6,4},{7,5},{8,10},{9,11},{10,... | collective-permute-start | bytes 417800 | tf_op jit(solution)/shard_map/ppermute | solution.py:51
  19.3 1.4 %collective-permute-start.8 = (bf16[32,2176]{1,0:T(8,128)(2,1)S(1)}, bf16[32,2176]{1,0:T(8,128)(2,1)S(1)}, u32[]{:S(2)}, u32[]{:S(2)}) collective-permute-start(bf16[32,2176]{1,0:T(8,128)(2,1)S(1)} %collective-permute-done.4.refs_2_), channel_id=1, source_target_pairs={{0,2},{1,3},{2,0},{3,1},{4,6},{5,7},{6,4},{7,5},{8,10},{9,11},{10,... | collective-permute-start | bytes 417800 | tf_op jit(solution)/shard_map/ppermute | solution.py:51
  19.5 1.4 %collective-permute-start.7 = (bf16[32,2176]{1,0:T(8,128)(2,1)S(1)}, bf16[32,2176]{1,0:T(8,128)(2,1)S(1)}, u32[]{:S(2)}, u32[]{:S(2)}) collective-permute-start(bf16[32,2176]{1,0:T(8,128)(2,1)S(1)} %collective-permute-done.3.refs_1_), channel_id=1, source_target_pairs={{0,2},{1,3},{2,0},{3,1},{4,6},{5,7},{6,4},{7,5},{8,10},{9,11},{10,... | collective-permute-start | bytes 417800 | tf_op jit(solution)/shard_map/ppermute | solution.py:51
  23.0 1.6 %collective-permute-start.10 = (bf16[64,2176]{1,0:T(8,128)(2,1)S(1)}, bf16[64,2176]{1,0:T(8,128)(2,1)S(1)}, u32[]{:S(2)}, u32[]{:S(2)}) collective-permute-start(bf16[64,2176]{1,0:T(8,128)(2,1)S(1)} %get-tuple-element.29), channel_id=1, source_target_pairs={{0,2},{1,3},{2,0},{3,1},{4,6},{5,7},{6,4},{7,5},{8,10},{9,11},{10,... | collective-permute-start | bytes 835592 | tf_op jit(solution)/shard_map/ppermute | solution.py:51
  24.7 4.5 %collective-permute-start.11 = (bf16[16,2176]{1,0:T(8,128)(2,1)S(1)}, bf16[16,2176]{1,0:T(8,128)(2,1)S(1)}, u32[]{:S(2)}, u32[]{:S(2)}) collective-permute-start(bf16[16,2176]{1,0:T(8,128)(2,1)S(1)} %get-tuple-element.36), channel_id=1, source_target_pairs={{0,4},{1,5},{2,6},{3,7},{4,0},{5,1},{6,2},{7,3},{8,12},{9,13},{10,... | collective-permute-start | bytes 208904 | tf_op jit(solution)/shard_map/ppermute | solution.py:51
  26.0 4.6 %collective-permute-start.12 = (bf16[16,2176]{1,0:T(8,128)(2,1)S(1)}, bf16[16,2176]{1,0:T(8,128)(2,1)S(1)}, u32[]{:S(2)}, u32[]{:S(2)}) collective-permute-start(bf16[16,2176]{1,0:T(8,128)(2,1)S(1)} %get-tuple-element.37), channel_id=1, source_target_pairs={{0,1},{1,0},{2,3},{3,2},{4,5},{5,4},{6,7},{7,6},{8,9},{9,8},{10,11... | collective-permute-start | bytes 208904 | tf_op jit(solution)/shard_map/ppermute | solution.py:51
  27.6 5.2 %collective-permute-start.13 = (bf16[16,2176]{1,0:T(8,128)(2,1)S(1)}, bf16[16,2176]{1,0:T(8,128)(2,1)S(1)}, u32[]{:S(2)}, u32[]{:S(2)}) collective-permute-start(bf16[16,2176]{1,0:T(8,128)(2,1)S(1)} %get-tuple-element.38), channel_id=1, source_target_pairs={{0,5},{1,4},{2,7},{3,6},{4,1},{5,0},{6,3},{7,2},{8,13},{9,12},{10,... | collective-permute-start | bytes 208904 | tf_op jit(solution)/shard_map/ppermute | solution.py:51
  32.9 5.0 %collective-permute-start.14 = (bf16[4,2560]{1,0:T(4,128)(2,1)S(1)}, bf16[4,2560]{1,0:T(4,128)(2,1)S(1)}, u32[]{:S(2)}, u32[]{:S(2)}) collective-permute-start(bf16[4,2560]{1,0:T(4,128)(2,1)S(1)} %get-tuple-element.41), channel_id=1, source_target_pairs={{0,8},{1,9},{2,10},{3,11},{4,12},{5,13},{6,14},{7,15},{8,24},{9,25... | collective-permute-start | bytes 61448 | tf_op jit(solution)/shard_map/ppermute | solution.py:65
  33.2 5.6 %collective-permute-start.15 = (bf16[4,2560]{1,0:T(4,128)(2,1)S(1)}, bf16[4,2560]{1,0:T(4,128)(2,1)S(1)}, u32[]{:S(2)}, u32[]{:S(2)}) collective-permute-start(bf16[4,2560]{1,0:T(4,128)(2,1)S(1)} %get-tuple-element.42), channel_id=1, source_target_pairs={{0,24},{1,25},{2,26},{3,27},{4,28},{5,29},{6,30},{7,31},{8,16},{9,... | collective-permute-start | bytes 61448 | tf_op jit(solution)/shard_map/ppermute | solution.py:65
  35.6 3.8 %copy-start = (bf16[2048,16]{0,1:T(8,128)(2,1)S(1)}, bf16[2048,16]{0,1:T(8,128)(2,1)}, u32[]{:S(2)}) copy-start(bf16[2048,16]{0,1:T(8,128)(2,1)} %param.12) | copy-start | bytes 196612
  35.6 3.8 %collective-permute-start.16 = (bf16[4,2560]{1,0:T(4,128)(2,1)S(1)}, bf16[4,2560]{1,0:T(4,128)(2,1)S(1)}, u32[]{:S(2)}, u32[]{:S(2)}) collective-permute-start(bf16[4,2560]{1,0:T(4,128)(2,1)S(1)} %get-tuple-element.43), channel_id=1, source_target_pairs={{0,16},{1,17},{2,18},{3,19},{4,20},{5,21},{6,22},{7,23},{8,0},{9,1... | collective-permute-start | bytes 61448 | tf_op jit(solution)/shard_map/ppermute | solution.py:65

commit v6 on v4

--- a/solution.py
+++ b/solution.py
@@ -391,6 +391,12 @@
     mean = jnp.sum(probs * scores, axis=0, keepdims=True)
     logit_grad = (probs * (scores - mean)).astype(BF16)
     mine = lax.dot_general(mine_ref[...], logit_grad, NT, preferred_element_type=F32)
+    grad = jnp.dot(logit_grad, column_ref[...], preferred_element_type=F32)
+    rows_out = grad_ref.shape[1]
+    first = own * rows_out % LANES
+    grad_ref[...] = pltpu.roll(grad, (LANES - first) % LANES, 1)[:, :rows_out]
+    grad_copy = pltpu.make_async_copy(grad_ref, grad_out, sems.at[1])
+    grad_copy.start()
     part = jnp.dot(mine.astype(BF16), router_ref[...], preferred_element_type=F32)
     total = kept_ref[...]
     for ref in arrived:
@@ -398,12 +404,6 @@
     x_ref[...] = (total + part[:tok]).astype(BF16)
     x_copy = pltpu.make_async_copy(x_ref, x_out, sems.at[0])
     x_copy.start()
-    grad = jnp.dot(logit_grad, column_ref[...], preferred_element_type=F32)
-    rows_out = grad_ref.shape[1]
-    first = own * rows_out % LANES
-    grad_ref[...] = pltpu.roll(grad, (LANES - first) % LANES, 1)[:, :rows_out]
-    grad_copy = pltpu.make_async_copy(grad_ref, grad_out, sems.at[1])
-    grad_copy.start()
     x_copy.wait()
     grad_copy.wait()
 

time: 40.2 us -> 40.1 us (level)
  no operation moved by 1% of the time
where the time goes in v6:
time: 40.1 us; the launch traced here: 39.9 us
  starting transfers between devices  18.4 us (46%)
  waiting for transfers between devices  13.7 us (34%)
  Pallas kernels  7.03 us (18%)
  between operations  0.7 us (2%)
    ppermute x14, starting transfers between devices, swap(): lax.ppermute(block, AXES, [(i, i ^ mask[i >> core & 1]) for i in range(co...  13.8 us
    ppermute x14, waiting for transfers between devices, swap(): lax.ppermute(block, AXES, [(i, i ^ mask[i >> core & 1]) for i in range(co...  12.3 us
    ppermute x3, starting transfers between devices, shift(): lax.ppermute(block, AXES, [(i, i ^ (i >> low & 3 ^ step[i >> low & 3]) <<...  4.66 us
    pallas_call x1, Pallas kernels, on_device(): pl.pallas_call(functools.partial(load_kernel, chunks), out_shape=(pltpu.V...  2.48 us
    pallas_call x1, Pallas kernels, on_device(): pl.pallas_call(functools.partial(units_kernel, basis, group_rows, tok, ex...  2.12 us
    ppermute x3, waiting for transfers between devices, shift(): lax.ppermute(block, AXES, [(i, i ^ (i >> low & 3 ^ step[i >> low & 3]) <<...  1.44 us
    pallas_call x1, Pallas kernels, on_device(): pl.pallas_call(functools.partial(final_kernel, len(arrived)), out_shape=(...  1.03 us
    pallas_call x1, Pallas kernels, on_device(): pl.pallas_call(prep_kernel, out_shape=jax.ShapeDtypeStruct((2, tok, width...  0.82 us
  transfers between devices with their start and end apart: 17, of which 13 were waited for; matrix products, arithmetic and copies ran while one was open for 0% of the time, Pallas kernels for 7%

profile of v6, /device:TPU:0, one launch (start us, length us, event | category | flops | bytes accessed | tf_op | source)
XLA Modules:
  0.0 39.9 jit_solution(6660387066128802050)
XLA Ops:
  0.6 0.8 %prep.1.refs_0_ = bf16[2,4,2176]{2,1,0:T(4,128)(2,1)S(1)} custom-call(bf16[4,2048]{1,0:T(4,128)(2,1)} %tokens_in.1, bf16[4,2048]{1,0:T(4,128)(2,1)} %grad_in.1, f32[4,16]{1,0:T(4,128)} %logits_in.1, s32[4,8]{1,0:T(4,128)} %chosen_in.1), custom_call_target="tpu_custom_call" | custom-call | tf_op jit(solution)/shard_map/prep/pallas_call | solution.py:433
  1.5 4.1 %collective-permute-start.2 = (bf16[2,4,2176]{2,1,0:T(4,128)(2,1)S(1)}, bf16[2,4,2176]{2,1,0:T(4,128)(2,1)S(1)}, u32[]{:S(2)}, u32[]{:S(2)}) collective-permute-start(bf16[2,4,2176]{2,1,0:T(4,128)(2,1)S(1)} %prep.1.refs_0_), channel_id=1, source_target_pairs={{0,16},{1,17},{2,18},{3,19},{4,20},{5,21},{6,22},{7,23},{8,24},{9,... | collective-permute-start | bytes 104456 | tf_op jit(solution)/shard_map/ppermute | solution.py:51
  5.6 1.3 %collective-permute-start.1 = (bf16[2,4,2176]{2,1,0:T(4,128)(2,1)S(1)}, bf16[2,4,2176]{2,1,0:T(4,128)(2,1)S(1)}, u32[]{:S(2)}, u32[]{:S(2)}) collective-permute-start(bf16[2,4,2176]{2,1,0:T(4,128)(2,1)S(1)} %prep.1.refs_0_), channel_id=1, source_target_pairs={{0,24},{1,25},{2,26},{3,27},{4,28},{5,29},{6,30},{7,31},{8,16},{9,... | collective-permute-start | bytes 104456 | tf_op jit(solution)/shard_map/ppermute | solution.py:51
  6.9 0.2 collective-permute-start
  7.1 0.7 %collective-permute-done.2.refs_3_ = bf16[2,4,2176]{2,1,0:T(4,128)(2,1)S(1)} collective-permute-done((bf16[2,4,2176]{2,1,0:T(4,128)(2,1)S(1)}, bf16[2,4,2176]{2,1,0:T(4,128)(2,1)S(1)}, u32[]{:S(2)}, u32[]{:S(2)}) %collective-permute-start.2) | collective-permute-done | bytes 34848 | tf_op jit(solution)/shard_map/ppermute | solution.py:51
  7.9 3.4 %collective-permute-done.1.refs_2_ = bf16[2,4,2176]{2,1,0:T(4,128)(2,1)S(1)} collective-permute-done((bf16[2,4,2176]{2,1,0:T(4,128)(2,1)S(1)}, bf16[2,4,2176]{2,1,0:T(4,128)(2,1)S(1)}, u32[]{:S(2)}, u32[]{:S(2)}) %collective-permute-start.1) | collective-permute-done | bytes 34848 | tf_op jit(solution)/shard_map/ppermute | solution.py:51
  11.4 2.5 %collective-permute-start.5 = (bf16[32,2176]{1,0:T(8,128)(2,1)S(1)}, bf16[32,2176]{1,0:T(8,128)(2,1)S(1)}, u32[]{:S(2)}, u32[]{:S(2)}) collective-permute-start(bf16[32,2176]{1,0:T(8,128)(2,1)S(1)} %join.1.block_in.refs_0_), channel_id=1, source_target_pairs={{0,5},{1,4},{2,7},{3,6},{4,1},{5,0},{6,3},{7,2},{8,13},{9,12},{10,... | collective-permute-start | bytes 417800 | tf_op jit(solution)/shard_map/ppermute | solution.py:51
  13.9 0.5 %collective-permute-start.4 = (bf16[32,2176]{1,0:T(8,128)(2,1)S(1)}, bf16[32,2176]{1,0:T(8,128)(2,1)S(1)}, u32[]{:S(2)}, u32[]{:S(2)}) collective-permute-start(bf16[32,2176]{1,0:T(8,128)(2,1)S(1)} %join.1.block_in.refs_0_), channel_id=1, source_target_pairs={{0,4},{1,5},{2,6},{3,7},{4,0},{5,1},{6,2},{7,3},{8,12},{9,13},{10,... | collective-permute-start | bytes 417800 | tf_op jit(solution)/shard_map/ppermute | solution.py:51
  14.4 0.5 %collective-permute-start.3 = (bf16[32,2176]{1,0:T(8,128)(2,1)S(1)}, bf16[32,2176]{1,0:T(8,128)(2,1)S(1)}, u32[]{:S(2)}, u32[]{:S(2)}) collective-permute-start(bf16[32,2176]{1,0:T(8,128)(2,1)S(1)} %join.1.block_in.refs_0_), channel_id=1, source_target_pairs={{0,1},{1,0},{2,3},{3,2},{4,5},{5,4},{6,7},{7,6},{8,9},{9,8},{10,11... | collective-permute-start | bytes 417800 | tf_op jit(solution)/shard_map/ppermute | solution.py:51
  14.9 2.5 %load.1 = (bf16[32,2176]{1,0:T(8,128)(2,1)S(1)}, bf16[2048,768]{1,0:T(8,128)(2,1)S(1)}, bf16[384,2048]{1,0:T(8,128)(2,1)S(1)}) custom-call(bf16[32,2176]{1,0:T(8,128)(2,1)S(1)} %join.1.block_in.refs_0_, bf16[1,2048,384]{2,1,0:T(8,128)(2,1)} %gate_in.1, bf16[1,2048,384]{2,1,0:T(8,128)(2,1)} %up_in.1, bf16[1,384,2048]{2,1,0:T(8,128)(2,1)} %down_in.1), custom_call_target="tpu_custom_call" | custom-call | bytes 9437184 | tf_op jit(solution)/shard_map/load/pallas_call | solution.py:470
  17.5 1.4 %collective-permute-done.5.refs_3_ = bf16[32,2176]{1,0:T(8,128)(2,1)S(1)} collective-permute-done((bf16[32,2176]{1,0:T(8,128)(2,1)S(1)}, bf16[32,2176]{1,0:T(8,128)(2,1)S(1)}, u32[]{:S(2)}, u32[]{:S(2)}) %collective-permute-start.5) | collective-permute-done | bytes 139296 | tf_op jit(solution)/shard_map/ppermute | solution.py:51
  18.9 0.8 %collective-permute-done.4.refs_2_ = bf16[32,2176]{1,0:T(8,128)(2,1)S(1)} collective-permute-done((bf16[32,2176]{1,0:T(8,128)(2,1)S(1)}, bf16[32,2176]{1,0:T(8,128)(2,1)S(1)}, u32[]{:S(2)}, u32[]{:S(2)}) %collective-permute-start.4) | collective-permute-done | bytes 139296 | tf_op jit(solution)/shard_map/ppermute | solution.py:51
  19.7 0.5 %collective-permute-start.7 = (bf16[32,2176]{1,0:T(8,128)(2,1)S(1)}, bf16[32,2176]{1,0:T(8,128)(2,1)S(1)}, u32[]{:S(2)}, u32[]{:S(2)}) collective-permute-start(bf16[32,2176]{1,0:T(8,128)(2,1)S(1)} %collective-permute-done.3.refs_1_), channel_id=1, source_target_pairs={{0,2},{1,3},{2,0},{3,1},{4,6},{5,7},{6,4},{7,5},{8,10},{9,11},{10,... | collective-permute-start | bytes 417800 | tf_op jit(solution)/shard_map/ppermute | solution.py:51
  20.2 0.8 %collective-permute-done.8.refs_6_ = bf16[32,2176]{1,0:T(8,128)(2,1)S(1)} collective-permute-done((bf16[32,2176]{1,0:T(8,128)(2,1)S(1)}, bf16[32,2176]{1,0:T(8,128)(2,1)S(1)}, u32[]{:S(2)}, u32[]{:S(2)}) %collective-permute-start.8) | collective-permute-done | bytes 139296 | tf_op jit(solution)/shard_map/ppermute | solution.py:51
  21.0 0.2 collective-permute-done.7.refs_5_
  21.2 2.1 %units.1 = (f32[64,2048]{1,0:T(8,128)S(1)}, bf16[64,2176]{1,0:T(8,128)(2,1)S(1)}, f32[2,128]{1,0:T(2,128)S(1)}) custom-call(bf16[32,2176]{1,0:T(8,128)(2,1)S(1)} %join.1.block_in.refs_0_, bf16[32,2176]{1,0:T(8,128)(2,1)S(1)} %collective-permute-done.3.refs_1_, bf16[32,2176]{1,0:T(8,128)(2,1)S(1)} %collective-permute-done.4.refs_2_, ...), custom_call_target="tpu_custom_call" | custom-call | flops 1006632960 | bytes 5767168 | tf_op jit(solution)/shard_map/units/pallas_call | solution.py:492
  23.3 0.4 collective-permute-start.10
  23.7 1.2 %collective-permute-done.10.refs_2_ = bf16[64,2176]{1,0:T(8,128)(2,1)S(1)} collective-permute-done((bf16[64,2176]{1,0:T(8,128)(2,1)S(1)}, bf16[64,2176]{1,0:T(8,128)(2,1)S(1)}, u32[]{:S(2)}, u32[]{:S(2)}) %collective-permute-start.10) | collective-permute-done | bytes 278560 | tf_op jit(solution)/shard_map/ppermute | solution.py:51
  25.0 0.1 add.2
  25.0 1.2 %collective-permute-start.11 = (bf16[16,2176]{1,0:T(8,128)(2,1)S(1)}, bf16[16,2176]{1,0:T(8,128)(2,1)S(1)}, u32[]{:S(2)}, u32[]{:S(2)}) collective-permute-start(bf16[16,2176]{1,0:T(8,128)(2,1)S(1)} %get-tuple-element.36), channel_id=1, source_target_pairs={{0,1},{1,0},{2,3},{3,2},{4,5},{5,4},{6,7},{7,6},{8,9},{9,8},{10,11... | collective-permute-start | bytes 208904 | tf_op jit(solution)/shard_map/ppermute | solution.py:51
  26.2 0.8 %collective-permute-start.12 = (bf16[16,2176]{1,0:T(8,128)(2,1)S(1)}, bf16[16,2176]{1,0:T(8,128)(2,1)S(1)}, u32[]{:S(2)}, u32[]{:S(2)}) collective-permute-start(bf16[16,2176]{1,0:T(8,128)(2,1)S(1)} %get-tuple-element.37), channel_id=1, source_target_pairs={{0,4},{1,5},{2,6},{3,7},{4,0},{5,1},{6,2},{7,3},{8,12},{9,13},{10,... | collective-permute-start | bytes 208904 | tf_op jit(solution)/shard_map/ppermute | solution.py:51
  27.1 1.5 %collective-permute-start.13 = (bf16[16,2176]{1,0:T(8,128)(2,1)S(1)}, bf16[16,2176]{1,0:T(8,128)(2,1)S(1)}, u32[]{:S(2)}, u32[]{:S(2)}) collective-permute-start(bf16[16,2176]{1,0:T(8,128)(2,1)S(1)} %get-tuple-element.38), channel_id=1, source_target_pairs={{0,5},{1,4},{2,7},{3,6},{4,1},{5,0},{6,3},{7,2},{8,13},{9,12},{10,... | collective-permute-start | bytes 208904 | tf_op jit(solution)/shard_map/ppermute | solution.py:51
  28.6 0.9 %collective-permute-done.11.refs_2_ = bf16[16,2176]{1,0:T(8,128)(2,1)S(1)} collective-permute-done((bf16[16,2176]{1,0:T(8,128)(2,1)S(1)}, bf16[16,2176]{1,0:T(8,128)(2,1)S(1)}, u32[]{:S(2)}, u32[]{:S(2)}) %collective-permute-start.11) | collective-permute-done | bytes 69664 | tf_op jit(solution)/shard_map/ppermute | solution.py:51
  29.5 1.8 %collective-permute-done.12.refs_3_ = bf16[16,2176]{1,0:T(8,128)(2,1)S(1)} collective-permute-done((bf16[16,2176]{1,0:T(8,128)(2,1)S(1)}, bf16[16,2176]{1,0:T(8,128)(2,1)S(1)}, u32[]{:S(2)}, u32[]{:S(2)}) %collective-permute-start.12) | collective-permute-done | bytes 69664 | tf_op jit(solution)/shard_map/ppermute | solution.py:51
  31.3 1.0 %collective-permute-done.13.refs_4_ = bf16[16,2176]{1,0:T(8,128)(2,1)S(1)} collective-permute-done((bf16[16,2176]{1,0:T(8,128)(2,1)S(1)}, bf16[16,2176]{1,0:T(8,128)(2,1)S(1)}, u32[]{:S(2)}, u32[]{:S(2)}) %collective-permute-start.13) | collective-permute-done | bytes 69664 | tf_op jit(solution)/shard_map/ppermute | solution.py:51
  32.3 0.4 collective-permute-start.14
  32.7 2.3 %collective-permute-start.15 = (bf16[4,2560]{1,0:T(4,128)(2,1)S(1)}, bf16[4,2560]{1,0:T(4,128)(2,1)S(1)}, u32[]{:S(2)}, u32[]{:S(2)}) collective-permute-start(bf16[4,2560]{1,0:T(4,128)(2,1)S(1)} %get-tuple-element.42), channel_id=1, source_target_pairs={{0,24},{1,25},{2,26},{3,27},{4,28},{5,29},{6,30},{7,31},{8,16},{9,... | collective-permute-start | bytes 61448 | tf_op jit(solution)/shard_map/ppermute | solution.py:65
  35.1 1.9 %collective-permute-start.16 = (bf16[4,2560]{1,0:T(4,128)(2,1)S(1)}, bf16[4,2560]{1,0:T(4,128)(2,1)S(1)}, u32[]{:S(2)}, u32[]{:S(2)}) collective-permute-start(bf16[4,2560]{1,0:T(4,128)(2,1)S(1)} %get-tuple-element.43), channel_id=1, source_target_pairs={{0,16},{1,17},{2,18},{3,19},{4,20},{5,21},{6,22},{7,23},{8,0},{9,1... | collective-permute-start | bytes 61448 | tf_op jit(solution)/shard_map/ppermute | solution.py:65
  37.0 0.4 tables.1
  37.4 0.9 %collective-permute-done.15.refs_8_ = bf16[4,2560]{1,0:T(4,128)(2,1)S(1)} collective-permute-done((bf16[4,2560]{1,0:T(4,128)(2,1)S(1)}, bf16[4,2560]{1,0:T(4,128)(2,1)S(1)}, u32[]{:S(2)}, u32[]{:S(2)}) %collective-permute-start.15) | collective-permute-done | bytes 20512 | tf_op jit(solution)/shard_map/ppermute | solution.py:65
  38.3 0.5 %collective-permute-done.16.refs_9_ = bf16[4,2560]{1,0:T(4,128)(2,1)S(1)} collective-permute-done((bf16[4,2560]{1,0:T(4,128)(2,1)S(1)}, bf16[4,2560]{1,0:T(4,128)(2,1)S(1)}, u32[]{:S(2)}, u32[]{:S(2)}) %collective-permute-start.16) | collective-permute-done | bytes 20512 | tf_op jit(solution)/shard_map/ppermute | solution.py:65
  38.8 1.0 %final.1 = (bf16[4,2048]{1,0:T(4,128)(2,1)}, f32[16,64]{1,0:T(8,128)}) custom-call(f32[16,128]{1,0:T(8,128)S(1)} %get-tuple-element.31.refs_0_, bf16[128,128]{1,0:T(8,128)(2,1)S(1)} %get-tuple-element.32.refs_1_, bf16[16,128]{1,0:T(8,128)(2,1)S(1)} %get-tuple-element.33.refs_2_, bf16[16,64]{1,0:T(8,128)(2,1)S(1)} %get-tuple-element.34.refs_3_, ...), custom_call_target="tpu_custom_call" | custom-call | tf_op jit(solution)/shard_map/final/pallas_call | solution.py:567
  (12 shorter events, 0.3 us)
Async XLA Ops:
  1.5 6.4 %collective-permute-start.2 = (bf16[2,4,2176]{2,1,0:T(4,128)(2,1)S(1)}, bf16[2,4,2176]{2,1,0:T(4,128)(2,1)S(1)}, u32[]{:S(2)}, u32[]{:S(2)}) collective-permute-start(bf16[2,4,2176]{2,1,0:T(4,128)(2,1)S(1)} %prep.1.refs_0_), channel_id=1, source_target_pairs={{0,16},{1,17},{2,18},{3,19},{4,20},{5,21},{6,22},{7,23},{8,24},{9,... | collective-permute-start | bytes 104456 | tf_op jit(solution)/shard_map/ppermute | solution.py:51
  5.6 5.7 %collective-permute-start.1 = (bf16[2,4,2176]{2,1,0:T(4,128)(2,1)S(1)}, bf16[2,4,2176]{2,1,0:T(4,128)(2,1)S(1)}, u32[]{:S(2)}, u32[]{:S(2)}) collective-permute-start(bf16[2,4,2176]{2,1,0:T(4,128)(2,1)S(1)} %prep.1.refs_0_), channel_id=1, source_target_pairs={{0,24},{1,25},{2,26},{3,27},{4,28},{5,29},{6,30},{7,31},{8,16},{9,... | collective-permute-start | bytes 104456 | tf_op jit(solution)/shard_map/ppermute | solution.py:51
  6.9 4.4 %collective-permute-start = (bf16[2,4,2176]{2,1,0:T(4,128)(2,1)S(1)}, bf16[2,4,2176]{2,1,0:T(4,128)(2,1)S(1)}, u32[]{:S(2)}, u32[]{:S(2)}) collective-permute-start(bf16[2,4,2176]{2,1,0:T(4,128)(2,1)S(1)} %prep.1.refs_0_), channel_id=1, source_target_pairs={{0,8},{1,9},{2,10},{3,11},{4,12},{5,13},{6,14},{7,15},{8,0},{9,1},... | collective-permute-start | bytes 104456 | tf_op jit(solution)/shard_map/ppermute | solution.py:51
  11.4 7.5 %collective-permute-start.5 = (bf16[32,2176]{1,0:T(8,128)(2,1)S(1)}, bf16[32,2176]{1,0:T(8,128)(2,1)S(1)}, u32[]{:S(2)}, u32[]{:S(2)}) collective-permute-start(bf16[32,2176]{1,0:T(8,128)(2,1)S(1)} %join.1.block_in.refs_0_), channel_id=1, source_target_pairs={{0,5},{1,4},{2,7},{3,6},{4,1},{5,0},{6,3},{7,2},{8,13},{9,12},{10,... | collective-permute-start | bytes 417800 | tf_op jit(solution)/shard_map/ppermute | solution.py:51
  13.9 5.8 %collective-permute-start.4 = (bf16[32,2176]{1,0:T(8,128)(2,1)S(1)}, bf16[32,2176]{1,0:T(8,128)(2,1)S(1)}, u32[]{:S(2)}, u32[]{:S(2)}) collective-permute-start(bf16[32,2176]{1,0:T(8,128)(2,1)S(1)} %join.1.block_in.refs_0_), channel_id=1, source_target_pairs={{0,4},{1,5},{2,6},{3,7},{4,0},{5,1},{6,2},{7,3},{8,12},{9,13},{10,... | collective-permute-start | bytes 417800 | tf_op jit(solution)/shard_map/ppermute | solution.py:51
  14.4 5.3 %collective-permute-start.3 = (bf16[32,2176]{1,0:T(8,128)(2,1)S(1)}, bf16[32,2176]{1,0:T(8,128)(2,1)S(1)}, u32[]{:S(2)}, u32[]{:S(2)}) collective-permute-start(bf16[32,2176]{1,0:T(8,128)(2,1)S(1)} %join.1.block_in.refs_0_), channel_id=1, source_target_pairs={{0,1},{1,0},{2,3},{3,2},{4,5},{5,4},{6,7},{7,6},{8,9},{9,8},{10,11... | collective-permute-start | bytes 417800 | tf_op jit(solution)/shard_map/ppermute | solution.py:51
  17.4 2.8 %collective-permute-start.6 = (bf16[32,2176]{1,0:T(8,128)(2,1)S(1)}, bf16[32,2176]{1,0:T(8,128)(2,1)S(1)}, u32[]{:S(2)}, u32[]{:S(2)}) collective-permute-start(bf16[32,2176]{1,0:T(8,128)(2,1)S(1)} %get-tuple-element.24), channel_id=1, source_target_pairs={{0,2},{1,3},{2,0},{3,1},{4,6},{5,7},{6,4},{7,5},{8,10},{9,11},{10,... | collective-permute-start | bytes 417800 | tf_op jit(solution)/shard_map/ppermute | solution.py:51
  18.9 1.4 %collective-permute-start.9 = (bf16[32,2176]{1,0:T(8,128)(2,1)S(1)}, bf16[32,2176]{1,0:T(8,128)(2,1)S(1)}, u32[]{:S(2)}, u32[]{:S(2)}) collective-permute-start(bf16[32,2176]{1,0:T(8,128)(2,1)S(1)} %collective-permute-done.5.refs_3_), channel_id=1, source_target_pairs={{0,2},{1,3},{2,0},{3,1},{4,6},{5,7},{6,4},{7,5},{8,10},{9,11},{10,... | collective-permute-start | bytes 417800 | tf_op jit(solution)/shard_map/ppermute | solution.py:51
  19.6 1.4 %collective-permute-start.8 = (bf16[32,2176]{1,0:T(8,128)(2,1)S(1)}, bf16[32,2176]{1,0:T(8,128)(2,1)S(1)}, u32[]{:S(2)}, u32[]{:S(2)}) collective-permute-start(bf16[32,2176]{1,0:T(8,128)(2,1)S(1)} %collective-permute-done.4.refs_2_), channel_id=1, source_target_pairs={{0,2},{1,3},{2,0},{3,1},{4,6},{5,7},{6,4},{7,5},{8,10},{9,11},{10,... | collective-permute-start | bytes 417800 | tf_op jit(solution)/shard_map/ppermute | solution.py:51
  19.7 1.6 %collective-permute-start.7 = (bf16[32,2176]{1,0:T(8,128)(2,1)S(1)}, bf16[32,2176]{1,0:T(8,128)(2,1)S(1)}, u32[]{:S(2)}, u32[]{:S(2)}) collective-permute-start(bf16[32,2176]{1,0:T(8,128)(2,1)S(1)} %collective-permute-done.3.refs_1_), channel_id=1, source_target_pairs={{0,2},{1,3},{2,0},{3,1},{4,6},{5,7},{6,4},{7,5},{8,10},{9,11},{10,... | collective-permute-start | bytes 417800 | tf_op jit(solution)/shard_map/ppermute | solution.py:51
  23.3 1.6 %collective-permute-start.10 = (bf16[64,2176]{1,0:T(8,128)(2,1)S(1)}, bf16[64,2176]{1,0:T(8,128)(2,1)S(1)}, u32[]{:S(2)}, u32[]{:S(2)}) collective-permute-start(bf16[64,2176]{1,0:T(8,128)(2,1)S(1)} %get-tuple-element.29), channel_id=1, source_target_pairs={{0,2},{1,3},{2,0},{3,1},{4,6},{5,7},{6,4},{7,5},{8,10},{9,11},{10,... | collective-permute-start | bytes 835592 | tf_op jit(solution)/shard_map/ppermute | solution.py:51
  25.0 4.5 %collective-permute-start.11 = (bf16[16,2176]{1,0:T(8,128)(2,1)S(1)}, bf16[16,2176]{1,0:T(8,128)(2,1)S(1)}, u32[]{:S(2)}, u32[]{:S(2)}) collective-permute-start(bf16[16,2176]{1,0:T(8,128)(2,1)S(1)} %get-tuple-element.36), channel_id=1, source_target_pairs={{0,1},{1,0},{2,3},{3,2},{4,5},{5,4},{6,7},{7,6},{8,9},{9,8},{10,11... | collective-permute-start | bytes 208904 | tf_op jit(solution)/shard_map/ppermute | solution.py:51
  26.2 5.1 %collective-permute-start.12 = (bf16[16,2176]{1,0:T(8,128)(2,1)S(1)}, bf16[16,2176]{1,0:T(8,128)(2,1)S(1)}, u32[]{:S(2)}, u32[]{:S(2)}) collective-permute-start(bf16[16,2176]{1,0:T(8,128)(2,1)S(1)} %get-tuple-element.37), channel_id=1, source_target_pairs={{0,4},{1,5},{2,6},{3,7},{4,0},{5,1},{6,2},{7,3},{8,12},{9,13},{10,... | collective-permute-start | bytes 208904 | tf_op jit(solution)/shard_map/ppermute | solution.py:51
  27.1 5.2 %collective-permute-start.13 = (bf16[16,2176]{1,0:T(8,128)(2,1)S(1)}, bf16[16,2176]{1,0:T(8,128)(2,1)S(1)}, u32[]{:S(2)}, u32[]{:S(2)}) collective-permute-start(bf16[16,2176]{1,0:T(8,128)(2,1)S(1)} %get-tuple-element.38), channel_id=1, source_target_pairs={{0,5},{1,4},{2,7},{3,6},{4,1},{5,0},{6,3},{7,2},{8,13},{9,12},{10,... | collective-permute-start | bytes 208904 | tf_op jit(solution)/shard_map/ppermute | solution.py:51
  32.3 5.1 %collective-permute-start.14 = (bf16[4,2560]{1,0:T(4,128)(2,1)S(1)}, bf16[4,2560]{1,0:T(4,128)(2,1)S(1)}, u32[]{:S(2)}, u32[]{:S(2)}) collective-permute-start(bf16[4,2560]{1,0:T(4,128)(2,1)S(1)} %get-tuple-element.41), channel_id=1, source_target_pairs={{0,8},{1,9},{2,10},{3,11},{4,12},{5,13},{6,14},{7,15},{8,24},{9,25... | collective-permute-start | bytes 61448 | tf_op jit(solution)/shard_map/ppermute | solution.py:65
  32.7 5.6 %collective-permute-start.15 = (bf16[4,2560]{1,0:T(4,128)(2,1)S(1)}, bf16[4,2560]{1,0:T(4,128)(2,1)S(1)}, u32[]{:S(2)}, u32[]{:S(2)}) collective-permute-start(bf16[4,2560]{1,0:T(4,128)(2,1)S(1)} %get-tuple-element.42), channel_id=1, source_target_pairs={{0,24},{1,25},{2,26},{3,27},{4,28},{5,29},{6,30},{7,31},{8,16},{9,... | collective-permute-start | bytes 61448 | tf_op jit(solution)/shard_map/ppermute | solution.py:65
  35.1 3.8 %copy-start = (bf16[2048,16]{0,1:T(8,128)(2,1)S(1)}, bf16[2048,16]{0,1:T(8,128)(2,1)}, u32[]{:S(2)}) copy-start(bf16[2048,16]{0,1:T(8,128)(2,1)} %param.12) | copy-start | bytes 196612
  35.1 3.8 %collective-permute-start.16 = (bf16[4,2560]{1,0:T(4,128)(2,1)S(1)}, bf16[4,2560]{1,0:T(4,128)(2,1)S(1)}, u32[]{:S(2)}, u32[]{:S(2)}) collective-permute-start(bf16[4,2560]{1,0:T(4,128)(2,1)S(1)} %get-tuple-element.43), channel_id=1, source_target_pairs={{0,16},{1,17},{2,18},{3,19},{4,20},{5,21},{6,22},{7,23},{8,0},{9,1... | collective-permute-start | bytes 61448 | tf_op jit(solution)/shard_map/ppermute | solution.py:65
